TPU v7x, 32 devices: a whole 2x2x4 slice. The times are simulated.
32 devices in a mesh: seq: 4 (over z), head: 2 (over x), batch: 4 (over y, core).
Axes of the slice: x: 2, y: 2, z: 4, core: 2. Of those that a mesh axis runs over, the one named last changes fastest.
Arguments:
- query: bfloat16 [8, 4, 128, 32, 128], P('batch', 'seq', None, 'head'), parts along dimension 0, may hold values from -6 to 6
- keys: bfloat16 [8, 4, 128, 8, 128], P('batch', 'seq', None, 'head'), parts along dimension 0, may hold values from -6 to 6
- values: bfloat16 [8, 4, 128, 8, 128], P('batch', 'seq', None, 'head'), parts along dimension 0, may hold values from -6 to 6
- grad_out: bfloat16 [8, 4, 128, 32, 128], P('batch', 'seq', None, 'head'), parts along dimension 0, may hold values from -6 to 6
- doc_starts: int32 [2048], P('batch'), parts along dimension 0, may hold values from 0 to 1024, as said below
Outputs:
- attended: bfloat16 [8, 4, 128, 32, 128], P('batch', 'seq', None, 'head'), parts along dimension 0
- grad_query: bfloat16 [8, 4, 128, 32, 128], P('batch', 'seq', None, 'head'), parts along dimension 0
- grad_keys: bfloat16 [8, 4, 128, 8, 128], P('batch', 'seq', None, 'head'), parts along dimension 0
- grad_values: bfloat16 [8, 4, 128, 8, 128], P('batch', 'seq', None, 'head'), parts along dimension 0
There are 4 independent parts, one for each index of `batch`. A program takes and returns all parts, laid end to end along the dimension named above; each array names one. Nothing has to cross between parts.
Inputs may be any that keep to these rules, and one draw needn't show every extreme that they name: `doc_starts`: entry 0 is 0; entries rise with differences of 2 to 256 until an entry reaches 1024, and every later entry equals 1024; one difference is exactly 256. So every document has at most 256 tokens.
All inputs are finite; a program needn't handle non-finite values.
Results may differ from a plain program's by a relative error of at most 0.0065.
Values may be sent and summed in bfloat16 or wider, within the bound.
No kernel may reach another device: no remote copies, remote signals or barrier semaphores. Data moves between devices by JAX's collectives and lax.ppermute only.
A program may use at most 128 MiB of HBM per device.

v0:
```python
import jax
import jax.numpy as jnp
from jax import lax
from jax.sharding import PartitionSpec as P


def shifted(value, axis, steps):
    count = lax.axis_size(axis)
    initial, last = (max(0, -steps), min(count, count - steps))
    return lax.ppermute(value, axis, [(source, source + steps) for source in range(initial, last)])


def doc_index(doc_starts, positions, span_len):
    blocks = positions.reshape(-1, span_len)

    def count_block(block_pos):
        below = (doc_starts[None, :] <= block_pos[:, None]).astype(jnp.int32)
        return jnp.sum(below, axis=1) - 1

    return lax.map(count_block, blocks).reshape(-1)


def softmax_rows(scores, allowed):
    scores = jnp.where(allowed[None], scores, -jnp.inf)
    top_score = jnp.max(scores, axis=-1, keepdims=True)
    expons = jnp.exp(scores - top_score)
    return expons / jnp.sum(expons, axis=-1, keepdims=True)


def grad_of_scores(weights, grad_weights, grad_output, attended, score_scale):
    delta = jnp.sum(grad_output.astype(jnp.float32) * attended.astype(jnp.float32), axis=-1)
    delta = jnp.transpose(delta, (1, 0))
    return (weights * (grad_weights - delta[..., None]) * score_scale).astype(jnp.bfloat16)


def head_dense(pieces, allowed, score_scale):
    queries, key_window, value_window, grad_output = pieces
    scores = (
        jnp.einsum("rgd,jd->grj", queries, key_window, preferred_element_type=jnp.float32)
        * score_scale
    )
    weights = softmax_rows(scores, allowed)
    weights_low = weights.astype(jnp.bfloat16)
    attended = jnp.einsum(
        "grj,jd->rgd", weights_low, value_window, preferred_element_type=jnp.float32
    ).astype(jnp.bfloat16)
    grad_weights = jnp.einsum(
        "rgd,jd->grj", grad_output, value_window, preferred_element_type=jnp.float32
    )
    grad_scores = grad_of_scores(weights, grad_weights, grad_output, attended, score_scale)
    grad_query = jnp.einsum(
        "grj,jd->rgd", grad_scores, key_window, preferred_element_type=jnp.float32
    )
    grad_keys = jnp.einsum("grj,rgd->jd", grad_scores, queries, preferred_element_type=jnp.float32)
    grad_values = jnp.einsum(
        "grj,rgd->jd", weights_low, grad_output, preferred_element_type=jnp.float32
    )
    return (attended, grad_query.astype(jnp.bfloat16), grad_keys, grad_values)


def body(query, keys, values, grad_out, doc_starts):
    shard_count = lax.axis_size("seq")
    device_index = lax.axis_index("seq")
    window = min(16, shard_count // 2)
    span_len = query.shape[2]
    head_count = query.shape[3]
    kv_heads = keys.shape[3]
    head_dim = query.shape[4]
    group_size = head_count // kv_heads
    score_scale = head_dim ** (-0.5)
    last_device = device_index == shard_count - 1
    current = jnp.stack([keys[:, 0], values[:, 0]], axis=1)

    def pass_forward(turn_index, state_now):
        moving, stored = state_now
        from_below = shifted(moving[0], "seq", 1)
        from_above = shifted(moving[1], "seq", -1)
        from_above = jnp.where(last_device, moving[0], from_above)
        moving = jnp.stack([from_below, from_above], axis=0)
        stored = lax.dynamic_update_index_in_dim(stored, moving, window - 1 - turn_index, 0)
        return (moving, stored)

    history = jnp.zeros((window,) + current.shape, jnp.bfloat16)
    moving, history = lax.fori_loop(0, window, pass_forward, (current, history))
    row_ids = jnp.arange(span_len, dtype=jnp.int32)
    key_count = (window + 1) * span_len
    span_firsts = [device_index, 2 * shard_count - 1 - device_index]
    outputs = []
    query_grads = []
    term_list = []
    for half_idx in range(2):
        token_pos = span_firsts[half_idx] * span_len + row_ids
        key_pos = (span_firsts[half_idx] - window) * span_len + jnp.arange(
            key_count, dtype=jnp.int32
        )
        key_doc = doc_index(doc_starts, key_pos, span_len)
        query_doc = key_doc[window * span_len :]
        allowed = (query_doc[:, None] == key_doc[None, :]) & (
            key_pos[None, :] <= token_pos[:, None]
        )
        windows = jnp.concatenate([history[:, half_idx], current[half_idx][None]], axis=0)
        key_window = jnp.transpose(windows[:, 0].reshape(key_count, kv_heads, head_dim), (1, 0, 2))
        value_window = jnp.transpose(
            windows[:, 1].reshape(key_count, kv_heads, head_dim), (1, 0, 2)
        )
        queries = jnp.transpose(
            query[half_idx, 0].reshape(span_len, kv_heads, group_size, head_dim), (1, 0, 2, 3)
        )
        grad_output = jnp.transpose(
            grad_out[half_idx, 0].reshape(span_len, kv_heads, group_size, head_dim), (1, 0, 2, 3)
        )
        attended, grad_query, grad_keys, grad_values = lax.map(
            lambda parts: head_dense(parts, allowed, score_scale),
            (queries, key_window, value_window, grad_output),
        )
        outputs.append(
            jnp.transpose(attended, (1, 0, 2, 3)).reshape(span_len, head_count, head_dim)
        )
        query_grads.append(
            jnp.transpose(grad_query, (1, 0, 2, 3)).reshape(span_len, head_count, head_dim)
        )
        paired = jnp.stack([grad_keys, grad_values], axis=0).reshape(
            2, kv_heads, window + 1, span_len, head_dim
        )
        term_list.append(jnp.transpose(paired, (2, 0, 3, 1, 4)))
    term_all = jnp.stack(term_list, axis=1)

    def pass_back(turn_index, totals):
        from_below = shifted(totals[0].astype(jnp.bfloat16), "seq", -1).astype(jnp.float32)
        from_above = shifted(totals[1].astype(jnp.bfloat16), "seq", 1).astype(jnp.float32)
        from_below = jnp.where(last_device, totals[1], from_below)
        return jnp.stack([from_below, from_above], axis=0) + lax.dynamic_index_in_dim(
            term_all, turn_index, 0, keepdims=False
        )

    totals = lax.fori_loop(1, window + 1, pass_back, term_all[0])
    grad_keys_out = totals[:, 0][:, None].astype(jnp.bfloat16)
    grad_values_out = totals[:, 1][:, None].astype(jnp.bfloat16)
    return (
        jnp.stack(outputs, axis=0)[:, None],
        jnp.stack(query_grads, axis=0)[:, None],
        grad_keys_out,
        grad_values_out,
    )


def solution(mesh):
    placed = (
        P("batch", "seq", None, "head", None),
        P("batch", "seq", None, "head", None),
        P("batch", "seq", None, "head", None),
        P("batch", "seq", None, "head", None),
        P("batch"),
    )
    return jax.shard_map(
        body,
        mesh=mesh,
        in_specs=placed,
        out_specs=(
            P("batch", "seq", None, "head", None),
            P("batch", "seq", None, "head", None),
            P("batch", "seq", None, "head", None),
            P("batch", "seq", None, "head", None),
        ),
        check_vma=False,
    )
```

profile of v0, /device:TPU:0, one launch (start us, length us, event | category | flops | bytes accessed | tf_op | source)
XLA Modules:
  0.0 162.7 jit_solution(17773953630697875237)
XLA Ops:
  3.3 25.6 %while.90 = (s32[]{:T(128)}, bf16[2,2,128,4,128]{4,3,2,1,0:T(4,128)(2,1)S(1)}, bf16[2,2,2,128,4,128]{5,3,0,4,2,1:T(8,128)(2,1)S(1)}, pred[]{:T(512)}, s32[]{:T(128)}, /*index=5*/s32[]{:T(128)}, s32[]{:T(128)}) while((s32[]{:T(128)}, bf16[2,2,128,4,128]{4,3,2,1,0:T(4,128)(2,1)S(1)}, bf16[2,2,2,128,4,128]{5,3,0,4,2,1:T(8,128)(2,1)S(1)}, ...), condition=%wide.region_1.2_spmd, body=%wide.region_0.1_spmd.sunk | while | flops 655366 | bytes 7078104 | solution.py:84
  4.8 5.6 %collective-permute-start.1 = (bf16[2,128,4,128]{3,2,1,0:T(4,128)(2,1)S(1)}, bf16[2,128,4,128]{3,2,1,0:T(4,128)(2,1)S(1)}, u32[]{:S(2)}, u32[]{:S(2)}) collective-permute-start(bf16[2,128,4,128]{3,2,1,0:T(4,128)(2,1)S(1)} %get-tuple-element.921), channel_id=1, source_target_pairs={{0,8},{8,16},{16,24},{1,9},{9,17},{17,25},{2,10},{10,18},{18,26},{... | collective-permute-start | bytes 786440 | tf_op jit(solution)/shard_map/while/body/eval_jaxpr/ppermute | solution.py:10
  10.4 4.3 %collective-permute-done = bf16[2,128,4,128]{3,2,1,0:T(4,128)(2,1)S(1)} collective-permute-done((bf16[2,128,4,128]{3,2,1,0:T(4,128)(2,1)S(1)}, bf16[2,128,4,128]{3,2,1,0:T(4,128)(2,1)S(1)}, u32[]{:S(2)}, u32[]{:S(2)}) %collective-permute-start) | collective-permute-done | bytes 262176 | tf_op jit(solution)/shard_map/while/body/eval_jaxpr/ppermute | solution.py:10
  18.3 5.0 %collective-permute-start.1 = (bf16[2,128,4,128]{3,2,1,0:T(4,128)(2,1)S(1)}, bf16[2,128,4,128]{3,2,1,0:T(4,128)(2,1)S(1)}, u32[]{:S(2)}, u32[]{:S(2)}) collective-permute-start(bf16[2,128,4,128]{3,2,1,0:T(4,128)(2,1)S(1)} %get-tuple-element.921), channel_id=1, source_target_pairs={{0,8},{8,16},{16,24},{1,9},{9,17},{17,25},{2,10},{10,18},{18,26},{... | collective-permute-start | bytes 786440 | tf_op jit(solution)/shard_map/while/body/eval_jaxpr/ppermute | solution.py:10
  23.4 3.5 %collective-permute-done = bf16[2,128,4,128]{3,2,1,0:T(4,128)(2,1)S(1)} collective-permute-done((bf16[2,128,4,128]{3,2,1,0:T(4,128)(2,1)S(1)}, bf16[2,128,4,128]{3,2,1,0:T(4,128)(2,1)S(1)}, u32[]{:S(2)}, u32[]{:S(2)}) %collective-permute-start) | collective-permute-done | bytes 262176 | tf_op jit(solution)/shard_map/while/body/eval_jaxpr/ppermute | solution.py:10
  35.1 36.3 %while.95 = (s32[]{:T(128)}, bf16[4,128,4,128]{1,3,2,0:T(8,128)(2,1)S(1)}, bf16[4,128,4,128]{1,3,2,0:T(8,128)(2,1)}, f32[4,384,128]{2,1,0:T(8,128)S(1)}, f32[4,3...) while((s32[]{:T(128)}, ...), condition=%wide.region_17.18_spmd.clone, body=%wide.region_13.17_spmd.clone.sunk | while | flops 406931072 | bytes 5398665 | solution.py:112
  53.5 2.2 %fusion.250 = (f32[4,128]{1,0:T(4,128)S(1)}, f32[4,128,384]{1,2,0:T(8,128)}) fusion(pred[128,384]{0,1:T(8,128)(4,1)S(1)} %compare_and_fusion.5, bf16[4,128,4,128]{3,1,2,0:T(8,128)(2,1)S(1)} %get-tuple-element.1044, s32[]{:T(128)} %get-tuple-element.1023, bf16[4,384,128]{2,1,0:T(8,128)(2,1)} %get-tuple-element.1043), kind=kOutput, calls=%fused_computation.151.clone.1 | convolution fusion | flops 51118464 | bytes 1068032 | tf_op jit(solution)/shard_map/while/body/eval_jaxpr/sub | solution.py:26
  77.8 47.0 %while.94 = (s32[]{:T(128)}, bf16[4,128,4,128]{1,3,2,0:T(8,128)(2,1)}, bf16[4,128,4,128]{1,3,2,0:T(8,128)(2,1)}, f32[4,384,128]{2,1,0:T(8,128)S(1)}, f32[4,384,1...) while((s32[]{:T(128)}, ...), condition=%wide.region_9.10_spmd.clone, body=%wide.region_5.9_spmd.clone.sunk | while | flops 406931072 | bytes 5398665 | solution.py:112
  78.0 2.2 %fusion.231 = (f32[4,128]{1,0:T(4,128)S(1)}, f32[4,128,384]{1,2,0:T(8,128)}) fusion(pred[128,384]{0,1:T(8,128)(4,1)S(1)} %compare_and_fusion.4, bf16[4,128,4,128]{3,1,2,0:T(8,128)(2,1)} %get-tuple-element.1104, s32[]{:T(128)} %get-tuple-element.1083, bf16[4,384,128]{2,1,0:T(8,128)(2,1)} %get-tuple-element.1103), kind=kOutput, calls=%fused_computation.150.clone.1 | convolution fusion | flops 51118464 | bytes 1068032 | tf_op jit(solution)/shard_map/while/body/eval_jaxpr/sub | solution.py:26
  80.2 2.3 %bitcast_dynamic-update-slice_fusion.4 = (bf16[4,128,4,128]{1,3,2,0:T(8,128)(2,1)}, bf16[128,4,128]{2,0,1:T(8,128)(2,1)S(1)}) fusion(bf16[4,128,4,128]{1,3,2,0:T(8,128)(2,1)} %get-tuple-element.1084, s32[]{:T(128)} %get-tuple-element.1083, f32[4,128]{1,0:T(4,128)S(1)} %get-tuple-element.949, pred[128,384]{0,1:T(8,128)(4,1)S(1)} %compare_and_fusion.4, ...), kind=kOutput, calls=%fused_computation.43.clone.1 | convolution fusion | flops 101712768 | bytes 643072 | tf_op jit(solution)/shard_map/while/body/eval_jaxpr/grj,jd->rgd/dot_general | solution.py:44
  89.7 2.2 %fusion.231 = (f32[4,128]{1,0:T(4,128)S(1)}, f32[4,128,384]{1,2,0:T(8,128)}) fusion(pred[128,384]{0,1:T(8,128)(4,1)S(1)} %compare_and_fusion.4, bf16[4,128,4,128]{3,1,2,0:T(8,128)(2,1)} %get-tuple-element.1104, s32[]{:T(128)} %get-tuple-element.1083, bf16[4,384,128]{2,1,0:T(8,128)(2,1)} %get-tuple-element.1103), kind=kOutput, calls=%fused_computation.150.clone.1 | convolution fusion | flops 51118464 | bytes 1068032 | tf_op jit(solution)/shard_map/while/body/eval_jaxpr/sub | solution.py:26
  91.9 2.3 %bitcast_dynamic-update-slice_fusion.4 = (bf16[4,128,4,128]{1,3,2,0:T(8,128)(2,1)}, bf16[128,4,128]{2,0,1:T(8,128)(2,1)S(1)}) fusion(bf16[4,128,4,128]{1,3,2,0:T(8,128)(2,1)} %get-tuple-element.1084, s32[]{:T(128)} %get-tuple-element.1083, f32[4,128]{1,0:T(4,128)S(1)} %get-tuple-element.949, pred[128,384]{0,1:T(8,128)(4,1)S(1)} %compare_and_fusion.4, ...), kind=kOutput, calls=%fused_computation.43.clone.1 | convolution fusion | flops 101712768 | bytes 643072 | tf_op jit(solution)/shard_map/while/body/eval_jaxpr/grj,jd->rgd/dot_general | solution.py:44
  101.5 2.2 %fusion.231 = (f32[4,128]{1,0:T(4,128)S(1)}, f32[4,128,384]{1,2,0:T(8,128)}) fusion(pred[128,384]{0,1:T(8,128)(4,1)S(1)} %compare_and_fusion.4, bf16[4,128,4,128]{3,1,2,0:T(8,128)(2,1)} %get-tuple-element.1104, s32[]{:T(128)} %get-tuple-element.1083, bf16[4,384,128]{2,1,0:T(8,128)(2,1)} %get-tuple-element.1103), kind=kOutput, calls=%fused_computation.150.clone.1 | convolution fusion | flops 51118464 | bytes 1068032 | tf_op jit(solution)/shard_map/while/body/eval_jaxpr/sub | solution.py:26
  103.7 2.3 %bitcast_dynamic-update-slice_fusion.4 = (bf16[4,128,4,128]{1,3,2,0:T(8,128)(2,1)}, bf16[128,4,128]{2,0,1:T(8,128)(2,1)S(1)}) fusion(bf16[4,128,4,128]{1,3,2,0:T(8,128)(2,1)} %get-tuple-element.1084, s32[]{:T(128)} %get-tuple-element.1083, f32[4,128]{1,0:T(4,128)S(1)} %get-tuple-element.949, pred[128,384]{0,1:T(8,128)(4,1)S(1)} %compare_and_fusion.4, ...), kind=kOutput, calls=%fused_computation.43.clone.1 | convolution fusion | flops 101712768 | bytes 643072 | tf_op jit(solution)/shard_map/while/body/eval_jaxpr/grj,jd->rgd/dot_general | solution.py:44
  113.2 2.2 %fusion.231 = (f32[4,128]{1,0:T(4,128)S(1)}, f32[4,128,384]{1,2,0:T(8,128)}) fusion(pred[128,384]{0,1:T(8,128)(4,1)S(1)} %compare_and_fusion.4, bf16[4,128,4,128]{3,1,2,0:T(8,128)(2,1)} %get-tuple-element.1104, s32[]{:T(128)} %get-tuple-element.1083, bf16[4,384,128]{2,1,0:T(8,128)(2,1)} %get-tuple-element.1103), kind=kOutput, calls=%fused_computation.150.clone.1 | convolution fusion | flops 51118464 | bytes 1068032 | tf_op jit(solution)/shard_map/while/body/eval_jaxpr/sub | solution.py:26
  115.4 2.3 %bitcast_dynamic-update-slice_fusion.4 = (bf16[4,128,4,128]{1,3,2,0:T(8,128)(2,1)}, bf16[128,4,128]{2,0,1:T(8,128)(2,1)S(1)}) fusion(bf16[4,128,4,128]{1,3,2,0:T(8,128)(2,1)} %get-tuple-element.1084, s32[]{:T(128)} %get-tuple-element.1083, f32[4,128]{1,0:T(4,128)S(1)} %get-tuple-element.949, pred[128,384]{0,1:T(8,128)(4,1)S(1)} %compare_and_fusion.4, ...), kind=kOutput, calls=%fused_computation.43.clone.1 | convolution fusion | flops 101712768 | bytes 643072 | tf_op jit(solution)/shard_map/while/body/eval_jaxpr/grj,jd->rgd/dot_general | solution.py:44
  126.2 2.5 %pad_maximum_fusion.1 = f32[3,2,2,128,4,128]{5,4,3,2,1,0:T(4,128)} fusion(f32[3,1,2,128,4,128]{5,4,3,2,1,0:T(4,128)S(1)} %maximum_bitcast_fusion.1, f32[3,1,2,128,4,128]{5,4,3,2,1,0:T(4,128)S(1)} %maximum_bitcast_fusion), kind=kLoop, calls=%fused_computation.121 | loop fusion | flops 786432 | bytes 6291456 | tf_op jit(solution)/shard_map/stack | solution.py:126
  128.9 28.6 %while.93 = (s32[]{:T(128)}, f32[2,2,128,4,128]{4,3,2,1,0:T(4,128)S(1)}, pred[]{:T(512)}, f32[3,2,2,128,4,128]{5,4,3,2,1,0:T(4,128)}, s32[]{:T(128)}, /*index=5*/s32[]{:T(128)}, s32[]{:T(128)}) while((s32[]{:T(128)}, f32[2,2,128,4,128]{4,3,2,1,0:T(4,128)S(1)}, pred[]{:T(512)}, f32[3,2,2,128,4,128]{5,4,3,2,1,0:T(4,128)}, s32[]{:T(128)}, ...), condition=%wide.region_19.20_spmd, body=%wide.region_18.19_spmd.sunk | while | flops 917509 | bytes 8388812 | solution.py:136
  129.3 4.4 %collective-permute-start.2 = (bf16[2,128,4,128]{3,2,1,0:T(4,128)(2,1)S(1)}, bf16[2,128,4,128]{3,2,1,0:T(4,128)(2,1)S(1)}, u32[]{:S(2)}, u32[]{:S(2)}) collective-permute-start(bf16[2,128,4,128]{3,2,1,0:T(4,128)(2,1)S(1)} %get-tuple-element.934), channel_id=1, source_target_pairs={{0,8},{8,16},{16,24},{1,9},{9,17},{17,25},{2,10},{10,18},{18,26},{... | collective-permute-start | bytes 786440 | tf_op jit(solution)/shard_map/while/body/eval_jaxpr/ppermute | solution.py:10
  135.0 2.5 %collective-permute-done.2 = bf16[2,128,4,128]{3,2,1,0:T(4,128)(2,1)S(1)} collective-permute-done((bf16[2,128,4,128]{3,2,1,0:T(4,128)(2,1)S(1)}, bf16[2,128,4,128]{3,2,1,0:T(4,128)(2,1)S(1)}, u32[]{:S(2)}, u32[]{:S(2)}) %collective-permute-start.2) | collective-permute-done | bytes 262176 | tf_op jit(solution)/shard_map/while/body/eval_jaxpr/ppermute | solution.py:10
  137.6 4.4 %collective-permute-done.3 = bf16[2,128,4,128]{3,2,1,0:T(4,128)(2,1)S(1)} collective-permute-done((bf16[2,128,4,128]{3,2,1,0:T(4,128)(2,1)S(1)}, bf16[2,128,4,128]{3,2,1,0:T(4,128)(2,1)S(1)}, u32[]{:S(2)}, u32[]{:S(2)}) %collective-permute-start.3) | collective-permute-done | bytes 262176 | tf_op jit(solution)/shard_map/while/body/eval_jaxpr/ppermute | solution.py:10
  143.9 3.6 %collective-permute-start.2 = (bf16[2,128,4,128]{3,2,1,0:T(4,128)(2,1)S(1)}, bf16[2,128,4,128]{3,2,1,0:T(4,128)(2,1)S(1)}, u32[]{:S(2)}, u32[]{:S(2)}) collective-permute-start(bf16[2,128,4,128]{3,2,1,0:T(4,128)(2,1)S(1)} %get-tuple-element.934), channel_id=1, source_target_pairs={{0,8},{8,16},{16,24},{1,9},{9,17},{17,25},{2,10},{10,18},{18,26},{... | collective-permute-start | bytes 786440 | tf_op jit(solution)/shard_map/while/body/eval_jaxpr/ppermute | solution.py:10
  148.9 2.5 %collective-permute-done.2 = bf16[2,128,4,128]{3,2,1,0:T(4,128)(2,1)S(1)} collective-permute-done((bf16[2,128,4,128]{3,2,1,0:T(4,128)(2,1)S(1)}, bf16[2,128,4,128]{3,2,1,0:T(4,128)(2,1)S(1)}, u32[]{:S(2)}, u32[]{:S(2)}) %collective-permute-start.2) | collective-permute-done | bytes 262176 | tf_op jit(solution)/shard_map/while/body/eval_jaxpr/ppermute | solution.py:10
  151.5 4.4 %collective-permute-done.3 = bf16[2,128,4,128]{3,2,1,0:T(4,128)(2,1)S(1)} collective-permute-done((bf16[2,128,4,128]{3,2,1,0:T(4,128)(2,1)S(1)}, bf16[2,128,4,128]{3,2,1,0:T(4,128)(2,1)S(1)}, u32[]{:S(2)}, u32[]{:S(2)}) %collective-permute-start.3) | collective-permute-done | bytes 262176 | tf_op jit(solution)/shard_map/while/body/eval_jaxpr/ppermute | solution.py:10
  (171 shorter events, 99.3 us)
Async XLA Ops:
  3.5 11.2 %collective-permute-start = (bf16[2,128,4,128]{3,2,1,0:T(4,128)(2,1)S(1)}, bf16[2,128,4,128]{3,2,1,0:T(4,128)(2,1)S(1)}, u32[]{:S(2)}, u32[]{:S(2)}) collective-permute-start(bf16[2,128,4,128]{3,2,1,0:T(4,128)(2,1)S(1)} %get-tuple-element.920), channel_id=1, source_target_pairs={{8,0},{16,8},{24,16},{9,1},{17,9},{25,17},{10,2},{18,10},{26,18},{... | collective-permute-start | bytes 786440 | tf_op jit(solution)/shard_map/while/body/eval_jaxpr/ppermute | solution.py:10
  4.8 11.1 %collective-permute-start.1 = (bf16[2,128,4,128]{3,2,1,0:T(4,128)(2,1)S(1)}, bf16[2,128,4,128]{3,2,1,0:T(4,128)(2,1)S(1)}, u32[]{:S(2)}, u32[]{:S(2)}) collective-permute-start(bf16[2,128,4,128]{3,2,1,0:T(4,128)(2,1)S(1)} %get-tuple-element.921), channel_id=1, source_target_pairs={{0,8},{8,16},{16,24},{1,9},{9,17},{17,25},{2,10},{10,18},{18,26},{... | collective-permute-start | bytes 786440 | tf_op jit(solution)/shard_map/while/body/eval_jaxpr/ppermute | solution.py:10
  17.0 9.8 %collective-permute-start = (bf16[2,128,4,128]{3,2,1,0:T(4,128)(2,1)S(1)}, bf16[2,128,4,128]{3,2,1,0:T(4,128)(2,1)S(1)}, u32[]{:S(2)}, u32[]{:S(2)}) collective-permute-start(bf16[2,128,4,128]{3,2,1,0:T(4,128)(2,1)S(1)} %get-tuple-element.920), channel_id=1, source_target_pairs={{8,0},{16,8},{24,16},{9,1},{17,9},{25,17},{10,2},{18,10},{26,18},{... | collective-permute-start | bytes 786440 | tf_op jit(solution)/shard_map/while/body/eval_jaxpr/ppermute | solution.py:10
  18.3 9.7 %collective-permute-start.1 = (bf16[2,128,4,128]{3,2,1,0:T(4,128)(2,1)S(1)}, bf16[2,128,4,128]{3,2,1,0:T(4,128)(2,1)S(1)}, u32[]{:S(2)}, u32[]{:S(2)}) collective-permute-start(bf16[2,128,4,128]{3,2,1,0:T(4,128)(2,1)S(1)} %get-tuple-element.921), channel_id=1, source_target_pairs={{0,8},{8,16},{16,24},{1,9},{9,17},{17,25},{2,10},{10,18},{18,26},{... | collective-permute-start | bytes 786440 | tf_op jit(solution)/shard_map/while/body/eval_jaxpr/ppermute | solution.py:10
  29.1 1.3 copy-start.9
  29.1 2.0 %copy-start.7 = (bf16[2,1,128,16,128]{4,3,2,1,0:T(8,128)(2,1)S(1)}, bf16[2,1,128,16,128]{4,3,2,1,0:T(8,128)(2,1)}, u32[]{:S(2)}) copy-start(bf16[2,1,128,16,128]{4,3,2,1,0:T(8,128)(2,1)} %param.17) | copy-start | bytes 3145732
  31.1 1.4 copy-start.8
  71.4 1.0 copy-start.2
  72.5 1.2 copy-start.5
  72.5 2.2 %copy-start.6 = (bf16[1,1,128,16,128]{4,3,2,1,0:T(8,128)(2,1)S(1)}, bf16[1,1,128,16,128]{4,3,2,1,0:T(8,128)(2,1)}, u32[]{:S(2)}) copy-start(bf16[1,1,128,16,128]{4,3,2,1,0:T(8,128)(2,1)} %get-tuple-element.672) | copy-start | bytes 1572868
  129.3 8.3 %collective-permute-start.2 = (bf16[2,128,4,128]{3,2,1,0:T(4,128)(2,1)S(1)}, bf16[2,128,4,128]{3,2,1,0:T(4,128)(2,1)S(1)}, u32[]{:S(2)}, u32[]{:S(2)}) collective-permute-start(bf16[2,128,4,128]{3,2,1,0:T(4,128)(2,1)S(1)} %get-tuple-element.934), channel_id=1, source_target_pairs={{0,8},{8,16},{16,24},{1,9},{9,17},{17,25},{2,10},{10,18},{18,26},{... | collective-permute-start | bytes 786440 | tf_op jit(solution)/shard_map/while/body/eval_jaxpr/ppermute | solution.py:10
  133.7 8.3 %collective-permute-start.3 = (bf16[2,128,4,128]{3,2,1,0:T(4,128)(2,1)S(1)}, bf16[2,128,4,128]{3,2,1,0:T(4,128)(2,1)S(1)}, u32[]{:S(2)}, u32[]{:S(2)}) collective-permute-start(bf16[2,128,4,128]{3,2,1,0:T(4,128)(2,1)S(1)} %get-tuple-element.935), channel_id=1, source_target_pairs={{8,0},{16,8},{24,16},{9,1},{17,9},{25,17},{10,2},{18,10},{26,18},{... | collective-permute-start | bytes 786440 | tf_op jit(solution)/shard_map/while/body/eval_jaxpr/ppermute | solution.py:10
  143.9 7.5 %collective-permute-start.2 = (bf16[2,128,4,128]{3,2,1,0:T(4,128)(2,1)S(1)}, bf16[2,128,4,128]{3,2,1,0:T(4,128)(2,1)S(1)}, u32[]{:S(2)}, u32[]{:S(2)}) collective-permute-start(bf16[2,128,4,128]{3,2,1,0:T(4,128)(2,1)S(1)} %get-tuple-element.934), channel_id=1, source_target_pairs={{0,8},{8,16},{16,24},{1,9},{9,17},{17,25},{2,10},{10,18},{18,26},{... | collective-permute-start | bytes 786440 | tf_op jit(solution)/shard_map/while/body/eval_jaxpr/ppermute | solution.py:10
  147.6 8.3 %collective-permute-start.3 = (bf16[2,128,4,128]{3,2,1,0:T(4,128)(2,1)S(1)}, bf16[2,128,4,128]{3,2,1,0:T(4,128)(2,1)S(1)}, u32[]{:S(2)}, u32[]{:S(2)}) collective-permute-start(bf16[2,128,4,128]{3,2,1,0:T(4,128)(2,1)S(1)} %get-tuple-element.935), channel_id=1, source_target_pairs={{8,0},{16,8},{24,16},{9,1},{17,9},{25,17},{10,2},{18,10},{26,18},{... | collective-permute-start | bytes 786440 | tf_op jit(solution)/shard_map/while/body/eval_jaxpr/ppermute | solution.py:10
  157.6 1.2 copy-start.1
  157.6 1.6 copy-start.4
  159.2 1.5 copy-start
  159.6 1.5 copy-start.3
where the time goes:
time: 164 us; the launch traced here: 163 us
  matrix products  77.5 us (47%)
  starting transfers between devices  23.8 us (15%)
  waiting for transfers between devices  23.7 us (14%)
  other arithmetic  18.7 us (11%)
  local copies, waits for them, and re-layouts  16.9 us (10%)
    ppermute x8, starting transfers between devices, shifted(): lax.ppermute(value, axis, [(source, source + steps) for source in range(i...  23.8 us
    ppermute x8, waiting for transfers between devices, shifted(): lax.ppermute(value, axis, [(source, source + steps) for source in range(i...  23.7 us
    sub x8, matrix products, softmax_rows(): expons = jnp.exp(scores - top_score)  17.5 us
    dot_general x8, matrix products, head_dense(): jnp.einsum('grj,jd->rgd', weights_low, value_window, preferred_element_ty...  15.5 us
    dot_general x8, matrix products, head_dense(): jnp.einsum('grj,jd->rgd', grad_scores, key_window, preferred_element_type...  14.4 us
    dot_general x8, matrix products, head_dense(): jnp.einsum('grj,rgd->jd', weights_low, grad_output, preferred_element_typ...  12.5 us
    dot_general x8, matrix products, head_dense(): jnp.einsum('rgd,jd->grj', grad_output, value_window, preferred_element_ty...  11.9 us
    dot_general x8, matrix products, head_dense(): jnp.einsum('grj,rgd->jd', grad_scores, queries, preferred_element_type=jn...  5.72 us
  transfers between devices with their start and end apart: 8, of which 8 were waited for; matrix products, arithmetic and copies ran while one was open for 0% of the time, Pallas kernels for 0%

commit v1 on v0

v1 whole, which is shorter than its diff:
```python
import functools

import jax
import jax.numpy as jnp
from jax import lax
from jax.experimental import pallas as pl
from jax.experimental.pallas import tpu as pltpu
from jax.sharding import PartitionSpec as P

LOG2E = 1.4426950408889634
NEG = -1e30


def swap_pairs(count):
    pairs_a = []
    for i in range(0, count - 1, 2):
        pairs_a += [(i, i + 1), (i + 1, i)]
    pairs_b = []
    for i in range(1, count - 1, 2):
        pairs_b += [(i, i + 1), (i + 1, i)]
    pairs_b.append((count - 1, count - 1))
    return pairs_a, pairs_b


def contract(lhs, rhs, lhs_dim, rhs_dim):
    return lax.dot_general(
        lhs, rhs, (((lhs_dim,), (rhs_dim,)), ((), ())), preferred_element_type=jnp.float32
    )


def attention_kernel(blocks, scale, info_ref, q_ref, do_ref, starts_ref, *refs):
    kv_refs = (refs[0:blocks], refs[blocks : 2 * blocks])
    o_ref, dq_ref = refs[2 * blocks : 2 * blocks + 2]
    deep_refs = refs[2 * blocks + 2 : 2 * blocks + 4]
    rest_refs = refs[2 * blocks + 4 : 2 * blocks + 6]
    k_all, v_all, s_all, p_all = refs[2 * blocks + 6 :]
    group, span, dim = q_ref.shape[1:]
    rows = group * span

    def each(body, init):
        if blocks <= 4:
            for t in range(blocks):
                init = body(t, init)
            return init
        return lax.fori_loop(0, blocks, body, init)

    for slot in range(2):
        half = info_ref[slot]
        span_first = info_ref[2 + slot] * span
        for t in range(blocks):
            k_all[t] = kv_refs[slot][t][0, 0]
            v_all[t] = kv_refs[slot][t][1, 0]
        queries = q_ref[half].reshape(rows, dim)
        grad_out = do_ref[half].reshape(rows, dim)
        start = starts_ref[half]
        token = span_first + lax.broadcasted_iota(jnp.int32, (1, span), 1)
        key_row = span_first + lax.broadcasted_iota(jnp.int32, (span, span), 0)

        def scores(t, top):
            key_pos = key_row - t * span
            allowed = (key_pos >= start) & (key_pos <= token)
            bias = jnp.where(allowed, 0.0, NEG)
            value = contract(k_all[t], queries, 1, 1) + jnp.concatenate([bias] * group, axis=1)
            s_all[t] = value
            return jnp.maximum(top, jnp.max(value, axis=0, keepdims=True))

        top = each(scores, jnp.full((1, rows), NEG, jnp.float32))

        def expons(t, total):
            value = jnp.exp2((s_all[t] - top) * (scale * LOG2E))
            s_all[t] = value
            return total + jnp.sum(value, axis=0, keepdims=True)

        total = each(expons, jnp.zeros((1, rows), jnp.float32))
        inverse = 1.0 / total

        def forward(t, carry):
            out, delta = carry
            weights = s_all[t] * inverse
            low = weights.astype(jnp.bfloat16)
            grad_weights = contract(v_all[t], grad_out, 1, 1)
            s_all[t] = weights
            p_all[t] = grad_weights
            delta = delta + jnp.sum(weights * grad_weights, axis=0, keepdims=True)
            out = out + contract(v_all[t], low, 0, 0)
            grad_value = contract(low, grad_out, 1, 0)
            store_term(t, 1, grad_value)
            return out, delta

        def store_term(t, which, value):
            if isinstance(t, int):
                if t == blocks - 1:
                    deep_refs[slot][which, 0] = value.astype(jnp.bfloat16)
                else:
                    rest_refs[slot][t, which, 0] = value
            else:
                @pl.when(t == blocks - 1)
                def _():
                    deep_refs[slot][which, 0] = value.astype(jnp.bfloat16)

                @pl.when(t < blocks - 1)
                def _():
                    rest_refs[slot][t, which, 0] = value

        out, delta = each(
            forward, (jnp.zeros((dim, rows), jnp.float32), jnp.zeros((1, rows), jnp.float32))
        )

        def backward(t, grad_query):
            low = (s_all[t] * (p_all[t] - delta)).astype(jnp.bfloat16)
            store_term(t, 0, contract(low, queries, 1, 0) * scale)
            return grad_query + contract(k_all[t], low, 0, 0)

        grad_query = each(backward, jnp.zeros((dim, rows), jnp.float32)) * scale
        for g in range(group):
            columns = slice(g * span, (g + 1) * span)
            o_ref[half, g] = out[:, columns].T.astype(jnp.bfloat16)
            dq_ref[half, g] = grad_query[:, columns].T.astype(jnp.bfloat16)


def attention_chunk(info, q_t, do_t, starts, kv_blocks, first_head, scale):
    blocks = len(kv_blocks[0])
    _, heads, span, dim = q_t.shape
    chunk = kv_blocks[0][0].shape[1]
    group = 4
    rows = group * span
    window = blocks - 1
    q_spec = pl.BlockSpec((2, group, span, dim), lambda m, info: (0, first_head + m, 0, 0))
    o_spec = pl.BlockSpec((2, group, span, dim), lambda m, info: (0, m, 0, 0))
    kv_spec = pl.BlockSpec((2, 1, span, dim), lambda m, info: (0, m, 0, 0))
    rest_spec = pl.BlockSpec((window, 2, 1, span, dim), lambda m, info: (0, 0, m, 0, 0))
    starts_spec = pl.BlockSpec((2, 1, span), lambda m, info: (0, 0, 0))
    deep = jax.ShapeDtypeStruct((2, chunk, span, dim), jnp.bfloat16)
    rest = jax.ShapeDtypeStruct((window, 2, chunk, span, dim), jnp.float32)
    out = jax.ShapeDtypeStruct((2, chunk * group, span, dim), jnp.bfloat16)
    macs = 2 * chunk * 5 * rows * blocks * span * dim
    return pl.pallas_call(
        functools.partial(attention_kernel, blocks, scale),
        grid_spec=pltpu.PrefetchScalarGridSpec(
            num_scalar_prefetch=1,
            grid=(chunk,),
            in_specs=[q_spec, q_spec, starts_spec] + [kv_spec] * (2 * blocks),
            out_specs=[o_spec, o_spec, kv_spec, kv_spec, rest_spec, rest_spec],
            scratch_shapes=[
                pltpu.VMEM((blocks, span, dim), jnp.bfloat16),
                pltpu.VMEM((blocks, span, dim), jnp.bfloat16),
                pltpu.VMEM((blocks, span, rows), jnp.float32),
                pltpu.VMEM((blocks, span, rows), jnp.float32),
            ],
        ),
        out_shape=[out, out, deep, deep, rest, rest],
        compiler_params=pltpu.CompilerParams(vmem_limit_bytes=48 * 1024 * 1024),
        cost_estimate=pl.CostEstimate(
            flops=2 * macs, bytes_accessed=8 * 1024 * 1024, transcendentals=0
        ),
        name="attention",
    )(info, q_t, do_t, starts, *kv_blocks[0], *kv_blocks[1])


def body(query, keys, values, grad_out, doc_starts):
    count = lax.axis_size("seq")
    device = lax.axis_index("seq")
    window = min(16, count // 2)
    span = query.shape[2]
    heads = query.shape[3]
    kv_heads = keys.shape[3]
    dim = query.shape[4]
    scale = dim ** (-0.5)
    pairs_a, pairs_b = swap_pairs(count)
    parity = device % 2
    chunks = 2
    chunk = kv_heads // chunks

    both = jnp.stack([keys[:, 0], values[:, 0]], axis=1)
    both = jnp.transpose(both, (0, 3, 1, 2, 4))
    half_of = (1 - parity, parity)
    own = [
        [
            jnp.transpose(
                lax.dynamic_slice(
                    both, (half, c * chunk, 0, 0, 0), (1, chunk, 2, span, dim)
                )[0],
                (1, 0, 2, 3),
            )
            for half in half_of
        ]
        for c in range(chunks)
    ]
    history = [([own[c][0]], [own[c][1]]) for c in range(chunks)]
    for _ in range(window):
        for c in range(chunks):
            line_a, line_b = history[c]
            next_a = lax.ppermute(line_b[-1], "seq", pairs_a)
            next_b = lax.ppermute(line_a[-1], "seq", pairs_b)
            line_a.append(next_a)
            line_b.append(next_b)

    q_t = jnp.transpose(query[:, 0], (0, 2, 1, 3))
    do_t = jnp.transpose(grad_out[:, 0], (0, 2, 1, 3))
    spans = jnp.stack([device, 2 * count - 1 - device])
    token = (spans[:, None] * span + jnp.arange(span, dtype=jnp.int32)[None, :]).astype(jnp.int32)
    starts = jnp.max(
        jnp.where(doc_starts[None, None, :] <= token[:, :, None], doc_starts[None, None, :], 0),
        axis=2,
    )[:, None, :]
    half_a, half_b = half_of
    info = jnp.stack(
        [half_a, half_b, jnp.where(half_a == 0, device, 2 * count - 1 - device),
         jnp.where(half_b == 0, device, 2 * count - 1 - device)]
    ).astype(jnp.int32)

    outs, dqs, totals = [], [], []
    for c in range(chunks):
        out, dq, deep_a, deep_b, rest_a, rest_b = attention_chunk(
            info, q_t, do_t, starts, history[c], c * chunk, scale
        )
        outs.append(out)
        dqs.append(dq)
        totals.append((deep_a, deep_b, rest_a, rest_b))
    finals = []
    for c in range(chunks):
        now_a, now_b, rest_a, rest_b = totals[c]
        for t in range(window - 1, -1, -1):
            from_a = lax.ppermute(now_a, "seq", pairs_a)
            from_b = lax.ppermute(now_b, "seq", pairs_b)
            now_a = (rest_a[t] + from_b.astype(jnp.float32)).astype(jnp.bfloat16)
            now_b = (rest_b[t] + from_a.astype(jnp.float32)).astype(jnp.bfloat16)
        finals.append((now_a, now_b))
    slots = jnp.stack(
        [jnp.concatenate([f[s] for f in finals], axis=1) for s in range(2)], axis=0
    )
    halves = jnp.where(parity == 0, slots[::-1], slots)
    halves = jnp.transpose(halves, (1, 0, 3, 2, 4))[:, :, None]
    out = jnp.transpose(jnp.concatenate(outs, axis=1), (0, 2, 1, 3))[:, None]
    dq = jnp.transpose(jnp.concatenate(dqs, axis=1), (0, 2, 1, 3))[:, None]
    return out, dq, halves[0], halves[1]


def solution(mesh):
    spec = P("batch", "seq", None, "head", None)
    return jax.shard_map(
        body,
        mesh=mesh,
        in_specs=(spec, spec, spec, spec, P("batch")),
        out_specs=(spec, spec, spec, spec),
        check_vma=False,
    )
```

time: 164 us -> 58 us (0.35)
  matrix products: 77.5 us -> 0 us
  waiting for transfers between devices: 23.7 us -> 3.17 us
  other arithmetic: 18.7 us -> 1.12 us
  Pallas kernels: 0 us -> 11.1 us
  starting transfers between devices: 23.8 us -> 33.4 us
  local copies, waits for them, and re-layouts: 16.9 us -> 7.86 us
    dot_general x40 -> x0, matrix products: 60 us -> none  [the longest x8 15.5 us: head_dense(): jnp.einsum('grj,jd->rgd', weights_low, value_window, preferred_element_ty...]
    ppermute x8 -> x16, waiting for transfers between devices: 23.7 us -> 3.17 us  [the longest x4 2.89 us: body(): from_a = lax.ppermute(now_a, 'seq', pairs_a)]
    sub x8 -> x0, matrix products: 17.5 us -> none  [softmax_rows(): expons = jnp.exp(scores - top_score)]
    pallas_call x0 -> x2, Pallas kernels: none -> 11.1 us  [attention_chunk(): pl.pallas_call(functools.partial(attention_kernel, blocks, scale), grid_s...]
    ppermute x8 -> x16, starting transfers between devices: 23.8 us -> 33.4 us  [the longest x4 15.8 us: body(): from_a = lax.ppermute(now_a, 'seq', pairs_a)]
    unnamed x21 -> x15, local copies, waits for them, and re-layouts: 1.33 us -> 7.71 us
    another operation x15 -> x1, local copies, waits for them, and re-layouts: 6.07 us -> 0.06 us  [body(): both = jnp.stack([keys[:, 0], values[:, 0]], axis=1)]
    slice x8 -> x0, local copies, waits for them, and re-layouts: 5.74 us -> none  [the longest x3 2.7 us: body(): grad_out[half_idx, 0].reshape(span_len, kv_heads, group_size, head_dim)]
  transfers between devices with their start and end apart: 8 -> 16, of which waited for: 8 -> 3; matrix products, arithmetic and copies ran while one was open for 0% -> 8% of each run, Pallas kernels for 0% -> 19%
where the time goes in v1:
time: 58 us; the launch traced here: 57.6 us
  starting transfers between devices  33.4 us (58%)
  Pallas kernels  11.1 us (19%)
  local copies, waits for them, and re-layouts  7.86 us (14%)
  waiting for transfers between devices  3.17 us (5%)
  other arithmetic  1.12 us (2%)
  between operations  0.96 us (2%)
    ppermute x4, starting transfers between devices, body(): from_a = lax.ppermute(now_a, 'seq', pairs_a)  15.8 us
    ppermute x4, starting transfers between devices, body(): next_a = lax.ppermute(line_b[-1], 'seq', pairs_a)  12.3 us
    pallas_call x2, Pallas kernels, attention_chunk(): pl.pallas_call(functools.partial(attention_kernel, blocks, scale), grid_s...  11.1 us
    unnamed x15, local copies, waits for them, and re-layouts  7.71 us
    ppermute x4, waiting for transfers between devices, body(): from_a = lax.ppermute(now_a, 'seq', pairs_a)  2.89 us
    ppermute x4, starting transfers between devices, body(): from_b = lax.ppermute(now_b, 'seq', pairs_b)  2.65 us
    ppermute x4, starting transfers between devices, body(): next_b = lax.ppermute(line_a[-1], 'seq', pairs_b)  2.64 us
  transfers between devices with their start and end apart: 16, of which 3 were waited for; matrix products, arithmetic and copies ran while one was open for 8% of the time, Pallas kernels for 19%

profile of v1, /device:TPU:0, one launch (start us, length us, event | category | flops | bytes accessed | tf_op | source)
XLA Modules:
  0.0 57.6 jit_solution(8559704741872022035)
XLA Ops:
  0.7 1.1 %copy_dynamic-update-slice_fusion.1 = bf16[2,2,128,4,128]{4,2,3,1,0:T(8,128)(2,1)S(1)} fusion(bf16[2,1,128,4,128]{4,3,2,1,0:T(4,128)(2,1)} %param.6), kind=kLoop, calls=%fused_computation.29 | loop fusion | bytes 524288
  1.9 0.7 %collective-permute-start.1 = (bf16[2,2,128,128]{3,2,1,0:T(8,128)(2,1)S(1)}, bf16[2,2,128,128]{3,2,1,0:T(8,128)(2,1)S(1)}, u32[]{:S(2)}, u32[]{:S(2)}) collective-permute-start(bf16[2,2,128,128]{3,2,1,0:T(8,128)(2,1)S(1)} %get-tuple-element.45.refs_0_), channel_id=1, source_target_pairs={{8,16},{16,8},{24,24},{9,17},{17,9},{25,25},{10,18},{18,10},{26,26... | collective-permute-start | bytes 393224 | tf_op jit(solution)/shard_map/ppermute | solution.py:194
  2.6 5.9 %collective-permute-start = (bf16[2,2,128,128]{3,2,1,0:T(8,128)(2,1)S(1)}, bf16[2,2,128,128]{3,2,1,0:T(8,128)(2,1)S(1)}, u32[]{:S(2)}, u32[]{:S(2)}) collective-permute-start(bf16[2,2,128,128]{3,2,1,0:T(8,128)(2,1)S(1)} %get-tuple-element.42.refs_3_), channel_id=1, source_target_pairs={{0,8},{8,0},{16,24},{24,16},{1,9},{9,1},{17,25},{25,17},{2,10},{10... | collective-permute-start | bytes 393224 | tf_op jit(solution)/shard_map/ppermute | solution.py:193
  8.5 0.7 %collective-permute-start.5 = (bf16[2,2,128,128]{3,2,1,0:T(8,128)(2,1)S(1)}, bf16[2,2,128,128]{3,2,1,0:T(8,128)(2,1)S(1)}, u32[]{:S(2)}, u32[]{:S(2)}) collective-permute-start(bf16[2,2,128,128]{3,2,1,0:T(8,128)(2,1)S(1)} %get-tuple-element.44.refs_0_), channel_id=1, source_target_pairs={{8,16},{16,8},{24,24},{9,17},{17,9},{25,25},{10,18},{18,10},{26,26... | collective-permute-start | bytes 393224 | tf_op jit(solution)/shard_map/ppermute | solution.py:194
  9.2 1.8 %collective-permute-start.4 = (bf16[2,2,128,128]{3,2,1,0:T(8,128)(2,1)S(1)}, bf16[2,2,128,128]{3,2,1,0:T(8,128)(2,1)S(1)}, u32[]{:S(2)}, u32[]{:S(2)}) collective-permute-start(bf16[2,2,128,128]{3,2,1,0:T(8,128)(2,1)S(1)} %get-tuple-element.43.refs_3_), channel_id=1, source_target_pairs={{0,8},{8,0},{16,24},{24,16},{1,9},{9,1},{17,25},{25,17},{2,10},{10... | collective-permute-start | bytes 393224 | tf_op jit(solution)/shard_map/ppermute | solution.py:193
  11.1 1.0 %collective-permute-start.2 = (bf16[2,2,128,128]{3,2,1,0:T(8,128)(2,1)S(1)}, bf16[2,2,128,128]{3,2,1,0:T(8,128)(2,1)S(1)}, u32[]{:S(2)}, u32[]{:S(2)}) collective-permute-start(bf16[2,2,128,128]{3,2,1,0:T(8,128)(2,1)S(1)} %collective-permute-done.1.refs_4_), channel_id=1, source_target_pairs={{0,8},{8,0},{16,24},{24,16},{1,9},{9,1},{17,25},{25,17},{2,10},{10... | collective-permute-start | bytes 393224 | tf_op jit(solution)/shard_map/ppermute | solution.py:193
  12.3 0.7 %collective-permute-start.3 = (bf16[2,2,128,128]{3,2,1,0:T(8,128)(2,1)S(1)}, bf16[2,2,128,128]{3,2,1,0:T(8,128)(2,1)S(1)}, u32[]{:S(2)}, u32[]{:S(2)}) collective-permute-start(bf16[2,2,128,128]{3,2,1,0:T(8,128)(2,1)S(1)} %collective-permute-done.refs_1_), channel_id=1, source_target_pairs={{8,16},{16,8},{24,24},{9,17},{17,9},{25,25},{10,18},{18,10},{26,26... | collective-permute-start | bytes 393224 | tf_op jit(solution)/shard_map/ppermute | solution.py:194
  13.2 3.7 %collective-permute-start.6 = (bf16[2,2,128,128]{3,2,1,0:T(8,128)(2,1)S(1)}, bf16[2,2,128,128]{3,2,1,0:T(8,128)(2,1)S(1)}, u32[]{:S(2)}, u32[]{:S(2)}) collective-permute-start(bf16[2,2,128,128]{3,2,1,0:T(8,128)(2,1)S(1)} %collective-permute-done.5.refs_4_), channel_id=1, source_target_pairs={{0,8},{8,0},{16,24},{24,16},{1,9},{9,1},{17,25},{25,17},{2,10},{10... | collective-permute-start | bytes 393224 | tf_op jit(solution)/shard_map/ppermute | solution.py:193
  16.9 0.7 %collective-permute-start.7 = (bf16[2,2,128,128]{3,2,1,0:T(8,128)(2,1)S(1)}, bf16[2,2,128,128]{3,2,1,0:T(8,128)(2,1)S(1)}, u32[]{:S(2)}, u32[]{:S(2)}) collective-permute-start(bf16[2,2,128,128]{3,2,1,0:T(8,128)(2,1)S(1)} %collective-permute-done.4.refs_1_), channel_id=1, source_target_pairs={{8,16},{16,8},{24,24},{9,17},{17,9},{25,25},{10,18},{18,10},{26,26... | collective-permute-start | bytes 393224 | tf_op jit(solution)/shard_map/ppermute | solution.py:194
  17.9 0.9 %copy-done.1 = bf16[2,1,128,16,128]{4,3,2,1,0:T(8,128)(2,1)S(1)} copy-done((bf16[2,1,128,16,128]{4,3,2,1,0:T(8,128)(2,1)S(1)}, bf16[2,1,128,16,128]{4,3,2,1,0:T(8,128)(2,1)}, u32[]{:S(2)}) %copy-start.1) | copy-done | bytes 1048600
  19.2 5.5 %attention.2 = (bf16[2,8,128,128]{3,2,1,0:T(8,128)(2,1)S(1)}, bf16[2,8,128,128]{3,2,1,0:T(8,128)(2,1)S(1)}, bf16[2,2,128,128]{3,2,1,0:T(8,128)(2,1)S(1)}, bf16[2...) custom-call(s32[4]{0:T(128)S(1)} %pad_add_fusion.info_ref, ...), custom_call_target="tpu_custom_call" | custom-call | flops 1006632960 | bytes 8388608 | tf_op jit(solution)/shard_map/attention/pallas_call | solution.py:137
  24.7 3.0 %collective-permute-start.8 = (bf16[2,2,128,128]{3,2,1,0:T(8,128)(2,1)S(1)}, bf16[2,2,128,128]{3,2,1,0:T(8,128)(2,1)S(1)}, u32[]{:S(2)}, u32[]{:S(2)}) collective-permute-start(bf16[2,2,128,128]{3,2,1,0:T(8,128)(2,1)S(1)} %get-tuple-element.22), channel_id=1, source_target_pairs={{0,8},{8,0},{16,24},{24,16},{1,9},{9,1},{17,25},{25,17},{2,10},{10... | collective-permute-start | bytes 393224 | tf_op jit(solution)/shard_map/ppermute | solution.py:224
  27.7 0.7 %collective-permute-start.12 = (bf16[2,2,128,128]{3,2,1,0:T(8,128)(2,1)S(1)}, bf16[2,2,128,128]{3,2,1,0:T(8,128)(2,1)S(1)}, u32[]{:S(2)}, u32[]{:S(2)}) collective-permute-start(bf16[2,2,128,128]{3,2,1,0:T(8,128)(2,1)S(1)} %get-tuple-element.26), channel_id=1, source_target_pairs={{8,16},{16,8},{24,24},{9,17},{17,9},{25,25},{10,18},{18,10},{26,26... | collective-permute-start | bytes 393224 | tf_op jit(solution)/shard_map/ppermute | solution.py:225
  28.4 5.5 %attention.3 = (bf16[2,8,128,128]{3,2,1,0:T(8,128)(2,1)S(1)}, bf16[2,8,128,128]{3,2,1,0:T(8,128)(2,1)S(1)}, bf16[2,2,128,128]{3,2,1,0:T(8,128)(2,1)S(1)}, bf16[2...) custom-call(s32[4]{0:T(128)S(1)} %pad_add_fusion.info_ref, ...), custom_call_target="tpu_custom_call" | custom-call | flops 1006632960 | bytes 8388608 | tf_op jit(solution)/shard_map/attention/pallas_call | solution.py:137
  34.0 2.1 %collective-permute-start.10 = (bf16[2,2,128,128]{3,2,1,0:T(8,128)(2,1)S(1)}, bf16[2,2,128,128]{3,2,1,0:T(8,128)(2,1)S(1)}, u32[]{:S(2)}, u32[]{:S(2)}) collective-permute-start(bf16[2,2,128,128]{3,2,1,0:T(8,128)(2,1)S(1)} %get-tuple-element.25), channel_id=1, source_target_pairs={{0,8},{8,0},{16,24},{24,16},{1,9},{9,1},{17,25},{25,17},{2,10},{10... | collective-permute-start | bytes 393224 | tf_op jit(solution)/shard_map/ppermute | solution.py:224
  36.9 1.6 %copy.21 = bf16[2,1,128,16,128]{4,3,2,1,0:T(8,128)(2,1)} copy(bf16[2,1,128,16,128]{4,2,3,0,1:T(8,128)(2,1)S(1)} %get-tuple-element.46) | data formatting | bytes 2097152
  38.6 1.6 %copy.22 = bf16[2,1,128,16,128]{4,3,2,1,0:T(8,128)(2,1)} copy(bf16[2,1,128,16,128]{4,2,3,0,1:T(8,128)(2,1)S(1)} %get-tuple-element.47) | data formatting | bytes 2097152
  40.3 0.7 %collective-permute-start.9 = (bf16[2,2,128,128]{3,2,1,0:T(8,128)(2,1)S(1)}, bf16[2,2,128,128]{3,2,1,0:T(8,128)(2,1)S(1)}, u32[]{:S(2)}, u32[]{:S(2)}) collective-permute-start(bf16[2,2,128,128]{3,2,1,0:T(8,128)(2,1)S(1)} %fusion.7), channel_id=1, source_target_pairs={{8,16},{16,8},{24,24},{9,17},{17,9},{25,25},{10,18},{18,10},{26,26... | collective-permute-start | bytes 393224 | tf_op jit(solution)/shard_map/ppermute | solution.py:225
  41.0 0.7 %collective-permute-start.11 = (bf16[2,2,128,128]{3,2,1,0:T(8,128)(2,1)S(1)}, bf16[2,2,128,128]{3,2,1,0:T(8,128)(2,1)S(1)}, u32[]{:S(2)}, u32[]{:S(2)}) collective-permute-start(bf16[2,2,128,128]{3,2,1,0:T(8,128)(2,1)S(1)} %fusion.5), channel_id=1, source_target_pairs={{8,16},{16,8},{24,24},{9,17},{17,9},{25,25},{10,18},{18,10},{26,26... | collective-permute-start | bytes 393224 | tf_op jit(solution)/shard_map/ppermute | solution.py:225
  41.8 8.1 %collective-permute-start.13 = (bf16[2,2,128,128]{3,2,1,0:T(8,128)(2,1)S(1)}, bf16[2,2,128,128]{3,2,1,0:T(8,128)(2,1)S(1)}, u32[]{:S(2)}, u32[]{:S(2)}) collective-permute-start(bf16[2,2,128,128]{3,2,1,0:T(8,128)(2,1)S(1)} %get-tuple-element.39), channel_id=1, source_target_pairs={{0,8},{8,0},{16,24},{24,16},{1,9},{9,1},{17,25},{25,17},{2,10},{10... | collective-permute-start | bytes 393224 | tf_op jit(solution)/shard_map/ppermute | solution.py:224
  49.9 2.6 %collective-permute-start.15 = (bf16[2,2,128,128]{3,2,1,0:T(8,128)(2,1)S(1)}, bf16[2,2,128,128]{3,2,1,0:T(8,128)(2,1)S(1)}, u32[]{:S(2)}, u32[]{:S(2)}) collective-permute-start(bf16[2,2,128,128]{3,2,1,0:T(8,128)(2,1)S(1)} %get-tuple-element.41), channel_id=1, source_target_pairs={{0,8},{8,0},{16,24},{24,16},{1,9},{9,1},{17,25},{25,17},{2,10},{10... | collective-permute-start | bytes 393224 | tf_op jit(solution)/shard_map/ppermute | solution.py:224
  52.9 2.6 %collective-permute-done.15 = bf16[2,2,128,128]{3,2,1,0:T(8,128)(2,1)S(1)} collective-permute-done((bf16[2,2,128,128]{3,2,1,0:T(8,128)(2,1)S(1)}, bf16[2,2,128,128]{3,2,1,0:T(8,128)(2,1)S(1)}, u32[]{:S(2)}, u32[]{:S(2)}) %collective-permute-start.15) | collective-permute-done | bytes 131104 | tf_op jit(solution)/shard_map/ppermute | solution.py:224
  55.8 0.9 %copy.23 = bf16[2,1,128,4,128]{4,3,2,1,0:T(4,128)(2,1)} copy(bf16[2,1,128,4,128]{4,2,3,0,1:T(8,128)(2,1)S(1)} %get-tuple-element.37) | data formatting | bytes 524288
  56.7 0.9 %copy.24 = bf16[2,1,128,4,128]{4,3,2,1,0:T(4,128)(2,1)} copy(bf16[2,1,128,4,128]{4,2,3,0,1:T(8,128)(2,1)S(1)} %get-tuple-element.36) | data formatting | bytes 524288
  (43 shorter events, 3.0 us)
Async XLA Ops:
  0.6 1.1 %copy-start.2 = (bf16[2,1,128,4,128]{4,3,2,1,0:T(4,128)(2,1)S(1)}, bf16[2,1,128,4,128]{4,3,2,1,0:T(4,128)(2,1)}, u32[]{:S(2)}) copy-start(bf16[2,1,128,4,128]{4,3,2,1,0:T(4,128)(2,1)} %param.7) | copy-start | bytes 786436
  0.7 17.0 %copy-start = (bf16[2,1,128,16,128]{4,3,2,1,0:T(8,128)(2,1)S(1)}, bf16[2,1,128,16,128]{4,3,2,1,0:T(8,128)(2,1)}, u32[]{:S(2)}) copy-start(bf16[2,1,128,16,128]{4,3,2,1,0:T(8,128)(2,1)} %param.8) | copy-start | bytes 3145732
  1.9 9.2 %collective-permute-start.1 = (bf16[2,2,128,128]{3,2,1,0:T(8,128)(2,1)S(1)}, bf16[2,2,128,128]{3,2,1,0:T(8,128)(2,1)S(1)}, u32[]{:S(2)}, u32[]{:S(2)}) collective-permute-start(bf16[2,2,128,128]{3,2,1,0:T(8,128)(2,1)S(1)} %get-tuple-element.45.refs_0_), channel_id=1, source_target_pairs={{8,16},{16,8},{24,24},{9,17},{17,9},{25,25},{10,18},{18,10},{26,26... | collective-permute-start | bytes 393224 | tf_op jit(solution)/shard_map/ppermute | solution.py:194
  2.6 9.7 %collective-permute-start = (bf16[2,2,128,128]{3,2,1,0:T(8,128)(2,1)S(1)}, bf16[2,2,128,128]{3,2,1,0:T(8,128)(2,1)S(1)}, u32[]{:S(2)}, u32[]{:S(2)}) collective-permute-start(bf16[2,2,128,128]{3,2,1,0:T(8,128)(2,1)S(1)} %get-tuple-element.42.refs_3_), channel_id=1, source_target_pairs={{0,8},{8,0},{16,24},{24,16},{1,9},{9,1},{17,25},{25,17},{2,10},{10... | collective-permute-start | bytes 393224 | tf_op jit(solution)/shard_map/ppermute | solution.py:193
  8.5 4.7 %collective-permute-start.5 = (bf16[2,2,128,128]{3,2,1,0:T(8,128)(2,1)S(1)}, bf16[2,2,128,128]{3,2,1,0:T(8,128)(2,1)S(1)}, u32[]{:S(2)}, u32[]{:S(2)}) collective-permute-start(bf16[2,2,128,128]{3,2,1,0:T(8,128)(2,1)S(1)} %get-tuple-element.44.refs_0_), channel_id=1, source_target_pairs={{8,16},{16,8},{24,24},{9,17},{17,9},{25,25},{10,18},{18,10},{26,26... | collective-permute-start | bytes 393224 | tf_op jit(solution)/shard_map/ppermute | solution.py:194
  9.2 7.8 %collective-permute-start.4 = (bf16[2,2,128,128]{3,2,1,0:T(8,128)(2,1)S(1)}, bf16[2,2,128,128]{3,2,1,0:T(8,128)(2,1)S(1)}, u32[]{:S(2)}, u32[]{:S(2)}) collective-permute-start(bf16[2,2,128,128]{3,2,1,0:T(8,128)(2,1)S(1)} %get-tuple-element.43.refs_3_), channel_id=1, source_target_pairs={{0,8},{8,0},{16,24},{24,16},{1,9},{9,1},{17,25},{25,17},{2,10},{10... | collective-permute-start | bytes 393224 | tf_op jit(solution)/shard_map/ppermute | solution.py:193
  10.9 2.0 %copy-start.3 = (s32[512]{0:T(512)S(1)}, s32[512]{0:T(512)}, u32[]{:S(2)}) copy-start(s32[512]{0:T(512)} %param.9) | copy-start | bytes 6148
  11.1 8.1 %collective-permute-start.2 = (bf16[2,2,128,128]{3,2,1,0:T(8,128)(2,1)S(1)}, bf16[2,2,128,128]{3,2,1,0:T(8,128)(2,1)S(1)}, u32[]{:S(2)}, u32[]{:S(2)}) collective-permute-start(bf16[2,2,128,128]{3,2,1,0:T(8,128)(2,1)S(1)} %collective-permute-done.1.refs_4_), channel_id=1, source_target_pairs={{0,8},{8,0},{16,24},{24,16},{1,9},{9,1},{17,25},{25,17},{2,10},{10... | collective-permute-start | bytes 393224 | tf_op jit(solution)/shard_map/ppermute | solution.py:193
  12.3 6.9 %collective-permute-start.3 = (bf16[2,2,128,128]{3,2,1,0:T(8,128)(2,1)S(1)}, bf16[2,2,128,128]{3,2,1,0:T(8,128)(2,1)S(1)}, u32[]{:S(2)}, u32[]{:S(2)}) collective-permute-start(bf16[2,2,128,128]{3,2,1,0:T(8,128)(2,1)S(1)} %collective-permute-done.refs_1_), channel_id=1, source_target_pairs={{8,16},{16,8},{24,24},{9,17},{17,9},{25,25},{10,18},{18,10},{26,26... | collective-permute-start | bytes 393224 | tf_op jit(solution)/shard_map/ppermute | solution.py:194
  13.2 15.2 %collective-permute-start.6 = (bf16[2,2,128,128]{3,2,1,0:T(8,128)(2,1)S(1)}, bf16[2,2,128,128]{3,2,1,0:T(8,128)(2,1)S(1)}, u32[]{:S(2)}, u32[]{:S(2)}) collective-permute-start(bf16[2,2,128,128]{3,2,1,0:T(8,128)(2,1)S(1)} %collective-permute-done.5.refs_4_), channel_id=1, source_target_pairs={{0,8},{8,0},{16,24},{24,16},{1,9},{9,1},{17,25},{25,17},{2,10},{10... | collective-permute-start | bytes 393224 | tf_op jit(solution)/shard_map/ppermute | solution.py:193
  16.9 11.5 %collective-permute-start.7 = (bf16[2,2,128,128]{3,2,1,0:T(8,128)(2,1)S(1)}, bf16[2,2,128,128]{3,2,1,0:T(8,128)(2,1)S(1)}, u32[]{:S(2)}, u32[]{:S(2)}) collective-permute-start(bf16[2,2,128,128]{3,2,1,0:T(8,128)(2,1)S(1)} %collective-permute-done.4.refs_1_), channel_id=1, source_target_pairs={{8,16},{16,8},{24,24},{9,17},{17,9},{25,25},{10,18},{18,10},{26,26... | collective-permute-start | bytes 393224 | tf_op jit(solution)/shard_map/ppermute | solution.py:194
  17.7 1.2 %copy-start.1 = (bf16[2,1,128,16,128]{4,3,2,1,0:T(8,128)(2,1)S(1)}, bf16[2,1,128,16,128]{4,3,2,1,0:T(8,128)(2,1)}, u32[]{:S(2)}) copy-start(bf16[2,1,128,16,128]{4,3,2,1,0:T(8,128)(2,1)} %param.5) | copy-start | bytes 3145732
  24.7 15.5 %collective-permute-start.8 = (bf16[2,2,128,128]{3,2,1,0:T(8,128)(2,1)S(1)}, bf16[2,2,128,128]{3,2,1,0:T(8,128)(2,1)S(1)}, u32[]{:S(2)}, u32[]{:S(2)}) collective-permute-start(bf16[2,2,128,128]{3,2,1,0:T(8,128)(2,1)S(1)} %get-tuple-element.22), channel_id=1, source_target_pairs={{0,8},{8,0},{16,24},{24,16},{1,9},{9,1},{17,25},{25,17},{2,10},{10... | collective-permute-start | bytes 393224 | tf_op jit(solution)/shard_map/ppermute | solution.py:224
  27.7 14.0 %collective-permute-start.12 = (bf16[2,2,128,128]{3,2,1,0:T(8,128)(2,1)S(1)}, bf16[2,2,128,128]{3,2,1,0:T(8,128)(2,1)S(1)}, u32[]{:S(2)}, u32[]{:S(2)}) collective-permute-start(bf16[2,2,128,128]{3,2,1,0:T(8,128)(2,1)S(1)} %get-tuple-element.26), channel_id=1, source_target_pairs={{8,16},{16,8},{24,24},{9,17},{17,9},{25,25},{10,18},{18,10},{26,26... | collective-permute-start | bytes 393224 | tf_op jit(solution)/shard_map/ppermute | solution.py:225
  34.0 7.0 %collective-permute-start.10 = (bf16[2,2,128,128]{3,2,1,0:T(8,128)(2,1)S(1)}, bf16[2,2,128,128]{3,2,1,0:T(8,128)(2,1)S(1)}, u32[]{:S(2)}, u32[]{:S(2)}) collective-permute-start(bf16[2,2,128,128]{3,2,1,0:T(8,128)(2,1)S(1)} %get-tuple-element.25), channel_id=1, source_target_pairs={{0,8},{8,0},{16,24},{24,16},{1,9},{9,1},{17,25},{25,17},{2,10},{10... | collective-permute-start | bytes 393224 | tf_op jit(solution)/shard_map/ppermute | solution.py:224
  36.1 13.8 %collective-permute-start.14 = (bf16[2,2,128,128]{3,2,1,0:T(8,128)(2,1)S(1)}, bf16[2,2,128,128]{3,2,1,0:T(8,128)(2,1)S(1)}, u32[]{:S(2)}, u32[]{:S(2)}) collective-permute-start(bf16[2,2,128,128]{3,2,1,0:T(8,128)(2,1)S(1)} %get-tuple-element.27), channel_id=1, source_target_pairs={{8,16},{16,8},{24,24},{9,17},{17,9},{25,25},{10,18},{18,10},{26,26... | collective-permute-start | bytes 393224 | tf_op jit(solution)/shard_map/ppermute | solution.py:225
  40.3 1.4 %collective-permute-start.9 = (bf16[2,2,128,128]{3,2,1,0:T(8,128)(2,1)S(1)}, bf16[2,2,128,128]{3,2,1,0:T(8,128)(2,1)S(1)}, u32[]{:S(2)}, u32[]{:S(2)}) collective-permute-start(bf16[2,2,128,128]{3,2,1,0:T(8,128)(2,1)S(1)} %fusion.7), channel_id=1, source_target_pairs={{8,16},{16,8},{24,24},{9,17},{17,9},{25,25},{10,18},{18,10},{26,26... | collective-permute-start | bytes 393224 | tf_op jit(solution)/shard_map/ppermute | solution.py:225
  41.0 8.9 %collective-permute-start.11 = (bf16[2,2,128,128]{3,2,1,0:T(8,128)(2,1)S(1)}, bf16[2,2,128,128]{3,2,1,0:T(8,128)(2,1)S(1)}, u32[]{:S(2)}, u32[]{:S(2)}) collective-permute-start(bf16[2,2,128,128]{3,2,1,0:T(8,128)(2,1)S(1)} %fusion.5), channel_id=1, source_target_pairs={{8,16},{16,8},{24,24},{9,17},{17,9},{25,25},{10,18},{18,10},{26,26... | collective-permute-start | bytes 393224 | tf_op jit(solution)/shard_map/ppermute | solution.py:225
  41.8 11.0 %collective-permute-start.13 = (bf16[2,2,128,128]{3,2,1,0:T(8,128)(2,1)S(1)}, bf16[2,2,128,128]{3,2,1,0:T(8,128)(2,1)S(1)}, u32[]{:S(2)}, u32[]{:S(2)}) collective-permute-start(bf16[2,2,128,128]{3,2,1,0:T(8,128)(2,1)S(1)} %get-tuple-element.39), channel_id=1, source_target_pairs={{0,8},{8,0},{16,24},{24,16},{1,9},{9,1},{17,25},{25,17},{2,10},{10... | collective-permute-start | bytes 393224 | tf_op jit(solution)/shard_map/ppermute | solution.py:224
  49.9 5.5 %collective-permute-start.15 = (bf16[2,2,128,128]{3,2,1,0:T(8,128)(2,1)S(1)}, bf16[2,2,128,128]{3,2,1,0:T(8,128)(2,1)S(1)}, u32[]{:S(2)}, u32[]{:S(2)}) collective-permute-start(bf16[2,2,128,128]{3,2,1,0:T(8,128)(2,1)S(1)} %get-tuple-element.41), channel_id=1, source_target_pairs={{0,8},{8,0},{16,24},{24,16},{1,9},{9,1},{17,25},{25,17},{2,10},{10... | collective-permute-start | bytes 393224 | tf_op jit(solution)/shard_map/ppermute | solution.py:224

commit v2 on v1

--- a/solution.py
+++ b/solution.py
@@ -157,82 +157,241 @@
     )(info, q_t, do_t, starts, *kv_blocks[0], *kv_blocks[1])
 
 
+def vmem_call(kernel, out_shape, macs, name, *args):
+    whole = pl.BlockSpec(memory_space=pltpu.VMEM)
+    moved = sum(a.size * a.dtype.itemsize for a in args[1:])
+    return pl.pallas_call(
+        kernel,
+        in_specs=[pl.BlockSpec(memory_space=pltpu.SMEM)] + [whole] * (len(args) - 1),
+        out_specs=[whole] * len(out_shape),
+        out_shape=out_shape,
+        compiler_params=pltpu.CompilerParams(vmem_limit_bytes=16 * 1024 * 1024),
+        cost_estimate=pl.CostEstimate(flops=8 * macs, bytes_accessed=moved, transcendentals=0),
+        name=name,
+    )(*args)
+
+
+def group_of(ref, half, m, group):
+    return ref[half, pl.ds(m * group, group)].reshape(group * ref.shape[2], ref.shape[3])
+
+
+def scores_kernel(info_ref, q_ref, do_ref, kv_a_ref, kv_b_ref, s_ref, dp_ref):
+    heads = kv_a_ref.shape[1]
+    group = q_ref.shape[1] // heads
+
+    def one_head(m, carry):
+        for slot, kv_ref in enumerate((kv_a_ref, kv_b_ref)):
+            half = info_ref[slot]
+            s_ref[slot, m] = contract(kv_ref[0, m], group_of(q_ref, half, m, group), 1, 1)
+            dp_ref[slot, m] = contract(kv_ref[1, m], group_of(do_ref, half, m, group), 1, 1)
+        return carry
+
+    lax.fori_loop(0, heads, one_head, 0)
+
+
+def later_keys(span, group, dtype):
+    row = lax.broadcasted_iota(jnp.int32, (span, span), 0)
+    column = lax.broadcasted_iota(jnp.int32, (span, span), 1)
+    return jnp.concatenate([(row > column).astype(jnp.float32).astype(dtype)] * group, axis=1)
+
+
+def softmax_kernel(scale, info_ref, starts_ref, q_ref, do_ref, kv_a_ref, kv_b_ref, s0_ref, dp0_ref, s1_ref,
+                   dp1_ref, deep_a_ref, deep_b_ref, low_ref, ds_ref):
+    heads, span, rows = s0_ref.shape[1:]
+    group = rows // span
+    row = lax.broadcasted_iota(jnp.int32, (span, span), 0)
+    column = lax.broadcasted_iota(jnp.int32, (span, span), 1)
+    far = row > column
+    far_wide = jnp.concatenate([far] * group, axis=1)
+    far_low = later_keys(span, group, jnp.bfloat16)
+
+    def one_head(m, carry):
+        for slot, (kv_ref, deep_ref) in enumerate(((kv_a_ref, deep_a_ref), (kv_b_ref, deep_b_ref))):
+            half = info_ref[slot]
+            first = info_ref[2 + slot] * span
+            start = starts_ref[half]
+            queries = group_of(q_ref, half, m, group)
+            grad_out = group_of(do_ref, half, m, group)
+            near_pos = jnp.where(far, first - 2 * span + row, first + row)
+            bias = jnp.where(near_pos >= start, 0.0, NEG)
+            bias_prev = jnp.where(first - span + row >= start, 0.0, NEG)
+            s2 = contract(kv_ref[0, m], queries, 1, 1)
+            dp2 = contract(kv_ref[1, m], grad_out, 1, 1)
+            s = jnp.where(far_wide, s2, s0_ref[slot, m]) + jnp.concatenate([bias] * group, axis=1)
+            dp = jnp.where(far_wide, dp2, dp0_ref[slot, m])
+            s_prev = s1_ref[slot, m] + jnp.concatenate([bias_prev] * group, axis=1)
+            dp_prev = dp1_ref[slot, m]
+            top = jnp.max(jnp.maximum(s, s_prev), axis=0, keepdims=True)
+            e = jnp.exp2((s - top) * (scale * LOG2E))
+            e_prev = jnp.exp2((s_prev - top) * (scale * LOG2E))
+            inverse = 1.0 / jnp.sum(e + e_prev, axis=0, keepdims=True)
+            w = e * inverse
+            w_prev = e_prev * inverse
+            delta = jnp.sum(w * dp + w_prev * dp_prev, axis=0, keepdims=True)
+            low = w.astype(jnp.bfloat16)
+            ds = (w * (dp - delta)).astype(jnp.bfloat16)
+            low_ref[slot, m, 0] = low
+            ds_ref[slot, m, 0] = ds
+            low_ref[slot, m, 1] = w_prev.astype(jnp.bfloat16)
+            ds_ref[slot, m, 1] = (w_prev * (dp_prev - delta)).astype(jnp.bfloat16)
+            deep_ref[0, m] = (contract(ds * far_low, queries, 1, 0) * scale).astype(jnp.bfloat16)
+            deep_ref[1, m] = contract(low * far_low, grad_out, 1, 0).astype(jnp.bfloat16)
+        return carry
+
+    lax.fori_loop(0, heads, one_head, 0)
+
+
+def terms_kernel(scale, info_ref, q_ref, do_ref, low_ref, ds_ref, prev_a_ref, prev_b_ref, own_a_ref, own_b_ref):
+    heads, _, span, rows = low_ref.shape[1:]
+    group = rows // span
+    own_low = 1 - later_keys(span, group, jnp.bfloat16)
+
+    def one_head(m, carry):
+        for slot, (prev_ref, own_ref) in enumerate(((prev_a_ref, own_a_ref), (prev_b_ref, own_b_ref))):
+            half = info_ref[slot]
+            queries = group_of(q_ref, half, m, group)
+            grad_out = group_of(do_ref, half, m, group)
+            ds = jnp.concatenate([ds_ref[slot, m, 1], ds_ref[slot, m, 0] * own_low], axis=0)
+            low = jnp.concatenate([low_ref[slot, m, 1], low_ref[slot, m, 0] * own_low], axis=0)
+            grad_key = contract(ds, queries, 1, 0) * scale
+            grad_value = contract(low, grad_out, 1, 0)
+            prev_ref[0, m] = grad_key[:span]
+            prev_ref[1, m] = grad_value[:span]
+            own_ref[0, m] = grad_key[span:]
+            own_ref[1, m] = grad_value[span:]
+        return carry
+
+    lax.fori_loop(0, heads, one_head, 0)
+
+
+def outputs_kernel(scale, info_ref, low_ref, ds_ref, kv_a0, kv_b0, kv_a1, kv_b1, kv_a2, kv_b2, o_ref, dq_ref):
+    heads, _, span, rows = low_ref.shape[1:]
+    group = rows // span
+    far_low = later_keys(span, group, jnp.bfloat16)
+    own_low = 1 - far_low
+
+    def one_head(m, carry):
+        for slot, kv_refs in enumerate(((kv_a0, kv_a1, kv_a2), (kv_b0, kv_b1, kv_b2))):
+            half = info_ref[slot]
+            low = low_ref[slot, m, 0]
+            ds = ds_ref[slot, m, 0]
+            low = jnp.concatenate([low * own_low, low_ref[slot, m, 1], low * far_low], axis=0)
+            ds = jnp.concatenate([ds * own_low, ds_ref[slot, m, 1], ds * far_low], axis=0)
+            keys = jnp.concatenate([ref[0, m] for ref in kv_refs], axis=0)
+            values = jnp.concatenate([ref[1, m] for ref in kv_refs], axis=0)
+            out = contract(values, low, 0, 0)
+            grad_query = contract(keys, ds, 0, 0) * scale
+            for g in range(group):
+                columns = slice(g * span, (g + 1) * span)
+                o_ref[half, m * group + g] = out[:, columns].T.astype(jnp.bfloat16)
+                dq_ref[half, m * group + g] = grad_query[:, columns].T.astype(jnp.bfloat16)
+        return carry
+
+    lax.fori_loop(0, heads, one_head, 0)
+
+
+def two_span_window(info, q_t, do_t, starts, own_a, own_b, pairs_a, pairs_b, scale):
+    _, kv_heads, span, dim = own_a.shape
+    heads = q_t.shape[1]
+    rows = heads // kv_heads * span
+    block = 2 * kv_heads * rows * span * dim
+    shape = jax.ShapeDtypeStruct
+    scores = [shape((2, kv_heads, span, rows), jnp.float32)] * 2
+    terms = [shape(own_a.shape, jnp.float32)] * 4
+    lows = [shape((2, kv_heads, 2, span, rows), jnp.bfloat16)] * 2
+    deeps = [shape(own_a.shape, jnp.bfloat16)] * 2
+    outs = [shape(q_t.shape, jnp.bfloat16)] * 2
+
+    b1 = lax.ppermute(own_a, "seq", pairs_b)
+    a1 = lax.ppermute(own_b, "seq", pairs_a)
+    s0, dp0 = vmem_call(scores_kernel, scores, 2 * block, "scores_own", info, q_t, do_t, own_a, own_b)
+    b2 = lax.ppermute(a1, "seq", pairs_b)
+    a2 = lax.ppermute(b1, "seq", pairs_a)
+    s1, dp1 = vmem_call(scores_kernel, scores, 2 * block, "scores_prev", info, q_t, do_t, a1, b1)
+    deep_a, deep_b, low, ds = vmem_call(
+        functools.partial(softmax_kernel, scale), deeps + lows, 4 * block, "softmax",
+        info, starts, q_t, do_t, a2, b2, s0, dp0, s1, dp1,
+    )
+    from_b = lax.ppermute(deep_b, "seq", pairs_b)
+    from_a = lax.ppermute(deep_a, "seq", pairs_a)
+    prev_a, prev_b, own_term_a, own_term_b = vmem_call(
+        functools.partial(terms_kernel, scale), terms, 4 * block, "terms", info, q_t, do_t, low, ds
+    )
+    out, dq = vmem_call(
+        functools.partial(outputs_kernel, scale), outs, 6 * block, "outputs",
+        info, low, ds, own_a, own_b, a1, b1, a2, b2,
+    )
+    next_b = (prev_b + from_a.astype(jnp.float32)).astype(jnp.bfloat16)
+    next_a = (prev_a + from_b.astype(jnp.float32)).astype(jnp.bfloat16)
+    last_b = lax.ppermute(next_b, "seq", pairs_b)
+    last_a = lax.ppermute(next_a, "seq", pairs_a)
+    final_a = (own_term_a + last_b.astype(jnp.float32)).astype(jnp.bfloat16)
+    final_b = (own_term_b + last_a.astype(jnp.float32)).astype(jnp.bfloat16)
+    return out, dq, final_a, final_b
+
+
+def any_window(info, q_t, do_t, starts, own_a, own_b, pairs_a, pairs_b, window, scale):
+    kv_heads = own_a.shape[1]
+    chunks = 2
+    chunk = kv_heads // chunks
+    parts = []
+    for c in range(chunks):
+        line_a = [own_a[:, c * chunk : (c + 1) * chunk]]
+        line_b = [own_b[:, c * chunk : (c + 1) * chunk]]
+        for _ in range(window):
+            next_a = lax.ppermute(line_b[-1], "seq", pairs_a)
+            next_b = lax.ppermute(line_a[-1], "seq", pairs_b)
+            line_a.append(next_a)
+            line_b.append(next_b)
+        out, dq, now_a, now_b, rest_a, rest_b = attention_chunk(
+            info, q_t, do_t, starts, (line_a, line_b), c * chunk, scale
+        )
+        for t in range(window - 1, -1, -1):
+            from_a = lax.ppermute(now_a, "seq", pairs_a)
+            from_b = lax.ppermute(now_b, "seq", pairs_b)
+            now_a = (rest_a[t] + from_b.astype(jnp.float32)).astype(jnp.bfloat16)
+            now_b = (rest_b[t] + from_a.astype(jnp.float32)).astype(jnp.bfloat16)
+        parts.append((out, dq, now_a, now_b))
+    return tuple(jnp.concatenate(arrays, axis=1) for arrays in zip(*parts))
+
+
 def body(query, keys, values, grad_out, doc_starts):
     count = lax.axis_size("seq")
     device = lax.axis_index("seq")
     window = min(16, count // 2)
     span = query.shape[2]
-    heads = query.shape[3]
     kv_heads = keys.shape[3]
     dim = query.shape[4]
     scale = dim ** (-0.5)
     pairs_a, pairs_b = swap_pairs(count)
     parity = device % 2
-    chunks = 2
-    chunk = kv_heads // chunks
-
-    both = jnp.stack([keys[:, 0], values[:, 0]], axis=1)
-    both = jnp.transpose(both, (0, 3, 1, 2, 4))
-    half_of = (1 - parity, parity)
-    own = [
-        [
-            jnp.transpose(
-                lax.dynamic_slice(
-                    both, (half, c * chunk, 0, 0, 0), (1, chunk, 2, span, dim)
-                )[0],
-                (1, 0, 2, 3),
-            )
-            for half in half_of
-        ]
-        for c in range(chunks)
-    ]
-    history = [([own[c][0]], [own[c][1]]) for c in range(chunks)]
-    for _ in range(window):
-        for c in range(chunks):
-            line_a, line_b = history[c]
-            next_a = lax.ppermute(line_b[-1], "seq", pairs_a)
-            next_b = lax.ppermute(line_a[-1], "seq", pairs_b)
-            line_a.append(next_a)
-            line_b.append(next_b)
-
+
+    half_a, half_b = 1 - parity, parity
+    both = jnp.transpose(jnp.stack([keys[:, 0], values[:, 0]], axis=1), (0, 1, 3, 2, 4))
+    own_a, own_b = (
+        lax.dynamic_index_in_dim(both, half, 0, keepdims=False) for half in (half_a, half_b)
+    )
     q_t = jnp.transpose(query[:, 0], (0, 2, 1, 3))
     do_t = jnp.transpose(grad_out[:, 0], (0, 2, 1, 3))
     spans = jnp.stack([device, 2 * count - 1 - device])
-    token = (spans[:, None] * span + jnp.arange(span, dtype=jnp.int32)[None, :]).astype(jnp.int32)
-    starts = jnp.max(
-        jnp.where(doc_starts[None, None, :] <= token[:, :, None], doc_starts[None, None, :], 0),
-        axis=2,
-    )[:, None, :]
-    half_a, half_b = half_of
-    info = jnp.stack(
-        [half_a, half_b, jnp.where(half_a == 0, device, 2 * count - 1 - device),
-         jnp.where(half_b == 0, device, 2 * count - 1 - device)]
-    ).astype(jnp.int32)
-
-    outs, dqs, totals = [], [], []
-    for c in range(chunks):
-        out, dq, deep_a, deep_b, rest_a, rest_b = attention_chunk(
-            info, q_t, do_t, starts, history[c], c * chunk, scale
+    token = spans[:, None] * span + jnp.arange(span, dtype=jnp.int32)[None, :]
+    below = doc_starts[None, None, :] <= token[:, :, None]
+    starts = jnp.max(jnp.where(below, doc_starts[None, None, :], 0), axis=2)[:, None, :]
+    span_a = jnp.where(half_a == 0, device, 2 * count - 1 - device)
+    info = jnp.stack([half_a, half_b, span_a, 2 * count - 1 - span_a]).astype(jnp.int32)
+
+    if window == 2:
+        out, dq, final_a, final_b = two_span_window(
+            info, q_t, do_t, starts, own_a, own_b, pairs_a, pairs_b, scale
         )
-        outs.append(out)
-        dqs.append(dq)
-        totals.append((deep_a, deep_b, rest_a, rest_b))
-    finals = []
-    for c in range(chunks):
-        now_a, now_b, rest_a, rest_b = totals[c]
-        for t in range(window - 1, -1, -1):
-            from_a = lax.ppermute(now_a, "seq", pairs_a)
-            from_b = lax.ppermute(now_b, "seq", pairs_b)
-            now_a = (rest_a[t] + from_b.astype(jnp.float32)).astype(jnp.bfloat16)
-            now_b = (rest_b[t] + from_a.astype(jnp.float32)).astype(jnp.bfloat16)
-        finals.append((now_a, now_b))
-    slots = jnp.stack(
-        [jnp.concatenate([f[s] for f in finals], axis=1) for s in range(2)], axis=0
-    )
-    halves = jnp.where(parity == 0, slots[::-1], slots)
+    else:
+        out, dq, final_a, final_b = any_window(
+            info, q_t, do_t, starts, own_a, own_b, pairs_a, pairs_b, window, scale
+        )
+    halves = jnp.where(parity == 0, jnp.stack([final_b, final_a]), jnp.stack([final_a, final_b]))
     halves = jnp.transpose(halves, (1, 0, 3, 2, 4))[:, :, None]
-    out = jnp.transpose(jnp.concatenate(outs, axis=1), (0, 2, 1, 3))[:, None]
-    dq = jnp.transpose(jnp.concatenate(dqs, axis=1), (0, 2, 1, 3))[:, None]
+    out = jnp.transpose(out, (0, 2, 1, 3))[:, None]
+    dq = jnp.transpose(dq, (0, 2, 1, 3))[:, None]
     return out, dq, halves[0], halves[1]
 
 

time: 58 us -> 54.3 us (0.936)
  the two profiles are of different devices: /device:TPU:0 before, /device:TPU:8 now
where the time goes in v2:
time: 54.3 us; the launch traced here: 53.8 us
  starting transfers between devices  16.6 us (31%)
  local copies, waits for them, and re-layouts  15.8 us (29%)
  Pallas kernels  15 us (28%)
  waiting for transfers between devices  3.62 us (7%)
  other arithmetic  1.84 us (3%)
  between operations  0.9 us (2%)
    pallas_call x5, Pallas kernels, vmem_call(): pl.pallas_call(kernel, in_specs=[pl.BlockSpec(memory_space=pltpu.SMEM)] +...  15 us
    unnamed x21, local copies, waits for them, and re-layouts  12.6 us
    ppermute x1, starting transfers between devices, two_span_window(): b1 = lax.ppermute(own_a, 'seq', pairs_b)  5.04 us
    ppermute x1, starting transfers between devices, two_span_window(): b2 = lax.ppermute(a1, 'seq', pairs_b)  3.47 us
    ppermute x1, starting transfers between devices, two_span_window(): from_b = lax.ppermute(deep_b, 'seq', pairs_b)  3.16 us
    ppermute x1, starting transfers between devices, two_span_window(): last_b = lax.ppermute(next_b, 'seq', pairs_b)  2.67 us
    transpose x1, local copies, waits for them, and re-layouts, body(): do_t = jnp.transpose(grad_out[:, 0], (0, 2, 1, 3))  2.08 us
    ppermute x1, starting transfers between devices, two_span_window(): last_a = lax.ppermute(next_a, 'seq', pairs_a)  2.07 us
  transfers between devices with their start and end apart: 8, of which 3 were waited for; matrix products, arithmetic and copies ran while one was open for 13% of the time, Pallas kernels for 18%

profile of v2, /device:TPU:8, one launch (start us, length us, event | category | flops | bytes accessed | tf_op | source)
XLA Modules:
  0.0 53.8 jit_solution(3430773739529547633)
XLA Ops:
  0.6 1.0 %copy_dynamic-update-slice_fusion.1 = bf16[2,2,128,4,128]{4,2,3,1,0:T(8,128)(2,1)S(1)} fusion(bf16[2,1,128,4,128]{4,3,2,1,0:T(4,128)(2,1)} %param.6), kind=kLoop, calls=%fused_computation.14 | loop fusion | bytes 524288
  1.7 1.0 %copy_dynamic-update-slice_fusion = bf16[2,2,128,4,128]{4,2,3,1,0:T(8,128)(2,1)S(1)} fusion(bf16[2,2,128,4,128]{4,2,3,1,0:T(8,128)(2,1)S(1)} %copy_dynamic-update-slice_fusion.1, bf16[2,1,128,4,128]{4,3,2,1,0:T(4,128)(2,1)} %param.7), kind=kLoop, calls=%fused_computation.13 | loop fusion | bytes 524288 | tf_op jit(solution)/shard_map/stack | solution.py:370
  2.8 5.0 %collective-permute-start = (bf16[2,4,128,128]{3,2,1,0:T(8,128)(2,1)S(1)}, bf16[2,4,128,128]{3,2,1,0:T(8,128)(2,1)}, u32[]{:S(2)}, u32[]{:S(2)}) collective-permute-start(bf16[2,4,128,128]{3,2,1,0:T(8,128)(2,1)S(1)} %get-tuple-element.43.kv_a_ref.kv_a0), channel_id=1, source_target_pairs={{8,16},{16,8},{24,24},{9,17},{17,9},{25,25},{10,18},{18,10},{26,26... | collective-permute-start | bytes 786440 | tf_op jit(solution)/shard_map/ppermute | solution.py:305
  7.9 2.1 %copy_bitcast_fusion = (bf16[2,16,128,128]{3,2,1,0:T(8,128)(2,1)S(1)}, bf16[2,16,128,128]{3,2,1,0:T(8,128)(2,1)S(1)}) fusion(bf16[2,1,128,16,128]{4,3,2,1,0:T(8,128)(2,1)} %param.8, bf16[2,1,128,16,128]{4,3,2,1,0:T(8,128)(2,1)} %param.5), kind=kLoop, calls=%fused_computation | loop fusion | bytes 4194304 | tf_op jit(solution)/shard_map/transpose | solution.py:375
  10.8 3.5 %collective-permute-start.3 = (bf16[2,4,128,128]{3,2,1,0:T(8,128)(2,1)S(1)}, bf16[2,4,128,128]{3,2,1,0:T(8,128)(2,1)S(1)}, u32[]{:S(2)}, u32[]{:S(2)}) collective-permute-start(bf16[2,4,128,128]{3,2,1,0:T(8,128)(2,1)S(1)} %collective-permute-done.2.kv_a_ref.kv_a1), channel_id=1, source_target_pairs={{8,16},{16,8},{24,24},{9,17},{17,9},{25,25},{10,18},{18,10},{26,26... | collective-permute-start | bytes 786440 | tf_op jit(solution)/shard_map/ppermute | solution.py:308
  14.4 1.7 %scores_own.1 = (f32[2,4,128,512]{3,2,1,0:T(8,128)S(1)}, f32[2,4,128,512]{3,2,1,0:T(8,128)S(1)}) custom-call(s32[4]{0:T(128)S(1)} %pad_add_fusion.info_ref, bf16[2,16,128,128]{3,2,1,0:T(8,128)(2,1)S(1)} %get-tuple-element.45.q_ref, bf16[2,16,128,128]{3,2,1,0:T(8,128)(2,1)S(1)} %get-tuple-element.44.do_ref, ...), custom_call_target="tpu_custom_call" | custom-call | flops 1073741824 | bytes 2621440 | tf_op jit(solution)/shard_map/scores_own/pallas_call | solution.py:163
  16.4 2.2 %scores_prev.1 = (f32[2,4,128,512]{3,2,1,0:T(8,128)S(1)}, f32[2,4,128,512]{3,2,1,0:T(8,128)S(1)}) custom-call(s32[4]{0:T(128)S(1)} %pad_add_fusion.info_ref, bf16[2,16,128,128]{3,2,1,0:T(8,128)(2,1)S(1)} %get-tuple-element.45.q_ref, bf16[2,16,128,128]{3,2,1,0:T(8,128)(2,1)S(1)} %get-tuple-element.44.do_ref, ...), custom_call_target="tpu_custom_call" | custom-call | flops 1073741824 | bytes 2621440 | tf_op jit(solution)/shard_map/scores_prev/pallas_call | solution.py:163
  18.5 1.5 %collective-permute-done.3.kv_b_ref.kv_b2 = bf16[2,4,128,128]{3,2,1,0:T(8,128)(2,1)S(1)} collective-permute-done((bf16[2,4,128,128]{3,2,1,0:T(8,128)(2,1)S(1)}, bf16[2,4,128,128]{3,2,1,0:T(8,128)(2,1)S(1)}, u32[]{:S(2)}, u32[]{:S(2)}) %collective-permute-start.3) | collective-permute-done | bytes 262176 | tf_op jit(solution)/shard_map/ppermute | solution.py:308
  20.0 1.5 %collective-permute-done.1.kv_a_ref.kv_a2 = bf16[2,4,128,128]{3,2,1,0:T(8,128)(2,1)S(1)} collective-permute-done((bf16[2,4,128,128]{3,2,1,0:T(8,128)(2,1)}, bf16[2,4,128,128]{3,2,1,0:T(8,128)(2,1)S(1)}, u32[]{:S(2)}, u32[]{:S(2)}) %collective-permute-start.1) | collective-permute-done | bytes 262176 | tf_op jit(solution)/shard_map/ppermute | solution.py:309
  21.5 5.6 %softmax.1 = (bf16[2,4,128,128]{3,2,1,0:T(8,128)(2,1)S(1)}, bf16[2,4,128,128]{3,2,1,0:T(8,128)(2,1)}, bf16[2,4,2,128,512]{4,3,2,1,0:T(8,128)(2,1)S(1)}, bf16[2,4,2,128,512]{4,3,2,1,0:T(8,128)(2,1)S(1)}) custom-call(s32[4]{0:T(128)S(1)} %pad_add_fusion.info_ref, s32[2,1,128]{2,1,0:T(1,128)S(1)} %bitcast.41, ...), custom_call_target="tpu_custom_call" | custom-call | flops 2147483648 | bytes 11011072 | tf_op jit(solution)/shard_map/softmax/pallas_call | solution.py:163
  27.1 1.3 %copy-done = bf16[2,4,2,128,512]{4,3,2,1,0:T(8,128)(2,1)} copy-done((bf16[2,4,2,128,512]{4,3,2,1,0:T(8,128)(2,1)}, bf16[2,4,2,128,512]{4,3,2,1,0:T(8,128)(2,1)S(1)}, u32[]{:S(2)}) %copy-start) | copy-done | bytes 2097176
  28.4 1.3 %copy-done.3 = bf16[2,4,2,128,512]{4,3,2,1,0:T(8,128)(2,1)} copy-done((bf16[2,4,2,128,512]{4,3,2,1,0:T(8,128)(2,1)}, bf16[2,4,2,128,512]{4,3,2,1,0:T(8,128)(2,1)S(1)}, u32[]{:S(2)}) %copy-start.3) | copy-done | bytes 2097176
  30.4 3.2 %collective-permute-start.4 = (bf16[2,4,128,128]{3,2,1,0:T(8,128)(2,1)}, bf16[2,4,128,128]{3,2,1,0:T(8,128)(2,1)}, u32[]{:S(2)}, u32[]{:S(2)}) collective-permute-start(bf16[2,4,128,128]{3,2,1,0:T(8,128)(2,1)} %get-tuple-element.28), channel_id=1, source_target_pairs={{8,16},{16,8},{24,24},{9,17},{17,9},{25,25},{10,18},{18,10},{26,26... | collective-permute-start | bytes 786440 | tf_op jit(solution)/shard_map/ppermute | solution.py:315
  33.7 1.6 %copy-done.1 = bf16[2,4,2,128,512]{4,3,2,1,0:T(8,128)(2,1)S(1)} copy-done((bf16[2,4,2,128,512]{4,3,2,1,0:T(8,128)(2,1)S(1)}, bf16[2,4,2,128,512]{4,3,2,1,0:T(8,128)(2,1)}, u32[]{:S(2)}) %copy-start.1) | copy-done | bytes 2097176
  35.3 1.6 %copy-done.4 = bf16[2,4,2,128,512]{4,3,2,1,0:T(8,128)(2,1)S(1)} copy-done((bf16[2,4,2,128,512]{4,3,2,1,0:T(8,128)(2,1)S(1)}, bf16[2,4,2,128,512]{4,3,2,1,0:T(8,128)(2,1)}, u32[]{:S(2)}) %copy-start.4) | copy-done | bytes 2097176
  36.9 2.3 %terms.1 = (f32[2,4,128,128]{3,2,1,0:T(8,128)S(1)}, f32[2,4,128,128]{3,2,1,0:T(8,128)S(1)}, f32[2,4,128,128]{3,2,1,0:T(8,128)S(1)}, f32[2,4,128,128]{3,2,1,0:T(8,128)S(1)}) custom-call(s32[4]{0:T(128)S(1)} %pad_add_fusion.info_ref, bf16[2,16,128,128]{3,2,1,0:T(8,128)(2,1)S(1)} %get-tuple-element.45.q_ref, ...), custom_call_target="tpu_custom_call" | custom-call | flops 2147483648 | bytes 6291456 | tf_op jit(solution)/shard_map/terms/pallas_call | solution.py:163
  39.2 1.2 %add_convert_fusion.3 = bf16[2,4,128,128]{3,2,1,0:T(8,128)(2,1)S(1)} fusion(f32[2,4,128,128]{3,2,1,0:T(8,128)S(1)} %get-tuple-element.27, bf16[2,4,128,128]{3,2,1,0:T(8,128)(2,1)} %collective-permute-done.4), kind=kLoop, calls=%fused_computation.7 | loop fusion | flops 393216 | bytes 1048576 | tf_op jit(solution)/shard_map/convert_element_type | solution.py:325
  40.3 2.1 %collective-permute-start.5 = (bf16[2,4,128,128]{3,2,1,0:T(8,128)(2,1)S(1)}, bf16[2,4,128,128]{3,2,1,0:T(8,128)(2,1)S(1)}, u32[]{:S(2)}, u32[]{:S(2)}) collective-permute-start(bf16[2,4,128,128]{3,2,1,0:T(8,128)(2,1)S(1)} %add_convert_fusion.3), channel_id=1, source_target_pairs={{0,8},{8,0},{16,24},{24,16},{1,9},{9,1},{17,25},{25,17},{2,10},{10... | collective-permute-start | bytes 786440 | tf_op jit(solution)/shard_map/ppermute | solution.py:327
  42.5 2.7 %collective-permute-start.7 = (bf16[2,4,128,128]{3,2,1,0:T(8,128)(2,1)S(1)}, bf16[2,4,128,128]{3,2,1,0:T(8,128)(2,1)S(1)}, u32[]{:S(2)}, u32[]{:S(2)}) collective-permute-start(bf16[2,4,128,128]{3,2,1,0:T(8,128)(2,1)S(1)} %add_convert_fusion.1), channel_id=1, source_target_pairs={{8,16},{16,8},{24,24},{9,17},{17,9},{25,25},{10,18},{18,10},{26,26... | collective-permute-start | bytes 786440 | tf_op jit(solution)/shard_map/ppermute | solution.py:326
  45.2 3.3 %outputs.1 = (bf16[2,16,128,128]{3,2,1,0:T(8,128)(2,1)S(1)}, bf16[2,16,128,128]{3,2,1,0:T(8,128)(2,1)S(1)}) custom-call(s32[4]{0:T(128)S(1)} %pad_add_fusion.info_ref, bf16[2,4,2,128,512]{4,3,2,1,0:T(8,128)(2,1)S(1)} %copy-done.2, bf16[2,4,2,128,512]{4,3,2,1,0:T(8,128)(2,1)S(1)} %copy-done.5, bf16[2,4,128,128]{3,2,1,0:T(8,128)(2,1)S(1)} %get-tuple-element.43.kv_a_ref.kv_a0, ...), custom_call_target="tpu_custom_call" | custom-call | flops 3221225472 | bytes 5767168 | tf_op jit(solution)/shard_map/outputs/pallas_call | solution.py:163
  48.5 1.6 %copy.21 = bf16[2,1,128,16,128]{4,3,2,1,0:T(8,128)(2,1)} copy(bf16[2,1,128,16,128]{4,2,3,0,1:T(8,128)(2,1)S(1)} %bitcast.40) | data formatting | bytes 2097152
  50.1 1.6 %copy.22 = bf16[2,1,128,16,128]{4,3,2,1,0:T(8,128)(2,1)} copy(bf16[2,1,128,16,128]{4,2,3,0,1:T(8,128)(2,1)S(1)} %bitcast.39) | data formatting | bytes 2097152
  52.0 0.9 %copy.24 = bf16[2,1,128,4,128]{4,3,2,1,0:T(4,128)(2,1)} copy(bf16[2,1,128,4,128]{4,2,3,0,1:T(8,128)(2,1)S(1)} %get-tuple-element.40) | data formatting | bytes 524288
  52.9 0.9 %copy.23 = bf16[2,1,128,4,128]{4,3,2,1,0:T(4,128)(2,1)} copy(bf16[2,1,128,4,128]{4,2,3,0,1:T(8,128)(2,1)S(1)} %get-tuple-element.41) | data formatting | bytes 524288
  (31 shorter events, 2.4 us)
Async XLA Ops:
  2.7 8.1 %collective-permute-start.2 = (bf16[2,4,128,128]{3,2,1,0:T(8,128)(2,1)S(1)}, bf16[2,4,128,128]{3,2,1,0:T(8,128)(2,1)S(1)}, u32[]{:S(2)}, u32[]{:S(2)}) collective-permute-start(bf16[2,4,128,128]{3,2,1,0:T(8,128)(2,1)S(1)} %get-tuple-element.42.kv_b_ref.kv_b0), channel_id=1, source_target_pairs={{0,8},{8,0},{16,24},{24,16},{1,9},{9,1},{17,25},{25,17},{2,10},{10... | collective-permute-start | bytes 786440 | tf_op jit(solution)/shard_map/ppermute | solution.py:306
  2.8 11.5 %collective-permute-start = (bf16[2,4,128,128]{3,2,1,0:T(8,128)(2,1)S(1)}, bf16[2,4,128,128]{3,2,1,0:T(8,128)(2,1)}, u32[]{:S(2)}, u32[]{:S(2)}) collective-permute-start(bf16[2,4,128,128]{3,2,1,0:T(8,128)(2,1)S(1)} %get-tuple-element.43.kv_a_ref.kv_a0), channel_id=1, source_target_pairs={{8,16},{16,8},{24,24},{9,17},{17,9},{25,25},{10,18},{18,10},{26,26... | collective-permute-start | bytes 786440 | tf_op jit(solution)/shard_map/ppermute | solution.py:305
  10.0 6.1 %copy-start.7 = (s32[512]{0:T(512)S(1)}, s32[512]{0:T(512)}, u32[]{:S(2)}) copy-start(s32[512]{0:T(512)} %param.9) | copy-start | bytes 6148
  10.8 9.2 %collective-permute-start.3 = (bf16[2,4,128,128]{3,2,1,0:T(8,128)(2,1)S(1)}, bf16[2,4,128,128]{3,2,1,0:T(8,128)(2,1)S(1)}, u32[]{:S(2)}, u32[]{:S(2)}) collective-permute-start(bf16[2,4,128,128]{3,2,1,0:T(8,128)(2,1)S(1)} %collective-permute-done.2.kv_a_ref.kv_a1), channel_id=1, source_target_pairs={{8,16},{16,8},{24,24},{9,17},{17,9},{25,25},{10,18},{18,10},{26,26... | collective-permute-start | bytes 786440 | tf_op jit(solution)/shard_map/ppermute | solution.py:308
  14.3 7.2 %collective-permute-start.1 = (bf16[2,4,128,128]{3,2,1,0:T(8,128)(2,1)}, bf16[2,4,128,128]{3,2,1,0:T(8,128)(2,1)S(1)}, u32[]{:S(2)}, u32[]{:S(2)}) collective-permute-start(bf16[2,4,128,128]{3,2,1,0:T(8,128)(2,1)} %collective-permute-done.kv_b_ref.kv_b1), channel_id=1, source_target_pairs={{0,8},{8,0},{16,24},{24,16},{1,9},{9,1},{17,25},{25,17},{2,10},{10... | collective-permute-start | bytes 786440 | tf_op jit(solution)/shard_map/ppermute | solution.py:309
  27.1 1.3 %copy-start = (bf16[2,4,2,128,512]{4,3,2,1,0:T(8,128)(2,1)}, bf16[2,4,2,128,512]{4,3,2,1,0:T(8,128)(2,1)S(1)}, u32[]{:S(2)}) copy-start(bf16[2,4,2,128,512]{4,3,2,1,0:T(8,128)(2,1)S(1)} %get-tuple-element.22.low_ref) | copy-start | bytes 6291460
  28.4 1.3 %copy-start.3 = (bf16[2,4,2,128,512]{4,3,2,1,0:T(8,128)(2,1)}, bf16[2,4,2,128,512]{4,3,2,1,0:T(8,128)(2,1)S(1)}, u32[]{:S(2)}) copy-start(bf16[2,4,2,128,512]{4,3,2,1,0:T(8,128)(2,1)S(1)} %get-tuple-element.23.ds_ref) | copy-start | bytes 6291460
  29.7 0.7 %copy-start.6 = (bf16[2,4,128,128]{3,2,1,0:T(8,128)(2,1)}, bf16[2,4,128,128]{3,2,1,0:T(8,128)(2,1)S(1)}, u32[]{:S(2)}) copy-start(bf16[2,4,128,128]{3,2,1,0:T(8,128)(2,1)S(1)} %get-tuple-element.31) | copy-start | bytes 786436
  30.4 8.7 %collective-permute-start.4 = (bf16[2,4,128,128]{3,2,1,0:T(8,128)(2,1)}, bf16[2,4,128,128]{3,2,1,0:T(8,128)(2,1)}, u32[]{:S(2)}, u32[]{:S(2)}) collective-permute-start(bf16[2,4,128,128]{3,2,1,0:T(8,128)(2,1)} %get-tuple-element.28), channel_id=1, source_target_pairs={{8,16},{16,8},{24,24},{9,17},{17,9},{25,25},{10,18},{18,10},{26,26... | collective-permute-start | bytes 786440 | tf_op jit(solution)/shard_map/ppermute | solution.py:315
  33.6 8.8 %collective-permute-start.6 = (bf16[2,4,128,128]{3,2,1,0:T(8,128)(2,1)}, bf16[2,4,128,128]{3,2,1,0:T(8,128)(2,1)S(1)}, u32[]{:S(2)}, u32[]{:S(2)}) collective-permute-start(bf16[2,4,128,128]{3,2,1,0:T(8,128)(2,1)} %copy-done.6), channel_id=1, source_target_pairs={{0,8},{8,0},{16,24},{24,16},{1,9},{9,1},{17,25},{25,17},{2,10},{10... | collective-permute-start | bytes 786440 | tf_op jit(solution)/shard_map/ppermute | solution.py:316
  33.7 1.6 %copy-start.1 = (bf16[2,4,2,128,512]{4,3,2,1,0:T(8,128)(2,1)S(1)}, bf16[2,4,2,128,512]{4,3,2,1,0:T(8,128)(2,1)}, u32[]{:S(2)}) copy-start(bf16[2,4,2,128,512]{4,3,2,1,0:T(8,128)(2,1)} %copy-done) | copy-start | bytes 6291460
  35.3 1.6 %copy-start.4 = (bf16[2,4,2,128,512]{4,3,2,1,0:T(8,128)(2,1)S(1)}, bf16[2,4,2,128,512]{4,3,2,1,0:T(8,128)(2,1)}, u32[]{:S(2)}) copy-start(bf16[2,4,2,128,512]{4,3,2,1,0:T(8,128)(2,1)} %copy-done.3) | copy-start | bytes 6291460
  36.9 8.3 %copy-start.5 = (bf16[2,4,2,128,512]{4,3,2,1,0:T(8,128)(2,1)S(1)}, bf16[2,4,2,128,512]{4,3,2,1,0:T(8,128)(2,1)}, u32[]{:S(2)}) copy-start(bf16[2,4,2,128,512]{4,3,2,1,0:T(8,128)(2,1)} %copy-done.3) | copy-start | bytes 6291460
  39.1 6.0 %copy-start.2 = (bf16[2,4,2,128,512]{4,3,2,1,0:T(8,128)(2,1)S(1)}, bf16[2,4,2,128,512]{4,3,2,1,0:T(8,128)(2,1)}, u32[]{:S(2)}) copy-start(bf16[2,4,2,128,512]{4,3,2,1,0:T(8,128)(2,1)} %copy-done) | copy-start | bytes 6291460
  40.3 11.4 %collective-permute-start.5 = (bf16[2,4,128,128]{3,2,1,0:T(8,128)(2,1)S(1)}, bf16[2,4,128,128]{3,2,1,0:T(8,128)(2,1)S(1)}, u32[]{:S(2)}, u32[]{:S(2)}) collective-permute-start(bf16[2,4,128,128]{3,2,1,0:T(8,128)(2,1)S(1)} %add_convert_fusion.3), channel_id=1, source_target_pairs={{0,8},{8,0},{16,24},{24,16},{1,9},{9,1},{17,25},{25,17},{2,10},{10... | collective-permute-start | bytes 786440 | tf_op jit(solution)/shard_map/ppermute | solution.py:327
  42.5 9.4 %collective-permute-start.7 = (bf16[2,4,128,128]{3,2,1,0:T(8,128)(2,1)S(1)}, bf16[2,4,128,128]{3,2,1,0:T(8,128)(2,1)S(1)}, u32[]{:S(2)}, u32[]{:S(2)}) collective-permute-start(bf16[2,4,128,128]{3,2,1,0:T(8,128)(2,1)S(1)} %add_convert_fusion.1), channel_id=1, source_target_pairs={{8,16},{16,8},{24,24},{9,17},{17,9},{25,25},{10,18},{18,10},{26,26... | collective-permute-start | bytes 786440 | tf_op jit(solution)/shard_map/ppermute | solution.py:326

commit v3 on v2

v3 whole, which is shorter than its diff:
```python
import functools

import jax
import jax.numpy as jnp
from jax import lax
from jax.experimental import pallas as pl
from jax.experimental.pallas import tpu as pltpu
from jax.sharding import PartitionSpec as P

LOG2E = 1.4426950408889634
NEG = -1e30


def swap_pairs(count):
    pairs_a = []
    for i in range(0, count - 1, 2):
        pairs_a += [(i, i + 1), (i + 1, i)]
    pairs_b = []
    for i in range(1, count - 1, 2):
        pairs_b += [(i, i + 1), (i + 1, i)]
    pairs_b.append((count - 1, count - 1))
    return pairs_a, pairs_b


def contract(lhs, rhs, lhs_dim, rhs_dim):
    return lax.dot_general(
        lhs, rhs, (((lhs_dim,), (rhs_dim,)), ((), ())), preferred_element_type=jnp.float32
    )


def attention_kernel(blocks, scale, info_ref, q_ref, do_ref, starts_ref, *refs):
    kv_refs = (refs[0:blocks], refs[blocks : 2 * blocks])
    o_ref, dq_ref = refs[2 * blocks : 2 * blocks + 2]
    deep_refs = refs[2 * blocks + 2 : 2 * blocks + 4]
    rest_refs = refs[2 * blocks + 4 : 2 * blocks + 6]
    k_all, v_all, s_all, p_all = refs[2 * blocks + 6 :]
    group, span, dim = q_ref.shape[1:]
    rows = group * span

    def each(body, init):
        if blocks <= 4:
            for t in range(blocks):
                init = body(t, init)
            return init
        return lax.fori_loop(0, blocks, body, init)

    for slot in range(2):
        half = info_ref[slot]
        span_first = info_ref[2 + slot] * span
        for t in range(blocks):
            k_all[t] = kv_refs[slot][t][0, 0]
            v_all[t] = kv_refs[slot][t][1, 0]
        queries = q_ref[half].reshape(rows, dim)
        grad_out = do_ref[half].reshape(rows, dim)
        start = starts_ref[half]
        token = span_first + lax.broadcasted_iota(jnp.int32, (1, span), 1)
        key_row = span_first + lax.broadcasted_iota(jnp.int32, (span, span), 0)

        def scores(t, top):
            key_pos = key_row - t * span
            allowed = (key_pos >= start) & (key_pos <= token)
            bias = jnp.where(allowed, 0.0, NEG)
            value = contract(k_all[t], queries, 1, 1) + jnp.concatenate([bias] * group, axis=1)
            s_all[t] = value
            return jnp.maximum(top, jnp.max(value, axis=0, keepdims=True))

        top = each(scores, jnp.full((1, rows), NEG, jnp.float32))

        def expons(t, total):
            value = jnp.exp2((s_all[t] - top) * (scale * LOG2E))
            s_all[t] = value
            return total + jnp.sum(value, axis=0, keepdims=True)

        total = each(expons, jnp.zeros((1, rows), jnp.float32))
        inverse = 1.0 / total

        def forward(t, carry):
            out, delta = carry
            weights = s_all[t] * inverse
            low = weights.astype(jnp.bfloat16)
            grad_weights = contract(v_all[t], grad_out, 1, 1)
            s_all[t] = weights
            p_all[t] = grad_weights
            delta = delta + jnp.sum(weights * grad_weights, axis=0, keepdims=True)
            out = out + contract(v_all[t], low, 0, 0)
            grad_value = contract(low, grad_out, 1, 0)
            store_term(t, 1, grad_value)
            return out, delta

        def store_term(t, which, value):
            if isinstance(t, int):
                if t == blocks - 1:
                    deep_refs[slot][which, 0] = value.astype(jnp.bfloat16)
                else:
                    rest_refs[slot][t, which, 0] = value
            else:
                @pl.when(t == blocks - 1)
                def _():
                    deep_refs[slot][which, 0] = value.astype(jnp.bfloat16)

                @pl.when(t < blocks - 1)
                def _():
                    rest_refs[slot][t, which, 0] = value

        out, delta = each(
            forward, (jnp.zeros((dim, rows), jnp.float32), jnp.zeros((1, rows), jnp.float32))
        )

        def backward(t, grad_query):
            low = (s_all[t] * (p_all[t] - delta)).astype(jnp.bfloat16)
            store_term(t, 0, contract(low, queries, 1, 0) * scale)
            return grad_query + contract(k_all[t], low, 0, 0)

        grad_query = each(backward, jnp.zeros((dim, rows), jnp.float32)) * scale
        for g in range(group):
            columns = slice(g * span, (g + 1) * span)
            o_ref[half, g] = out[:, columns].T.astype(jnp.bfloat16)
            dq_ref[half, g] = grad_query[:, columns].T.astype(jnp.bfloat16)


def attention_chunk(info, q_t, do_t, starts, kv_blocks, first_head, scale):
    blocks = len(kv_blocks[0])
    _, heads, span, dim = q_t.shape
    chunk = kv_blocks[0][0].shape[1]
    group = 4
    rows = group * span
    window = blocks - 1
    q_spec = pl.BlockSpec((2, group, span, dim), lambda m, info: (0, first_head + m, 0, 0))
    o_spec = pl.BlockSpec((2, group, span, dim), lambda m, info: (0, m, 0, 0))
    kv_spec = pl.BlockSpec((2, 1, span, dim), lambda m, info: (0, m, 0, 0))
    rest_spec = pl.BlockSpec((window, 2, 1, span, dim), lambda m, info: (0, 0, m, 0, 0))
    starts_spec = pl.BlockSpec((2, 1, span), lambda m, info: (0, 0, 0))
    deep = jax.ShapeDtypeStruct((2, chunk, span, dim), jnp.bfloat16)
    rest = jax.ShapeDtypeStruct((window, 2, chunk, span, dim), jnp.float32)
    out = jax.ShapeDtypeStruct((2, chunk * group, span, dim), jnp.bfloat16)
    macs = 2 * chunk * 5 * rows * blocks * span * dim
    return pl.pallas_call(
        functools.partial(attention_kernel, blocks, scale),
        grid_spec=pltpu.PrefetchScalarGridSpec(
            num_scalar_prefetch=1,
            grid=(chunk,),
            in_specs=[q_spec, q_spec, starts_spec] + [kv_spec] * (2 * blocks),
            out_specs=[o_spec, o_spec, kv_spec, kv_spec, rest_spec, rest_spec],
            scratch_shapes=[
                pltpu.VMEM((blocks, span, dim), jnp.bfloat16),
                pltpu.VMEM((blocks, span, dim), jnp.bfloat16),
                pltpu.VMEM((blocks, span, rows), jnp.float32),
                pltpu.VMEM((blocks, span, rows), jnp.float32),
            ],
        ),
        out_shape=[out, out, deep, deep, rest, rest],
        compiler_params=pltpu.CompilerParams(vmem_limit_bytes=48 * 1024 * 1024),
        cost_estimate=pl.CostEstimate(
            flops=2 * macs, bytes_accessed=8 * 1024 * 1024, transcendentals=0
        ),
        name="attention",
    )(info, q_t, do_t, starts, *kv_blocks[0], *kv_blocks[1])


def vmem_call(kernel, out_shape, macs, name, *args, aliases=None):
    whole = pl.BlockSpec(memory_space=pltpu.VMEM)
    moved = sum(a.size * a.dtype.itemsize for a in args[1:])
    return pl.pallas_call(
        kernel,
        in_specs=[pl.BlockSpec(memory_space=pltpu.SMEM)] + [whole] * (len(args) - 1),
        out_specs=[whole] * len(out_shape),
        out_shape=out_shape,
        input_output_aliases=aliases or {},
        compiler_params=pltpu.CompilerParams(vmem_limit_bytes=16 * 1024 * 1024),
        cost_estimate=pl.CostEstimate(flops=8 * macs, bytes_accessed=moved, transcendentals=0),
        name=name,
    )(*args)


def group_of(ref, half, m, group):
    return ref[half, pl.ds(m * group, group)].reshape(group * ref.shape[2], ref.shape[3])


def later_keys(span, group, dtype):
    row = lax.broadcasted_iota(jnp.int32, (span, span), 0)
    column = lax.broadcasted_iota(jnp.int32, (span, span), 1)
    return jnp.concatenate([(row > column).astype(jnp.float32).astype(dtype)] * group, axis=1)


def softmax_kernel(scale, first_head, info_ref, starts_ref, q_ref, do_ref, own_a, own_b, prev_a, prev_b, far_a, far_b, *refs):
    deep_refs = refs[-4:-2]
    low_ref, ds_ref = refs[-2:]
    heads, span, rows = low_ref.shape[1], low_ref.shape[3], low_ref.shape[4]
    group = rows // span
    row = lax.broadcasted_iota(jnp.int32, (span, span), 0)
    column = lax.broadcasted_iota(jnp.int32, (span, span), 1)
    far = row > column
    far_wide = jnp.concatenate([far] * group, axis=1)
    far_low = later_keys(span, group, jnp.bfloat16)
    slots = range(2)
    halves, bias, bias_prev = [], [], []
    for slot in slots:
        half = info_ref[slot]
        first = info_ref[2 + slot] * span
        start = starts_ref[half]
        position = jnp.where(far, first - 2 * span + row, first + row)
        halves.append(half)
        bias.append(jnp.where(position >= start, 0.0, NEG))
        bias_prev.append(jnp.where(first - span + row >= start, 0.0, NEG))
    kv_refs = ((own_a, prev_a, far_a), (own_b, prev_b, far_b))

    def one_head(step, carry):
        m = first_head + step
        queries = [group_of(q_ref, halves[i], m, group) for i in slots]
        grad_out = [group_of(do_ref, halves[i], m, group) for i in slots]
        scores, grads = [], []
        for i in slots:
            own, prev, far_kv = kv_refs[i]
            for which, rhs, result in ((0, queries[i], scores), (1, grad_out[i], grads)):
                stack = jnp.concatenate([own[m, which], prev[m, which], far_kv[step, which]], axis=0)
                result.append(contract(stack, rhs, 1, 1))
        near_s = [
            jnp.where(far_wide, x[2 * span :], x[:span]) + jnp.concatenate([bias[i]] * group, axis=1)
            for i, x in enumerate(scores)
        ]
        prev_s = [
            x[span : 2 * span] + jnp.concatenate([bias_prev[i]] * group, axis=1)
            for i, x in enumerate(scores)
        ]
        near_dp = [jnp.where(far_wide, x[2 * span :], x[:span]) for x in grads]
        prev_dp = [x[span : 2 * span] for x in grads]
        top = [jnp.max(jnp.maximum(near_s[i], prev_s[i]), axis=0, keepdims=True) for i in slots]
        near_e = [jnp.exp2((near_s[i] - top[i]) * (scale * LOG2E)) for i in slots]
        prev_e = [jnp.exp2((prev_s[i] - top[i]) * (scale * LOG2E)) for i in slots]
        inverse = [1.0 / jnp.sum(near_e[i] + prev_e[i], axis=0, keepdims=True) for i in slots]
        near_w = [near_e[i] * inverse[i] for i in slots]
        prev_w = [prev_e[i] * inverse[i] for i in slots]
        delta = [
            jnp.sum(near_w[i] * near_dp[i] + prev_w[i] * prev_dp[i], axis=0, keepdims=True)
            for i in slots
        ]
        near_low = [x.astype(jnp.bfloat16) for x in near_w]
        near_ds = [(near_w[i] * (near_dp[i] - delta[i])).astype(jnp.bfloat16) for i in slots]
        for i in slots:
            low_ref[i, m, 0] = near_low[i]
            ds_ref[i, m, 0] = near_ds[i]
            low_ref[i, m, 1] = prev_w[i].astype(jnp.bfloat16)
            ds_ref[i, m, 1] = (prev_w[i] * (prev_dp[i] - delta[i])).astype(jnp.bfloat16)
        for i in slots:
            key_term = contract(near_ds[i] * far_low, queries[i], 1, 0) * scale
            value_term = contract(near_low[i] * far_low, grad_out[i], 1, 0)
            deep_refs[i][m, 0] = key_term.astype(jnp.bfloat16)
            deep_refs[i][m, 1] = value_term.astype(jnp.bfloat16)
        return carry

    lax.fori_loop(0, far_a.shape[0], one_head, 0)


def rest_kernel(scale, info_ref, q_ref, do_ref, low_ref, ds_ref, *refs):
    own_kv, prev_kv, far_kv = refs[0:2], refs[2:4], refs[4:8]
    prev_refs = refs[8:10]
    late_refs, late_scratch, sems = refs[10:14], refs[14:18], refs[18]
    own_refs = late_scratch[:2]
    o_ref, dq_ref = late_scratch[2:]
    heads, _, span, rows = low_ref.shape[1:]
    chunk = far_kv[0].shape[0]
    group = rows // span
    far_low = later_keys(span, group, jnp.bfloat16)
    own_low = 1 - far_low

    def copies(m):
        blocks = (pl.ds(m, 1), pl.ds(m, 1)) + ((slice(None), pl.ds(m * group, group)),) * 2
        return [
            pltpu.make_async_copy(scratch.at[block], ref.at[block], sems.at[m, i])
            for i, (scratch, ref, block) in enumerate(zip(late_scratch, late_refs, blocks))
        ]

    def one_head(far_pair, first_head, step, carry):
        m = first_head + step
        for slot in range(2):
            half = info_ref[slot]
            own, prev, far = own_kv[slot], prev_kv[slot], far_pair[slot]
            queries = group_of(q_ref, half, m, group)
            grad_out = group_of(do_ref, half, m, group)
            low = low_ref[slot, m, 0]
            ds = ds_ref[slot, m, 0]
            low = jnp.concatenate([low_ref[slot, m, 1], low * own_low, low * far_low], axis=0)
            ds = jnp.concatenate([ds_ref[slot, m, 1], ds * own_low, ds * far_low], axis=0)
            grad_key = contract(ds[: 2 * span], queries, 1, 0) * scale
            grad_value = contract(low[: 2 * span], grad_out, 1, 0)
            prev_refs[slot][m, 0] = grad_key[:span]
            prev_refs[slot][m, 1] = grad_value[:span]
            own_refs[slot][m, 0] = grad_key[span:]
            own_refs[slot][m, 1] = grad_value[span:]
            keys = jnp.concatenate([prev[m, 0], own[m, 0], far[step, 0]], axis=0)
            values = jnp.concatenate([prev[m, 1], own[m, 1], far[step, 1]], axis=0)
            out = contract(values, low, 0, 0)
            grad_query = contract(keys, ds, 0, 0) * scale
            for g in range(group):
                columns = slice(g * span, (g + 1) * span)
                o_ref[half, m * group + g] = out[:, columns].T.astype(jnp.bfloat16)
                dq_ref[half, m * group + g] = grad_query[:, columns].T.astype(jnp.bfloat16)
        for copy in copies(m):
            copy.start()
        return carry

    for c in range(heads // chunk):
        lax.fori_loop(0, chunk, functools.partial(one_head, far_kv[2 * c : 2 * c + 2], c * chunk), 0)

    def finish(m, carry):
        for copy in copies(m):
            copy.wait()
        return carry

    lax.fori_loop(0, heads, finish, 0)


def rest_call(scale, macs, info, q_t, do_t, low, ds, own, prev, far):
    kv_heads = own[0].shape[0]
    whole = pl.BlockSpec(memory_space=pltpu.VMEM)
    outside = pl.BlockSpec(memory_space=pltpu.HBM)
    shape = jax.ShapeDtypeStruct
    terms = [shape(own[0].shape, jnp.float32)] * 4
    outs = [shape(q_t.shape, jnp.bfloat16)] * 2
    return pl.pallas_call(
        functools.partial(rest_kernel, scale),
        in_specs=[pl.BlockSpec(memory_space=pltpu.SMEM)] + [whole] * 12,
        out_specs=[whole] * 2 + [outside] * 4,
        out_shape=terms + outs,
        scratch_shapes=[pltpu.VMEM(x.shape, x.dtype) for x in terms[2:] + outs]
        + [pltpu.SemaphoreType.DMA((kv_heads, 4))],
        compiler_params=pltpu.CompilerParams(vmem_limit_bytes=16 * 1024 * 1024),
        cost_estimate=pl.CostEstimate(
            flops=8 * macs, bytes_accessed=8 * 1024 * 1024, transcendentals=0
        ),
        name="rest",
    )(info, q_t, do_t, low, ds, *own, *prev, *far)


def pack_kernel(info_ref, keys_ref, values_ref, own_a_ref, own_b_ref, raw, sems):
    copies = []
    for slot in (1, 0):
        for which, ref in enumerate((keys_ref, values_ref)):
            copies.append(
                pltpu.make_async_copy(
                    ref.at[info_ref[slot], 0], raw.at[slot, which], sems.at[slot, which]
                )
            )
            copies[-1].start()
    index = 0
    for slot in (1, 0):
        own_ref = (own_a_ref, own_b_ref)[slot]
        for which in range(2):
            copies[index].wait()
            index += 1
            tokens = jnp.swapaxes(raw[slot, which].astype(jnp.float32), 0, 1)
            own_ref[:, which] = tokens.astype(jnp.bfloat16)


def pack_call(info, keys, values):
    _, _, span, kv_heads, dim = keys.shape
    outside = pl.BlockSpec(memory_space=pl.ANY)
    whole = pl.BlockSpec(memory_space=pltpu.VMEM)
    return pl.pallas_call(
        pack_kernel,
        in_specs=[pl.BlockSpec(memory_space=pltpu.SMEM), outside, outside],
        out_specs=[whole] * 2,
        out_shape=[jax.ShapeDtypeStruct((kv_heads, 2, span, dim), jnp.bfloat16)] * 2,
        scratch_shapes=[
            pltpu.VMEM((2, 2, span, kv_heads, dim), jnp.bfloat16),
            pltpu.SemaphoreType.DMA((2, 2)),
        ],
        name="pack",
    )(info, keys, values)


def unpack_kernel(info_ref, own_a, own_b, last_a, last_b, grad_keys_ref, grad_values_ref):
    for slot, (own, last) in enumerate(((own_a, last_b), (own_b, last_a))):
        half = info_ref[slot]
        for which, ref in enumerate((grad_keys_ref, grad_values_ref)):
            total = own[:, which] + last[:, which].astype(jnp.float32)
            ref[half, 0] = jnp.swapaxes(total, 0, 1).astype(jnp.bfloat16)


def two_span_window(info, q_t, do_t, starts, own_a, own_b, pairs_a, pairs_b, scale):
    kv_heads, _, span, dim = own_a.shape
    heads = q_t.shape[1]
    rows = heads // kv_heads * span
    block = 2 * kv_heads * rows * span * dim
    chunk = kv_heads // 2
    shape = jax.ShapeDtypeStruct
    lows = [shape((2, kv_heads, 2, span, rows), jnp.bfloat16)] * 2
    deeps = [shape(own_a.shape, jnp.bfloat16)] * 2

    b1 = lax.ppermute(own_a, "seq", pairs_b)
    a1 = lax.ppermute(own_b, "seq", pairs_a)
    far = []
    for c in range(2):
        heads_of = slice(c * chunk, (c + 1) * chunk)
        far_b = lax.ppermute(a1[heads_of], "seq", pairs_b)
        far_a = lax.ppermute(b1[heads_of], "seq", pairs_a)
        far.append((far_a, far_b))
    held = ()
    for c in range(2):
        args = (info, starts, q_t, do_t, own_a, own_b, a1, b1, *far[c])
        held = vmem_call(
            functools.partial(softmax_kernel, scale, c * chunk), deeps + lows, 4 * block, "softmax",
            *args, *held, aliases={len(args) + i: i for i in range(len(held))},
        )
    deep_a, deep_b, low, ds = held
    from_a = lax.ppermute(deep_a, "seq", pairs_a)
    from_b = lax.ppermute(deep_b, "seq", pairs_b)
    prev_a, prev_b, own_term_a, own_term_b, out, dq = rest_call(
        scale, 10 * block, info, q_t, do_t, low, ds, (own_a, own_b), (a1, b1), (*far[0], *far[1])
    )
    next_a = (prev_a + from_b.astype(jnp.float32)).astype(jnp.bfloat16)
    next_b = (prev_b + from_a.astype(jnp.float32)).astype(jnp.bfloat16)
    last_a = lax.ppermute(next_a, "seq", pairs_a)
    last_b = lax.ppermute(next_b, "seq", pairs_b)
    grads = [shape((2, 1, span, kv_heads, dim), jnp.bfloat16)] * 2
    grad_keys, grad_values = vmem_call(
        unpack_kernel, grads, 1024, "unpack", info, own_term_a, own_term_b, last_a, last_b
    )
    return out, dq, grad_keys, grad_values


def any_window(info, q_t, do_t, starts, own_a, own_b, pairs_a, pairs_b, window, scale):
    kv_heads = own_a.shape[0]
    chunks = 2
    chunk = kv_heads // chunks
    parts = []
    for c in range(chunks):
        line_a = [jnp.swapaxes(own_a[c * chunk : (c + 1) * chunk], 0, 1)]
        line_b = [jnp.swapaxes(own_b[c * chunk : (c + 1) * chunk], 0, 1)]
        for _ in range(window):
            next_a = lax.ppermute(line_b[-1], "seq", pairs_a)
            next_b = lax.ppermute(line_a[-1], "seq", pairs_b)
            line_a.append(next_a)
            line_b.append(next_b)
        out, dq, now_a, now_b, rest_a, rest_b = attention_chunk(
            info, q_t, do_t, starts, (line_a, line_b), c * chunk, scale
        )
        for t in range(window - 1, -1, -1):
            from_a = lax.ppermute(now_a, "seq", pairs_a)
            from_b = lax.ppermute(now_b, "seq", pairs_b)
            now_a = (rest_a[t] + from_b.astype(jnp.float32)).astype(jnp.bfloat16)
            now_b = (rest_b[t] + from_a.astype(jnp.float32)).astype(jnp.bfloat16)
        parts.append((out, dq, now_a, now_b))
    out, dq, final_a, final_b = (jnp.concatenate(arrays, axis=1) for arrays in zip(*parts))
    final_a, final_b = jnp.swapaxes(final_a, 0, 1), jnp.swapaxes(final_b, 0, 1)
    halves = jnp.where(info[0] == 1, jnp.stack([final_b, final_a]), jnp.stack([final_a, final_b]))
    halves = jnp.transpose(halves, (2, 0, 3, 1, 4))[:, :, None]
    return out, dq, halves[0], halves[1]


def body(query, keys, values, grad_out, doc_starts):
    count = lax.axis_size("seq")
    device = lax.axis_index("seq")
    window = min(16, count // 2)
    span = query.shape[2]
    dim = query.shape[4]
    scale = dim ** (-0.5)
    pairs_a, pairs_b = swap_pairs(count)
    parity = device % 2

    half_a, half_b = 1 - parity, parity
    span_a = jnp.where(half_a == 0, device, 2 * count - 1 - device)
    info = jnp.stack([half_a, half_b, span_a, 2 * count - 1 - span_a]).astype(jnp.int32)
    own_a, own_b = pack_call(info, keys, values)
    q_t = jnp.transpose(query[:, 0], (0, 2, 1, 3))
    do_t = jnp.transpose(grad_out[:, 0], (0, 2, 1, 3))
    spans = jnp.stack([device, 2 * count - 1 - device])
    token = spans[:, None] * span + jnp.arange(span, dtype=jnp.int32)[None, :]
    below = doc_starts[None, None, :] <= token[:, :, None]
    starts = jnp.max(jnp.where(below, doc_starts[None, None, :], 0), axis=2)[:, None, :]

    if window == 2:
        out, dq, grad_keys, grad_values = two_span_window(
            info, q_t, do_t, starts, own_a, own_b, pairs_a, pairs_b, scale
        )
    else:
        out, dq, grad_keys, grad_values = any_window(
            info, q_t, do_t, starts, own_a, own_b, pairs_a, pairs_b, window, scale
        )
    out = jnp.transpose(out, (0, 2, 1, 3))[:, None]
    dq = jnp.transpose(dq, (0, 2, 1, 3))[:, None]
    return out, dq, grad_keys, grad_values


def solution(mesh):
    spec = P("batch", "seq", None, "head", None)
    return jax.shard_map(
        body,
        mesh=mesh,
        in_specs=(spec, spec, spec, spec, P("batch")),
        out_specs=(spec, spec, spec, spec),
        check_vma=False,
    )
```

time: 54.3 us -> 49.4 us (0.910)
  the two profiles are of different devices: /device:TPU:8 before, /device:TPU:22 now
where the time goes in v3:
time: 49.4 us; the launch traced here: 49.1 us
  starting transfers between devices  17.2 us (35%)
  Pallas kernels  15.2 us (31%)
  waiting for transfers between devices  9.34 us (19%)
  local copies, waits for them, and re-layouts  5.44 us (11%)
  other arithmetic  1.07 us (2%)
  between operations  0.83 us (2%)
    pallas_call x3, Pallas kernels, vmem_call(): pl.pallas_call(kernel, in_specs=[pl.BlockSpec(memory_space=pltpu.SMEM)] +...  7.08 us
    ppermute x2, starting transfers between devices, two_span_window(): far_b = lax.ppermute(a1[heads_of], 'seq', pairs_b)  5.84 us
    pallas_call x1, Pallas kernels, rest_call(): pl.pallas_call(functools.partial(rest_kernel, scale), in_specs=[pl.BlockS...  5.54 us
    ppermute x1, waiting for transfers between devices, two_span_window(): b1 = lax.ppermute(own_a, 'seq', pairs_b)  4.72 us
    ppermute x1, starting transfers between devices, two_span_window(): from_b = lax.ppermute(deep_b, 'seq', pairs_b)  3.59 us
    unnamed x10, local copies, waits for them, and re-layouts  3.32 us
    ppermute x1, waiting for transfers between devices, two_span_window(): last_b = lax.ppermute(next_b, 'seq', pairs_b)  2.69 us
    pallas_call x1, Pallas kernels, pack_call(): pl.pallas_call(pack_kernel, in_specs=[pl.BlockSpec(memory_space=pltpu.SME...  2.6 us
  transfers between devices with their start and end apart: 10, of which 5 were waited for; matrix products, arithmetic and copies ran while one was open for 12% of the time, Pallas kernels for 17%

profile of v3, /device:TPU:22, one launch (start us, length us, event | category | flops | bytes accessed | tf_op | source)
XLA Modules:
  0.0 49.1 jit_solution(12071179460084839790)
XLA Ops:
  0.6 0.6 %pad_add_fusion.info_ref = s32[4]{0:T(128)} fusion(s32[1]{0:T(128)} %bitcast.3, s32[1]{0:T(128)} %bitcast.2, s32[1]{0:T(128)} %bitcast.1, s32[1]{0:T(128)} %bitcast), kind=kLoop, calls=%fused_computation.6 | loop fusion | flops 12 | bytes 32 | tf_op jit(solution)/shard_map/stack | solution.py:463
  1.2 2.6 %pack.1 = (bf16[4,2,128,128]{3,2,1,0:T(8,128)(2,1)}, bf16[4,2,128,128]{3,2,1,0:T(8,128)(2,1)}) custom-call(s32[4]{0:T(128)} %pad_add_fusion.info_ref, bf16[2,1,128,4,128]{4,3,2,1,0:T(4,128)(2,1)} %keys_ref.1, bf16[2,1,128,4,128]{4,3,2,1,0:T(4,128)(2,1)} %values_ref.1), custom_call_target="tpu_custom_call" | custom-call | tf_op jit(solution)/shard_map/pack/pallas_call | solution.py:359
  3.9 2.4 %collective-permute-start.1 = (bf16[4,2,128,128]{3,2,1,0:T(8,128)(2,1)}, bf16[4,2,128,128]{3,2,1,0:T(8,128)(2,1)S(1)}, u32[]{:S(2)}, u32[]{:S(2)}) collective-permute-start(bf16[4,2,128,128]{3,2,1,0:T(8,128)(2,1)} %get-tuple-element.22.own_a.refs_0_), channel_id=1, source_target_pairs={{8,16},{16,8},{24,24},{9,17},{17,9},{25,25},{10,18},{18,10},{26,26... | collective-permute-start | bytes 786440 | tf_op jit(solution)/shard_map/ppermute | solution.py:390
  6.3 0.9 %collective-permute-start = (bf16[4,2,128,128]{3,2,1,0:T(8,128)(2,1)}, bf16[4,2,128,128]{3,2,1,0:T(8,128)(2,1)S(1)}, u32[]{:S(2)}, u32[]{:S(2)}) collective-permute-start(bf16[4,2,128,128]{3,2,1,0:T(8,128)(2,1)} %get-tuple-element.23.own_b.refs_1_), channel_id=1, source_target_pairs={{0,8},{8,0},{16,24},{24,16},{1,9},{9,1},{17,25},{25,17},{2,10},{10... | collective-permute-start | bytes 786440 | tf_op jit(solution)/shard_map/ppermute | solution.py:391
  7.1 2.1 %copy_bitcast_fusion = (bf16[2,16,128,128]{3,2,1,0:T(8,128)(2,1)S(1)}, bf16[2,16,128,128]{3,2,1,0:T(8,128)(2,1)S(1)}) fusion(bf16[2,1,128,16,128]{4,3,2,1,0:T(8,128)(2,1)} %param.8, bf16[2,1,128,16,128]{4,3,2,1,0:T(8,128)(2,1)} %param.5), kind=kLoop, calls=%fused_computation | loop fusion | bytes 4194304 | tf_op jit(solution)/shard_map/transpose | solution.py:466
  9.2 0.1 add_multiply_fusion
  9.3 4.7 %collective-permute-done.1.prev_b.refs_3_ = bf16[4,2,128,128]{3,2,1,0:T(8,128)(2,1)S(1)} collective-permute-done((bf16[4,2,128,128]{3,2,1,0:T(8,128)(2,1)}, bf16[4,2,128,128]{3,2,1,0:T(8,128)(2,1)S(1)}, u32[]{:S(2)}, u32[]{:S(2)}) %collective-permute-start.1) | collective-permute-done | bytes 262176 | tf_op jit(solution)/shard_map/ppermute | solution.py:390
  14.0 0.1 collective-permute-start.4
  14.1 0.2 collective-permute-done.prev_a.refs_2_
  14.3 3.5 %collective-permute-start.5 = (bf16[2,2,128,128]{3,2,1,0:T(8,128)(2,1)S(1)}, bf16[2,2,128,128]{3,2,1,0:T(8,128)(2,1)S(1)}, u32[]{:S(2)}, u32[]{:S(2)}) collective-permute-start(bf16[2,2,128,128]{3,2,1,0:T(8,128)(2,1)S(1)} %get-tuple-element.48), channel_id=1, source_target_pairs={{8,16},{16,8},{24,24},{9,17},{17,9},{25,25},{10,18},{18,10},{26,26... | collective-permute-start | bytes 393224 | tf_op jit(solution)/shard_map/ppermute | solution.py:395
  17.9 0.2 select_reduce_fusion
  18.2 2.4 %collective-permute-start.3 = (bf16[2,2,128,128]{3,2,1,0:T(8,128)(2,1)S(1)}, bf16[2,2,128,128]{3,2,1,0:T(8,128)(2,1)S(1)}, u32[]{:S(2)}, u32[]{:S(2)}) collective-permute-start(bf16[2,2,128,128]{3,2,1,0:T(8,128)(2,1)S(1)} %get-tuple-element.49), channel_id=1, source_target_pairs={{8,16},{16,8},{24,24},{9,17},{17,9},{25,25},{10,18},{18,10},{26,26... | collective-permute-start | bytes 393224 | tf_op jit(solution)/shard_map/ppermute | solution.py:395
  20.6 0.9 %collective-permute-done.5.far_b.refs_5_ = bf16[2,2,128,128]{3,2,1,0:T(8,128)(2,1)S(1)} collective-permute-done((bf16[2,2,128,128]{3,2,1,0:T(8,128)(2,1)S(1)}, bf16[2,2,128,128]{3,2,1,0:T(8,128)(2,1)S(1)}, u32[]{:S(2)}, u32[]{:S(2)}) %collective-permute-start.5) | collective-permute-done | bytes 131104 | tf_op jit(solution)/shard_map/ppermute | solution.py:395
  21.4 2.8 %softmax.2 = (bf16[4,2,128,128]{3,2,1,0:T(8,128)(2,1)S(1)}, bf16[4,2,128,128]{3,2,1,0:T(8,128)(2,1)S(1)}, bf16[2,4,2,128,512]{4,3,2,1,0:T(8,128)(2,1)S(1)}, bf16[2,4,2,128,512]{4,3,2,1,0:T(8,128)(2,1)S(1)}) custom-call(s32[4]{0:T(128)S(1)} %copy-done.2, s32[2,1,128]{2,1,0:T(1,128)S(1)} %bitcast.23, bf16[2,16,128,128]{3,2,1,0:T(8,128)(2,1)S(1)} %get-tuple-element.53.q_ref, ...), custom_call_target="tpu_custom_call" | custom-call | flops 2147483648 | bytes 3408896 | tf_op jit(solution)/shard_map/softmax/pallas_call | solution.py:163
  24.2 0.8 %collective-permute-done.3.far_b.refs_7_ = bf16[2,2,128,128]{3,2,1,0:T(8,128)(2,1)S(1)} collective-permute-done((bf16[2,2,128,128]{3,2,1,0:T(8,128)(2,1)S(1)}, bf16[2,2,128,128]{3,2,1,0:T(8,128)(2,1)S(1)}, u32[]{:S(2)}, u32[]{:S(2)}) %collective-permute-start.3) | collective-permute-done | bytes 131104 | tf_op jit(solution)/shard_map/ppermute | solution.py:395
  25.0 2.7 %softmax.3 = (bf16[4,2,128,128]{3,2,1,0:T(8,128)(2,1)S(1)}, bf16[4,2,128,128]{3,2,1,0:T(8,128)(2,1)S(1)}, bf16[2,4,2,128,512]{4,3,2,1,0:T(8,128)(2,1)S(1)}, bf16[2,4,2,128,512]{4,3,2,1,0:T(8,128)(2,1)S(1)}) custom-call(s32[4]{0:T(128)S(1)} %copy-done.2, ...), custom_call_target="tpu_custom_call", output_to_operand_aliasing={{0}: (10, {}), {1}: (11, {}), {2}: (12, {}), {3}: (13, {})} | custom-call | flops 2147483648 | bytes 8127488 | tf_op jit(solution)/shard_map/softmax/pallas_call | solution.py:163
  27.8 3.6 %collective-permute-start.6 = (bf16[4,2,128,128]{3,2,1,0:T(8,128)(2,1)S(1)}, bf16[4,2,128,128]{3,2,1,0:T(8,128)(2,1)S(1)}, u32[]{:S(2)}, u32[]{:S(2)}) collective-permute-start(bf16[4,2,128,128]{3,2,1,0:T(8,128)(2,1)S(1)} %get-tuple-element.35), channel_id=1, source_target_pairs={{8,16},{16,8},{24,24},{9,17},{17,9},{25,25},{10,18},{18,10},{26,26... | collective-permute-start | bytes 786440 | tf_op jit(solution)/shard_map/ppermute | solution.py:407
  31.5 5.5 %rest.1 = (f32[4,2,128,128]{3,2,1,0:T(8,128)S(1)}, f32[4,2,128,128]{3,2,1,0:T(8,128)S(1)}, f32[4,2,128,128]{3,2,1,0:T(8,128)S(1)}, f32[4,2,128,128]{3,2,1,0:T(8,...) custom-call(s32[4]{0:T(128)S(1)} %copy-done.2, ...), custom_call_target="tpu_custom_call" | custom-call | flops 5368709120 | bytes 8388608 | tf_op jit(solution)/shard_map/rest/pallas_call | solution.py:320
  37.1 2.1 %collective-permute-start.7 = (bf16[4,2,128,128]{3,2,1,0:T(8,128)(2,1)S(1)}, bf16[4,2,128,128]{3,2,1,0:T(8,128)(2,1)S(1)}, u32[]{:S(2)}, u32[]{:S(2)}) collective-permute-start(bf16[4,2,128,128]{3,2,1,0:T(8,128)(2,1)S(1)} %add_convert_fusion.1), channel_id=1, source_target_pairs={{0,8},{8,0},{16,24},{24,16},{1,9},{9,1},{17,25},{25,17},{2,10},{10... | collective-permute-start | bytes 786440 | tf_op jit(solution)/shard_map/ppermute | solution.py:413
  39.2 2.3 %collective-permute-start.9 = (bf16[4,2,128,128]{3,2,1,0:T(8,128)(2,1)S(1)}, bf16[4,2,128,128]{3,2,1,0:T(8,128)(2,1)S(1)}, u32[]{:S(2)}, u32[]{:S(2)}) collective-permute-start(bf16[4,2,128,128]{3,2,1,0:T(8,128)(2,1)S(1)} %add_convert_fusion), channel_id=1, source_target_pairs={{8,16},{16,8},{24,24},{9,17},{17,9},{25,25},{10,18},{18,10},{26,26... | collective-permute-start | bytes 786440 | tf_op jit(solution)/shard_map/ppermute | solution.py:414
  41.5 1.6 %copy.19 = bf16[2,1,128,16,128]{4,3,2,1,0:T(8,128)(2,1)} copy(bf16[2,1,128,16,128]{4,2,3,0,1:T(8,128)(2,1)S(1)} %bitcast.22) | data formatting | bytes 2097152
  43.2 1.6 %copy.20 = bf16[2,1,128,16,128]{4,3,2,1,0:T(8,128)(2,1)} copy(bf16[2,1,128,16,128]{4,2,3,0,1:T(8,128)(2,1)S(1)} %bitcast.21) | data formatting | bytes 2097152
  44.8 2.7 %collective-permute-done.9.last_b = bf16[4,2,128,128]{3,2,1,0:T(8,128)(2,1)S(1)} collective-permute-done((bf16[4,2,128,128]{3,2,1,0:T(8,128)(2,1)S(1)}, bf16[4,2,128,128]{3,2,1,0:T(8,128)(2,1)S(1)}, u32[]{:S(2)}, u32[]{:S(2)}) %collective-permute-start.9) | collective-permute-done | bytes 262176 | tf_op jit(solution)/shard_map/ppermute | solution.py:414
  47.5 1.6 %unpack.1 = (bf16[2,1,128,4,128]{4,3,2,1,0:T(4,128)(2,1)}, bf16[2,1,128,4,128]{4,3,2,1,0:T(4,128)(2,1)}) custom-call(s32[4]{0:T(128)S(1)} %copy-done.2, f32[4,2,128,128]{3,2,1,0:T(8,128)S(1)} %get-tuple-element.32.own_a, f32[4,2,128,128]{3,2,1,0:T(8,128)S(1)} %get-tuple-element.33.own_b, bf16[4,2,128,128]{3,2,1,0:T(8,128)(2,1)S(1)} %collective-permute-done.7.last_a, ...), custom_call_target="tpu_custom_call" | custom-call | flops 8192 | bytes 1572864 | tf_op jit(solution)/shard_map/unpack/pallas_call | solution.py:163
  (20 shorter events, 0.4 us)
Async XLA Ops:
  3.9 10.1 %collective-permute-start.1 = (bf16[4,2,128,128]{3,2,1,0:T(8,128)(2,1)}, bf16[4,2,128,128]{3,2,1,0:T(8,128)(2,1)S(1)}, u32[]{:S(2)}, u32[]{:S(2)}) collective-permute-start(bf16[4,2,128,128]{3,2,1,0:T(8,128)(2,1)} %get-tuple-element.22.own_a.refs_0_), channel_id=1, source_target_pairs={{8,16},{16,8},{24,24},{9,17},{17,9},{25,25},{10,18},{18,10},{26,26... | collective-permute-start | bytes 786440 | tf_op jit(solution)/shard_map/ppermute | solution.py:390
  6.2 11.7 %copy-start.3 = (s32[512]{0:T(512)S(1)}, s32[512]{0:T(512)}, u32[]{:S(2)}) copy-start(s32[512]{0:T(512)} %param.9) | copy-start | bytes 6148
  6.2 15.2 %copy-start = (bf16[4,2,128,128]{3,2,1,0:T(8,128)(2,1)S(1)}, bf16[4,2,128,128]{3,2,1,0:T(8,128)(2,1)}, u32[]{:S(2)}) copy-start(bf16[4,2,128,128]{3,2,1,0:T(8,128)(2,1)} %get-tuple-element.22.own_a.refs_0_) | copy-start | bytes 786436
  6.2 15.2 %copy-start.1 = (bf16[4,2,128,128]{3,2,1,0:T(8,128)(2,1)S(1)}, bf16[4,2,128,128]{3,2,1,0:T(8,128)(2,1)}, u32[]{:S(2)}) copy-start(bf16[4,2,128,128]{3,2,1,0:T(8,128)(2,1)} %get-tuple-element.23.own_b.refs_1_) | copy-start | bytes 786436
  6.3 15.2 %copy-start.2 = (s32[4]{0:T(128)S(1)}, s32[4]{0:T(128)}, u32[]{:S(2)}) copy-start(s32[4]{0:T(128)} %pad_add_fusion.info_ref) | copy-start | bytes 52
  6.3 8.0 %collective-permute-start = (bf16[4,2,128,128]{3,2,1,0:T(8,128)(2,1)}, bf16[4,2,128,128]{3,2,1,0:T(8,128)(2,1)S(1)}, u32[]{:S(2)}, u32[]{:S(2)}) collective-permute-start(bf16[4,2,128,128]{3,2,1,0:T(8,128)(2,1)} %get-tuple-element.23.own_b.refs_1_), channel_id=1, source_target_pairs={{0,8},{8,0},{16,24},{24,16},{1,9},{9,1},{17,25},{25,17},{2,10},{10... | collective-permute-start | bytes 786440 | tf_op jit(solution)/shard_map/ppermute | solution.py:391
  14.0 6.5 %collective-permute-start.4 = (bf16[2,2,128,128]{3,2,1,0:T(8,128)(2,1)S(1)}, bf16[2,2,128,128]{3,2,1,0:T(8,128)(2,1)S(1)}, u32[]{:S(2)}, u32[]{:S(2)}) collective-permute-start(bf16[2,2,128,128]{3,2,1,0:T(8,128)(2,1)S(1)} %get-tuple-element.50), channel_id=1, source_target_pairs={{0,8},{8,0},{16,24},{24,16},{1,9},{9,1},{17,25},{25,17},{2,10},{10... | collective-permute-start | bytes 393224 | tf_op jit(solution)/shard_map/ppermute | solution.py:396
  14.3 7.1 %collective-permute-start.5 = (bf16[2,2,128,128]{3,2,1,0:T(8,128)(2,1)S(1)}, bf16[2,2,128,128]{3,2,1,0:T(8,128)(2,1)S(1)}, u32[]{:S(2)}, u32[]{:S(2)}) collective-permute-start(bf16[2,2,128,128]{3,2,1,0:T(8,128)(2,1)S(1)} %get-tuple-element.48), channel_id=1, source_target_pairs={{8,16},{16,8},{24,24},{9,17},{17,9},{25,25},{10,18},{18,10},{26,26... | collective-permute-start | bytes 393224 | tf_op jit(solution)/shard_map/ppermute | solution.py:395
  18.1 6.1 %collective-permute-start.2 = (bf16[2,2,128,128]{3,2,1,0:T(8,128)(2,1)S(1)}, bf16[2,2,128,128]{3,2,1,0:T(8,128)(2,1)S(1)}, u32[]{:S(2)}, u32[]{:S(2)}) collective-permute-start(bf16[2,2,128,128]{3,2,1,0:T(8,128)(2,1)S(1)} %get-tuple-element.51), channel_id=1, source_target_pairs={{0,8},{8,0},{16,24},{24,16},{1,9},{9,1},{17,25},{25,17},{2,10},{10... | collective-permute-start | bytes 393224 | tf_op jit(solution)/shard_map/ppermute | solution.py:396
  18.2 6.9 %collective-permute-start.3 = (bf16[2,2,128,128]{3,2,1,0:T(8,128)(2,1)S(1)}, bf16[2,2,128,128]{3,2,1,0:T(8,128)(2,1)S(1)}, u32[]{:S(2)}, u32[]{:S(2)}) collective-permute-start(bf16[2,2,128,128]{3,2,1,0:T(8,128)(2,1)S(1)} %get-tuple-element.49), channel_id=1, source_target_pairs={{8,16},{16,8},{24,24},{9,17},{17,9},{25,25},{10,18},{18,10},{26,26... | collective-permute-start | bytes 393224 | tf_op jit(solution)/shard_map/ppermute | solution.py:395
  27.8 9.2 %collective-permute-start.6 = (bf16[4,2,128,128]{3,2,1,0:T(8,128)(2,1)S(1)}, bf16[4,2,128,128]{3,2,1,0:T(8,128)(2,1)S(1)}, u32[]{:S(2)}, u32[]{:S(2)}) collective-permute-start(bf16[4,2,128,128]{3,2,1,0:T(8,128)(2,1)S(1)} %get-tuple-element.35), channel_id=1, source_target_pairs={{8,16},{16,8},{24,24},{9,17},{17,9},{25,25},{10,18},{18,10},{26,26... | collective-permute-start | bytes 786440 | tf_op jit(solution)/shard_map/ppermute | solution.py:407
  31.4 7.8 %collective-permute-start.8 = (bf16[4,2,128,128]{3,2,1,0:T(8,128)(2,1)S(1)}, bf16[4,2,128,128]{3,2,1,0:T(8,128)(2,1)S(1)}, u32[]{:S(2)}, u32[]{:S(2)}) collective-permute-start(bf16[4,2,128,128]{3,2,1,0:T(8,128)(2,1)S(1)} %get-tuple-element.37), channel_id=1, source_target_pairs={{0,8},{8,0},{16,24},{24,16},{1,9},{9,1},{17,25},{25,17},{2,10},{10... | collective-permute-start | bytes 786440 | tf_op jit(solution)/shard_map/ppermute | solution.py:406
  37.1 7.7 %collective-permute-start.7 = (bf16[4,2,128,128]{3,2,1,0:T(8,128)(2,1)S(1)}, bf16[4,2,128,128]{3,2,1,0:T(8,128)(2,1)S(1)}, u32[]{:S(2)}, u32[]{:S(2)}) collective-permute-start(bf16[4,2,128,128]{3,2,1,0:T(8,128)(2,1)S(1)} %add_convert_fusion.1), channel_id=1, source_target_pairs={{0,8},{8,0},{16,24},{24,16},{1,9},{9,1},{17,25},{25,17},{2,10},{10... | collective-permute-start | bytes 786440 | tf_op jit(solution)/shard_map/ppermute | solution.py:413
  39.2 8.3 %collective-permute-start.9 = (bf16[4,2,128,128]{3,2,1,0:T(8,128)(2,1)S(1)}, bf16[4,2,128,128]{3,2,1,0:T(8,128)(2,1)S(1)}, u32[]{:S(2)}, u32[]{:S(2)}) collective-permute-start(bf16[4,2,128,128]{3,2,1,0:T(8,128)(2,1)S(1)} %add_convert_fusion), channel_id=1, source_target_pairs={{8,16},{16,8},{24,24},{9,17},{17,9},{25,25},{10,18},{18,10},{26,26... | collective-permute-start | bytes 786440 | tf_op jit(solution)/shard_map/ppermute | solution.py:414

commit v4 on v3

--- a/solution.py
+++ b/solution.py
@@ -332,43 +332,6 @@
     )(info, q_t, do_t, low, ds, *own, *prev, *far)
 
 
-def pack_kernel(info_ref, keys_ref, values_ref, own_a_ref, own_b_ref, raw, sems):
-    copies = []
-    for slot in (1, 0):
-        for which, ref in enumerate((keys_ref, values_ref)):
-            copies.append(
-                pltpu.make_async_copy(
-                    ref.at[info_ref[slot], 0], raw.at[slot, which], sems.at[slot, which]
-                )
-            )
-            copies[-1].start()
-    index = 0
-    for slot in (1, 0):
-        own_ref = (own_a_ref, own_b_ref)[slot]
-        for which in range(2):
-            copies[index].wait()
-            index += 1
-            tokens = jnp.swapaxes(raw[slot, which].astype(jnp.float32), 0, 1)
-            own_ref[:, which] = tokens.astype(jnp.bfloat16)
-
-
-def pack_call(info, keys, values):
-    _, _, span, kv_heads, dim = keys.shape
-    outside = pl.BlockSpec(memory_space=pl.ANY)
-    whole = pl.BlockSpec(memory_space=pltpu.VMEM)
-    return pl.pallas_call(
-        pack_kernel,
-        in_specs=[pl.BlockSpec(memory_space=pltpu.SMEM), outside, outside],
-        out_specs=[whole] * 2,
-        out_shape=[jax.ShapeDtypeStruct((kv_heads, 2, span, dim), jnp.bfloat16)] * 2,
-        scratch_shapes=[
-            pltpu.VMEM((2, 2, span, kv_heads, dim), jnp.bfloat16),
-            pltpu.SemaphoreType.DMA((2, 2)),
-        ],
-        name="pack",
-    )(info, keys, values)
-
-
 def unpack_kernel(info_ref, own_a, own_b, last_a, last_b, grad_keys_ref, grad_values_ref):
     for slot, (own, last) in enumerate(((own_a, last_b), (own_b, last_a))):
         half = info_ref[slot]
@@ -408,6 +371,7 @@
     prev_a, prev_b, own_term_a, own_term_b, out, dq = rest_call(
         scale, 10 * block, info, q_t, do_t, low, ds, (own_a, own_b), (a1, b1), (*far[0], *far[1])
     )
+    from_a, from_b = lax.optimization_barrier((from_a, from_b))
     next_a = (prev_a + from_b.astype(jnp.float32)).astype(jnp.bfloat16)
     next_b = (prev_b + from_a.astype(jnp.float32)).astype(jnp.bfloat16)
     last_a = lax.ppermute(next_a, "seq", pairs_a)
@@ -461,7 +425,12 @@
     half_a, half_b = 1 - parity, parity
     span_a = jnp.where(half_a == 0, device, 2 * count - 1 - device)
     info = jnp.stack([half_a, half_b, span_a, 2 * count - 1 - span_a]).astype(jnp.int32)
-    own_a, own_b = pack_call(info, keys, values)
+
+    def payload(half):
+        pair = [lax.dynamic_index_in_dim(x[:, 0], half, 0, keepdims=False) for x in (keys, values)]
+        return jnp.transpose(jnp.stack(pair), (2, 0, 1, 3))
+
+    own_a, own_b = payload(half_a), payload(half_b)
     q_t = jnp.transpose(query[:, 0], (0, 2, 1, 3))
     do_t = jnp.transpose(grad_out[:, 0], (0, 2, 1, 3))
     spans = jnp.stack([device, 2 * count - 1 - device])

time: 49.4 us -> 44.5 us (0.901)
  the two profiles are of different devices: /device:TPU:22 before, /device:TPU:8 now
where the time goes in v4:
time: 44.5 us; the launch traced here: 44.3 us
  starting transfers between devices  18.2 us (41%)
  Pallas kernels  12.6 us (28%)
  local copies, waits for them, and re-layouts  6.79 us (15%)
  waiting for transfers between devices  5.13 us (12%)
  between operations  0.89 us (2%)
  other arithmetic  0.61 us (1%)
    pallas_call x3, Pallas kernels, vmem_call(): pl.pallas_call(kernel, in_specs=[pl.BlockSpec(memory_space=pltpu.SMEM)] +...  7.06 us
    ppermute x2, starting transfers between devices, two_span_window(): far_b = lax.ppermute(a1[heads_of], 'seq', pairs_b)  6.72 us
    pallas_call x1, Pallas kernels, rest_call(): pl.pallas_call(functools.partial(rest_kernel, scale), in_specs=[pl.BlockS...  5.56 us
    ppermute x1, starting transfers between devices, two_span_window(): b1 = lax.ppermute(own_a, 'seq', pairs_b)  5.04 us
    ppermute x1, starting transfers between devices, two_span_window(): from_b = lax.ppermute(deep_b, 'seq', pairs_b)  3.46 us
    unnamed x4, local copies, waits for them, and re-layouts  3.3 us
    ppermute x1, starting transfers between devices, two_span_window(): last_b = lax.ppermute(next_b, 'seq', pairs_b)  2.66 us
    ppermute x2, waiting for transfers between devices, two_span_window(): far_a = lax.ppermute(b1[heads_of], 'seq', pairs_a)  2.18 us
  transfers between devices with their start and end apart: 10, of which 5 were waited for; matrix products, arithmetic and copies ran while one was open for 14% of the time, Pallas kernels for 19%

profile of v4, /device:TPU:8, one launch (start us, length us, event | category | flops | bytes accessed | tf_op | source)
XLA Modules:
  0.0 44.3 jit_solution(9244072723673825029)
XLA Ops:
  0.7 1.3 %constant_dynamic-slice_fusion = (bf16[1,1,128,4,128]{4,3,2,1,0:T(4,128)(2,1)S(1)}, bf16[1,1,128,4,128]{4,3,2,1,0:T(4,128)(2,1)S(1)}, bf16[1,1,128,4,128]{4,3,2,...) fusion(bf16[2,1,128,4,128]{4,3,2,1,0:T(4,128)(2,1)} %param.7, s32[]{:T(128)S(6)} %select_n.27, s32[]{:T(128)S(6)} %select_n.26, ...), kind=kLoop, calls=%fused_computation.12 | loop fusion | bytes 1048584 | tf_op jit(solution)/shard_map/jit(dynamic_index_in_dim)/dynamic_slice | solution.py:430
  2.0 0.1 collective-permute-start
  2.2 5.0 %collective-permute-start.1 = (bf16[4,2,128,128]{3,2,1,0:T(8,128)(2,1)S(1)}, bf16[4,2,128,128]{3,2,1,0:T(8,128)(2,1)S(1)}, u32[]{:S(2)}, u32[]{:S(2)}) collective-permute-start(bf16[4,2,128,128]{3,2,1,0:T(8,128)(2,1)S(1)} %maximum_bitcast_fusion.own_a.refs_0_), channel_id=1, source_target_pairs={{8,16},{16,8},{24,24},{9,17},{17,9},{25,25},{10,18},{18,10},{26,26... | collective-permute-start | bytes 786440 | tf_op jit(solution)/shard_map/ppermute | solution.py:353
  7.3 2.1 %copy_bitcast_fusion = (bf16[2,16,128,128]{3,2,1,0:T(8,128)(2,1)S(1)}, bf16[2,16,128,128]{3,2,1,0:T(8,128)(2,1)S(1)}) fusion(bf16[2,1,128,16,128]{4,3,2,1,0:T(8,128)(2,1)} %param.8, bf16[2,1,128,16,128]{4,3,2,1,0:T(8,128)(2,1)} %param.5), kind=kLoop, calls=%fused_computation | loop fusion | bytes 4194304 | tf_op jit(solution)/shard_map/transpose | solution.py:435
  9.4 0.1 add_multiply_fusion
  9.4 0.1 iota_add_fusion
  9.5 0.6 %collective-permute-done.prev_a.refs_2_ = bf16[4,2,128,128]{3,2,1,0:T(8,128)(2,1)S(1)} collective-permute-done((bf16[4,2,128,128]{3,2,1,0:T(8,128)(2,1)S(1)}, bf16[4,2,128,128]{3,2,1,0:T(8,128)(2,1)S(1)}, u32[]{:S(2)}, u32[]{:S(2)}) %collective-permute-start) | collective-permute-done | bytes 262176 | tf_op jit(solution)/shard_map/ppermute | solution.py:354
  10.2 3.5 %collective-permute-start.5 = (bf16[2,2,128,128]{3,2,1,0:T(8,128)(2,1)S(1)}, bf16[2,2,128,128]{3,2,1,0:T(8,128)(2,1)S(1)}, u32[]{:S(2)}, u32[]{:S(2)}) collective-permute-start(bf16[2,2,128,128]{3,2,1,0:T(8,128)(2,1)S(1)} %get-tuple-element.48), channel_id=1, source_target_pairs={{8,16},{16,8},{24,24},{9,17},{17,9},{25,25},{10,18},{18,10},{26,26... | collective-permute-start | bytes 393224 | tf_op jit(solution)/shard_map/ppermute | solution.py:358
  13.8 0.1 pad_add_fusion.info_ref
  13.9 0.2 select_reduce_fusion
  14.1 3.2 %collective-permute-start.3 = (bf16[2,2,128,128]{3,2,1,0:T(8,128)(2,1)S(1)}, bf16[2,2,128,128]{3,2,1,0:T(8,128)(2,1)S(1)}, u32[]{:S(2)}, u32[]{:S(2)}) collective-permute-start(bf16[2,2,128,128]{3,2,1,0:T(8,128)(2,1)S(1)} %get-tuple-element.49), channel_id=1, source_target_pairs={{8,16},{16,8},{24,24},{9,17},{17,9},{25,25},{10,18},{18,10},{26,26... | collective-permute-start | bytes 393224 | tf_op jit(solution)/shard_map/ppermute | solution.py:358
  17.4 1.7 %collective-permute-done.4.far_a.refs_4_ = bf16[2,2,128,128]{3,2,1,0:T(8,128)(2,1)S(1)} collective-permute-done((bf16[2,2,128,128]{3,2,1,0:T(8,128)(2,1)S(1)}, bf16[2,2,128,128]{3,2,1,0:T(8,128)(2,1)S(1)}, u32[]{:S(2)}, u32[]{:S(2)}) %collective-permute-start.4) | collective-permute-done | bytes 131104 | tf_op jit(solution)/shard_map/ppermute | solution.py:359
  19.1 2.7 %softmax.2 = (bf16[4,2,128,128]{3,2,1,0:T(8,128)(2,1)S(1)}, bf16[4,2,128,128]{3,2,1,0:T(8,128)(2,1)S(1)}, bf16[2,4,2,128,512]{4,3,2,1,0:T(8,128)(2,1)S(1)}, bf16[2,4,2,128,512]{4,3,2,1,0:T(8,128)(2,1)S(1)}) custom-call(s32[4]{0:T(128)S(1)} %pad_add_fusion.info_ref, s32[2,1,128]{2,1,0:T(1,128)S(1)} %bitcast.39, ...), custom_call_target="tpu_custom_call" | custom-call | flops 2147483648 | bytes 3408896 | tf_op jit(solution)/shard_map/softmax/pallas_call | solution.py:163
  21.9 0.5 %collective-permute-done.2.far_a.refs_6_ = bf16[2,2,128,128]{3,2,1,0:T(8,128)(2,1)S(1)} collective-permute-done((bf16[2,2,128,128]{3,2,1,0:T(8,128)(2,1)S(1)}, bf16[2,2,128,128]{3,2,1,0:T(8,128)(2,1)S(1)}, u32[]{:S(2)}, u32[]{:S(2)}) %collective-permute-start.2) | collective-permute-done | bytes 131104 | tf_op jit(solution)/shard_map/ppermute | solution.py:359
  22.3 2.7 %softmax.3 = (bf16[4,2,128,128]{3,2,1,0:T(8,128)(2,1)S(1)}, bf16[4,2,128,128]{3,2,1,0:T(8,128)(2,1)S(1)}, bf16[2,4,2,128,512]{4,3,2,1,0:T(8,128)(2,1)S(1)}, bf16[2,4,2,128,512]{4,3,2,1,0:T(8,128)(2,1)S(1)}) custom-call(s32[4]{0:T(128)S(1)} %pad_add_fusion.info_ref, ...), custom_call_target="tpu_custom_call", output_to_operand_aliasing={{0}: (10, {}), {1}: (11, {}), {2}: (12, {}), {3}: (13, {})} | custom-call | flops 2147483648 | bytes 8127488 | tf_op jit(solution)/shard_map/softmax/pallas_call | solution.py:163
  25.1 0.1 collective-permute-start.6
  25.2 3.5 %collective-permute-start.7 = (bf16[4,2,128,128]{3,2,1,0:T(8,128)(2,1)S(1)}, bf16[4,2,128,128]{3,2,1,0:T(8,128)(2,1)S(1)}, u32[]{:S(2)}, u32[]{:S(2)}) collective-permute-start(bf16[4,2,128,128]{3,2,1,0:T(8,128)(2,1)S(1)} %get-tuple-element.34), channel_id=1, source_target_pairs={{8,16},{16,8},{24,24},{9,17},{17,9},{25,25},{10,18},{18,10},{26,26... | collective-permute-start | bytes 786440 | tf_op jit(solution)/shard_map/ppermute | solution.py:370
  28.6 5.6 %rest.1 = (f32[4,2,128,128]{3,2,1,0:T(8,128)S(1)}, f32[4,2,128,128]{3,2,1,0:T(8,128)S(1)}, f32[4,2,128,128]{3,2,1,0:T(8,128)S(1)}, f32[4,2,128,128]{3,2,1,0:T(8,...) custom-call(s32[4]{0:T(128)S(1)} %pad_add_fusion.info_ref, ...), custom_call_target="tpu_custom_call" | custom-call | flops 5368709120 | bytes 8388608 | tf_op jit(solution)/shard_map/rest/pallas_call | solution.py:320
  34.4 2.7 %collective-permute-start.9 = (bf16[4,2,128,128]{3,2,1,0:T(8,128)(2,1)S(1)}, bf16[4,2,128,128]{3,2,1,0:T(8,128)(2,1)S(1)}, u32[]{:S(2)}, u32[]{:S(2)}) collective-permute-start(bf16[4,2,128,128]{3,2,1,0:T(8,128)(2,1)S(1)} %add_convert_fusion), channel_id=1, source_target_pairs={{8,16},{16,8},{24,24},{9,17},{17,9},{25,25},{10,18},{18,10},{26,26... | collective-permute-start | bytes 786440 | tf_op jit(solution)/shard_map/ppermute | solution.py:378
  37.1 1.6 %copy.27 = bf16[2,1,128,16,128]{4,3,2,1,0:T(8,128)(2,1)} copy(bf16[2,1,128,16,128]{4,2,3,0,1:T(8,128)(2,1)S(1)} %bitcast.38) | data formatting | bytes 2097152
  38.8 1.6 %copy.28 = bf16[2,1,128,16,128]{4,3,2,1,0:T(8,128)(2,1)} copy(bf16[2,1,128,16,128]{4,2,3,0,1:T(8,128)(2,1)S(1)} %bitcast.37) | data formatting | bytes 2097152
  40.4 0.3 collective-permute-done.8.last_a
  40.7 2.0 %collective-permute-done.9.last_b = bf16[4,2,128,128]{3,2,1,0:T(8,128)(2,1)S(1)} collective-permute-done((bf16[4,2,128,128]{3,2,1,0:T(8,128)(2,1)S(1)}, bf16[4,2,128,128]{3,2,1,0:T(8,128)(2,1)S(1)}, u32[]{:S(2)}, u32[]{:S(2)}) %collective-permute-start.9) | collective-permute-done | bytes 262176 | tf_op jit(solution)/shard_map/ppermute | solution.py:378
  42.7 1.6 %unpack.1 = (bf16[2,1,128,4,128]{4,3,2,1,0:T(4,128)(2,1)}, bf16[2,1,128,4,128]{4,3,2,1,0:T(4,128)(2,1)}) custom-call(s32[4]{0:T(128)S(1)} %pad_add_fusion.info_ref, f32[4,2,128,128]{3,2,1,0:T(8,128)S(1)} %get-tuple-element.30.own_a, f32[4,2,128,128]{3,2,1,0:T(8,128)S(1)} %get-tuple-element.31.own_b, ...), custom_call_target="tpu_custom_call" | custom-call | flops 8192 | bytes 1572864 | tf_op jit(solution)/shard_map/unpack/pallas_call | solution.py:163
  (20 shorter events, 0.5 us)
Async XLA Ops:
  2.0 8.1 %collective-permute-start = (bf16[4,2,128,128]{3,2,1,0:T(8,128)(2,1)S(1)}, bf16[4,2,128,128]{3,2,1,0:T(8,128)(2,1)S(1)}, u32[]{:S(2)}, u32[]{:S(2)}) collective-permute-start(bf16[4,2,128,128]{3,2,1,0:T(8,128)(2,1)S(1)} %maximum_bitcast_fusion.1.own_b.refs_1_), channel_id=1, source_target_pairs={{0,8},{8,0},{16,24},{24,16},{1,9},{9,1},{17,25},{25,17},{2,10},{10... | collective-permute-start | bytes 786440 | tf_op jit(solution)/shard_map/ppermute | solution.py:354
  2.2 11.5 %collective-permute-start.1 = (bf16[4,2,128,128]{3,2,1,0:T(8,128)(2,1)S(1)}, bf16[4,2,128,128]{3,2,1,0:T(8,128)(2,1)S(1)}, u32[]{:S(2)}, u32[]{:S(2)}) collective-permute-start(bf16[4,2,128,128]{3,2,1,0:T(8,128)(2,1)S(1)} %maximum_bitcast_fusion.own_a.refs_0_), channel_id=1, source_target_pairs={{8,16},{16,8},{24,24},{9,17},{17,9},{25,25},{10,18},{18,10},{26,26... | collective-permute-start | bytes 786440 | tf_op jit(solution)/shard_map/ppermute | solution.py:353
  7.3 6.6 %copy-start = (s32[512]{0:T(512)S(1)}, s32[512]{0:T(512)}, u32[]{:S(2)}) copy-start(s32[512]{0:T(512)} %param.9) | copy-start | bytes 6148
  10.2 7.2 %collective-permute-start.5 = (bf16[2,2,128,128]{3,2,1,0:T(8,128)(2,1)S(1)}, bf16[2,2,128,128]{3,2,1,0:T(8,128)(2,1)S(1)}, u32[]{:S(2)}, u32[]{:S(2)}) collective-permute-start(bf16[2,2,128,128]{3,2,1,0:T(8,128)(2,1)S(1)} %get-tuple-element.48), channel_id=1, source_target_pairs={{8,16},{16,8},{24,24},{9,17},{17,9},{25,25},{10,18},{18,10},{26,26... | collective-permute-start | bytes 393224 | tf_op jit(solution)/shard_map/ppermute | solution.py:358
  13.7 5.4 %collective-permute-start.4 = (bf16[2,2,128,128]{3,2,1,0:T(8,128)(2,1)S(1)}, bf16[2,2,128,128]{3,2,1,0:T(8,128)(2,1)S(1)}, u32[]{:S(2)}, u32[]{:S(2)}) collective-permute-start(bf16[2,2,128,128]{3,2,1,0:T(8,128)(2,1)S(1)} %get-tuple-element.50), channel_id=1, source_target_pairs={{0,8},{8,0},{16,24},{24,16},{1,9},{9,1},{17,25},{25,17},{2,10},{10... | collective-permute-start | bytes 393224 | tf_op jit(solution)/shard_map/ppermute | solution.py:359
  14.1 7.8 %collective-permute-start.3 = (bf16[2,2,128,128]{3,2,1,0:T(8,128)(2,1)S(1)}, bf16[2,2,128,128]{3,2,1,0:T(8,128)(2,1)S(1)}, u32[]{:S(2)}, u32[]{:S(2)}) collective-permute-start(bf16[2,2,128,128]{3,2,1,0:T(8,128)(2,1)S(1)} %get-tuple-element.49), channel_id=1, source_target_pairs={{8,16},{16,8},{24,24},{9,17},{17,9},{25,25},{10,18},{18,10},{26,26... | collective-permute-start | bytes 393224 | tf_op jit(solution)/shard_map/ppermute | solution.py:358
  17.3 5.0 %collective-permute-start.2 = (bf16[2,2,128,128]{3,2,1,0:T(8,128)(2,1)S(1)}, bf16[2,2,128,128]{3,2,1,0:T(8,128)(2,1)S(1)}, u32[]{:S(2)}, u32[]{:S(2)}) collective-permute-start(bf16[2,2,128,128]{3,2,1,0:T(8,128)(2,1)S(1)} %get-tuple-element.51), channel_id=1, source_target_pairs={{0,8},{8,0},{16,24},{24,16},{1,9},{9,1},{17,25},{25,17},{2,10},{10... | collective-permute-start | bytes 393224 | tf_op jit(solution)/shard_map/ppermute | solution.py:359
  25.1 9.1 %collective-permute-start.6 = (bf16[4,2,128,128]{3,2,1,0:T(8,128)(2,1)S(1)}, bf16[4,2,128,128]{3,2,1,0:T(8,128)(2,1)S(1)}, u32[]{:S(2)}, u32[]{:S(2)}) collective-permute-start(bf16[4,2,128,128]{3,2,1,0:T(8,128)(2,1)S(1)} %get-tuple-element.33), channel_id=1, source_target_pairs={{0,8},{8,0},{16,24},{24,16},{1,9},{9,1},{17,25},{25,17},{2,10},{10... | collective-permute-start | bytes 786440 | tf_op jit(solution)/shard_map/ppermute | solution.py:369
  25.2 9.1 %collective-permute-start.7 = (bf16[4,2,128,128]{3,2,1,0:T(8,128)(2,1)S(1)}, bf16[4,2,128,128]{3,2,1,0:T(8,128)(2,1)S(1)}, u32[]{:S(2)}, u32[]{:S(2)}) collective-permute-start(bf16[4,2,128,128]{3,2,1,0:T(8,128)(2,1)S(1)} %get-tuple-element.34), channel_id=1, source_target_pairs={{8,16},{16,8},{24,24},{9,17},{17,9},{25,25},{10,18},{18,10},{26,26... | collective-permute-start | bytes 786440 | tf_op jit(solution)/shard_map/ppermute | solution.py:370
  34.3 6.4 %collective-permute-start.8 = (bf16[4,2,128,128]{3,2,1,0:T(8,128)(2,1)S(1)}, bf16[4,2,128,128]{3,2,1,0:T(8,128)(2,1)S(1)}, u32[]{:S(2)}, u32[]{:S(2)}) collective-permute-start(bf16[4,2,128,128]{3,2,1,0:T(8,128)(2,1)S(1)} %add_convert_fusion.1), channel_id=1, source_target_pairs={{0,8},{8,0},{16,24},{24,16},{1,9},{9,1},{17,25},{25,17},{2,10},{10... | collective-permute-start | bytes 786440 | tf_op jit(solution)/shard_map/ppermute | solution.py:377
  34.4 8.3 %collective-permute-start.9 = (bf16[4,2,128,128]{3,2,1,0:T(8,128)(2,1)S(1)}, bf16[4,2,128,128]{3,2,1,0:T(8,128)(2,1)S(1)}, u32[]{:S(2)}, u32[]{:S(2)}) collective-permute-start(bf16[4,2,128,128]{3,2,1,0:T(8,128)(2,1)S(1)} %add_convert_fusion), channel_id=1, source_target_pairs={{8,16},{16,8},{24,24},{9,17},{17,9},{25,25},{10,18},{18,10},{26,26... | collective-permute-start | bytes 786440 | tf_op jit(solution)/shard_map/ppermute | solution.py:378

commit v5 on v4

--- a/solution.py
+++ b/solution.py
@@ -176,160 +176,145 @@
     return ref[half, pl.ds(m * group, group)].reshape(group * ref.shape[2], ref.shape[3])
 
 
-def later_keys(span, group, dtype):
-    row = lax.broadcasted_iota(jnp.int32, (span, span), 0)
-    column = lax.broadcasted_iota(jnp.int32, (span, span), 1)
-    return jnp.concatenate([(row > column).astype(jnp.float32).astype(dtype)] * group, axis=1)
-
-
-def softmax_kernel(scale, first_head, info_ref, starts_ref, q_ref, do_ref, own_a, own_b, prev_a, prev_b, far_a, far_b, *refs):
-    deep_refs = refs[-4:-2]
-    low_ref, ds_ref = refs[-2:]
-    heads, span, rows = low_ref.shape[1], low_ref.shape[3], low_ref.shape[4]
+def near_kernel(scale, info_ref, starts_ref, q_ref, do_ref, own_a, own_b, prev_a, prev_b, e_ref, dp_ref, stats_ref):
+    heads, span, rows = e_ref.shape[1], e_ref.shape[2] // 2, e_ref.shape[3]
     group = rows // span
     row = lax.broadcasted_iota(jnp.int32, (span, span), 0)
     column = lax.broadcasted_iota(jnp.int32, (span, span), 1)
-    far = row > column
-    far_wide = jnp.concatenate([far] * group, axis=1)
-    far_low = later_keys(span, group, jnp.bfloat16)
     slots = range(2)
-    halves, bias, bias_prev = [], [], []
+    kv_refs = ((prev_a, own_a), (prev_b, own_b))
+    halves, biases = [], []
     for slot in slots:
         half = info_ref[slot]
         first = info_ref[2 + slot] * span
         start = starts_ref[half]
-        position = jnp.where(far, first - 2 * span + row, first + row)
+        prev_bias = jnp.where(first - span + row >= start, 0.0, NEG)
+        own_bias = jnp.where((first + row >= start) & (row <= column), 0.0, NEG)
         halves.append(half)
-        bias.append(jnp.where(position >= start, 0.0, NEG))
-        bias_prev.append(jnp.where(first - span + row >= start, 0.0, NEG))
-    kv_refs = ((own_a, prev_a, far_a), (own_b, prev_b, far_b))
-
-    def one_head(step, carry):
-        m = first_head + step
+        biases.append(jnp.concatenate([prev_bias, own_bias], axis=0))
+
+    def one_head(m, carry):
+        scores, grads = [], []
+        for i in slots:
+            keys, values = (
+                jnp.concatenate([ref[m, which] for ref in kv_refs[i]], axis=0) for which in range(2)
+            )
+            scores.append(contract(keys, group_of(q_ref, halves[i], m, group), 1, 1))
+            grads.append(contract(values, group_of(do_ref, halves[i], m, group), 1, 1))
+        scores = [x + jnp.concatenate([biases[i]] * group, axis=1) for i, x in enumerate(scores)]
+        top = [jnp.max(x, axis=0, keepdims=True) for x in scores]
+        e = [jnp.exp2((scores[i] - top[i]) * (scale * LOG2E)) for i in slots]
+        for i in slots:
+            e_ref[i, m] = e[i]
+            dp_ref[i, m] = grads[i]
+            stats_ref[i, m, 0:1] = top[i]
+            stats_ref[i, m, 1:2] = jnp.sum(e[i], axis=0, keepdims=True)
+            stats_ref[i, m, 2:3] = jnp.sum(e[i] * grads[i], axis=0, keepdims=True)
+        return carry
+
+    lax.fori_loop(0, heads, one_head, 0)
+
+
+def far_kernel(scale, info_ref, starts_ref, q_ref, do_ref, far_a, far_b, stats_ref, deep_a, deep_b, low_ref, ds_ref, norm_ref):
+    heads, span, rows = low_ref.shape[1:]
+    group = rows // span
+    row = lax.broadcasted_iota(jnp.int32, (span, span), 0)
+    column = lax.broadcasted_iota(jnp.int32, (span, span), 1)
+    factor = scale * LOG2E
+    slots = range(2)
+    halves, biases = [], []
+    for slot in slots:
+        half = info_ref[slot]
+        first = info_ref[2 + slot] * span
+        allowed = (first - 2 * span + row >= starts_ref[half]) & (row > column)
+        halves.append(half)
+        biases.append(jnp.where(allowed, 0.0, NEG))
+    far_refs = (far_a, far_b)
+    deep_refs = (deep_a, deep_b)
+
+    def one_head(m, carry):
         queries = [group_of(q_ref, halves[i], m, group) for i in slots]
         grad_out = [group_of(do_ref, halves[i], m, group) for i in slots]
-        scores, grads = [], []
-        for i in slots:
-            own, prev, far_kv = kv_refs[i]
-            for which, rhs, result in ((0, queries[i], scores), (1, grad_out[i], grads)):
-                stack = jnp.concatenate([own[m, which], prev[m, which], far_kv[step, which]], axis=0)
-                result.append(contract(stack, rhs, 1, 1))
-        near_s = [
-            jnp.where(far_wide, x[2 * span :], x[:span]) + jnp.concatenate([bias[i]] * group, axis=1)
-            for i, x in enumerate(scores)
-        ]
-        prev_s = [
-            x[span : 2 * span] + jnp.concatenate([bias_prev[i]] * group, axis=1)
-            for i, x in enumerate(scores)
-        ]
-        near_dp = [jnp.where(far_wide, x[2 * span :], x[:span]) for x in grads]
-        prev_dp = [x[span : 2 * span] for x in grads]
-        top = [jnp.max(jnp.maximum(near_s[i], prev_s[i]), axis=0, keepdims=True) for i in slots]
-        near_e = [jnp.exp2((near_s[i] - top[i]) * (scale * LOG2E)) for i in slots]
-        prev_e = [jnp.exp2((prev_s[i] - top[i]) * (scale * LOG2E)) for i in slots]
-        inverse = [1.0 / jnp.sum(near_e[i] + prev_e[i], axis=0, keepdims=True) for i in slots]
-        near_w = [near_e[i] * inverse[i] for i in slots]
-        prev_w = [prev_e[i] * inverse[i] for i in slots]
-        delta = [
-            jnp.sum(near_w[i] * near_dp[i] + prev_w[i] * prev_dp[i], axis=0, keepdims=True)
+        scores = [
+            contract(far_refs[i][m, 0], queries[i], 1, 1)
+            + jnp.concatenate([biases[i]] * group, axis=1)
             for i in slots
         ]
-        near_low = [x.astype(jnp.bfloat16) for x in near_w]
-        near_ds = [(near_w[i] * (near_dp[i] - delta[i])).astype(jnp.bfloat16) for i in slots]
-        for i in slots:
-            low_ref[i, m, 0] = near_low[i]
-            ds_ref[i, m, 0] = near_ds[i]
-            low_ref[i, m, 1] = prev_w[i].astype(jnp.bfloat16)
-            ds_ref[i, m, 1] = (prev_w[i] * (prev_dp[i] - delta[i])).astype(jnp.bfloat16)
-        for i in slots:
-            key_term = contract(near_ds[i] * far_low, queries[i], 1, 0) * scale
-            value_term = contract(near_low[i] * far_low, grad_out[i], 1, 0)
-            deep_refs[i][m, 0] = key_term.astype(jnp.bfloat16)
-            deep_refs[i][m, 1] = value_term.astype(jnp.bfloat16)
+        grads = [contract(far_refs[i][m, 1], grad_out[i], 1, 1) for i in slots]
+        near_top = [stats_ref[i, m, 0:1] for i in slots]
+        top = [
+            jnp.maximum(near_top[i], jnp.max(scores[i], axis=0, keepdims=True)) for i in slots
+        ]
+        near = [jnp.exp2((near_top[i] - top[i]) * factor) for i in slots]
+        e = [jnp.exp2((scores[i] - top[i]) * factor) for i in slots]
+        inverse = [
+            1.0 / (near[i] * stats_ref[i, m, 1:2] + jnp.sum(e[i], axis=0, keepdims=True))
+            for i in slots
+        ]
+        delta = [
+            (
+                near[i] * stats_ref[i, m, 2:3]
+                + jnp.sum(e[i] * grads[i], axis=0, keepdims=True)
+            )
+            * inverse[i]
+            for i in slots
+        ]
+        weights = [e[i] * inverse[i] for i in slots]
+        low = [x.astype(jnp.bfloat16) for x in weights]
+        ds = [(weights[i] * (grads[i] - delta[i])).astype(jnp.bfloat16) for i in slots]
+        for i in slots:
+            low_ref[i, m] = low[i]
+            ds_ref[i, m] = ds[i]
+            norm_ref[i, m, 0:1] = near[i] * inverse[i]
+            norm_ref[i, m, 1:2] = delta[i]
+        for i in slots:
+            deep_refs[i][m, 0] = (contract(ds[i], queries[i], 1, 0) * scale).astype(jnp.bfloat16)
+            deep_refs[i][m, 1] = contract(low[i], grad_out[i], 1, 0).astype(jnp.bfloat16)
         return carry
 
-    lax.fori_loop(0, far_a.shape[0], one_head, 0)
-
-
-def rest_kernel(scale, info_ref, q_ref, do_ref, low_ref, ds_ref, *refs):
-    own_kv, prev_kv, far_kv = refs[0:2], refs[2:4], refs[4:8]
-    prev_refs = refs[8:10]
-    late_refs, late_scratch, sems = refs[10:14], refs[14:18], refs[18]
-    own_refs = late_scratch[:2]
-    o_ref, dq_ref = late_scratch[2:]
-    heads, _, span, rows = low_ref.shape[1:]
-    chunk = far_kv[0].shape[0]
+    lax.fori_loop(0, heads, one_head, 0)
+
+
+def rest_kernel(scale, info_ref, q_ref, do_ref, e_ref, dp_ref, *refs):
+    far_low, far_ds, norm = refs[:3]
+    own_kv, prev_kv, far_kv = refs[3:5], refs[5:7], refs[7:9]
+    prev_refs, own_refs = refs[9:11], refs[11:13]
+    o_ref, dq_ref = refs[13:]
+    heads, span, rows = e_ref.shape[1], e_ref.shape[2] // 2, e_ref.shape[3]
     group = rows // span
-    far_low = later_keys(span, group, jnp.bfloat16)
-    own_low = 1 - far_low
-
-    def copies(m):
-        blocks = (pl.ds(m, 1), pl.ds(m, 1)) + ((slice(None), pl.ds(m * group, group)),) * 2
-        return [
-            pltpu.make_async_copy(scratch.at[block], ref.at[block], sems.at[m, i])
-            for i, (scratch, ref, block) in enumerate(zip(late_scratch, late_refs, blocks))
-        ]
-
-    def one_head(far_pair, first_head, step, carry):
-        m = first_head + step
-        for slot in range(2):
-            half = info_ref[slot]
-            own, prev, far = own_kv[slot], prev_kv[slot], far_pair[slot]
-            queries = group_of(q_ref, half, m, group)
-            grad_out = group_of(do_ref, half, m, group)
-            low = low_ref[slot, m, 0]
-            ds = ds_ref[slot, m, 0]
-            low = jnp.concatenate([low_ref[slot, m, 1], low * own_low, low * far_low], axis=0)
-            ds = jnp.concatenate([ds_ref[slot, m, 1], ds * own_low, ds * far_low], axis=0)
-            grad_key = contract(ds[: 2 * span], queries, 1, 0) * scale
-            grad_value = contract(low[: 2 * span], grad_out, 1, 0)
-            prev_refs[slot][m, 0] = grad_key[:span]
-            prev_refs[slot][m, 1] = grad_value[:span]
-            own_refs[slot][m, 0] = grad_key[span:]
-            own_refs[slot][m, 1] = grad_value[span:]
-            keys = jnp.concatenate([prev[m, 0], own[m, 0], far[step, 0]], axis=0)
-            values = jnp.concatenate([prev[m, 1], own[m, 1], far[step, 1]], axis=0)
-            out = contract(values, low, 0, 0)
-            grad_query = contract(keys, ds, 0, 0) * scale
+    slots = range(2)
+
+    def one_head(m, carry):
+        queries = [group_of(q_ref, info_ref[i], m, group) for i in slots]
+        grad_out = [group_of(do_ref, info_ref[i], m, group) for i in slots]
+        low, ds = [], []
+        for i in slots:
+            weights = e_ref[i, m] * norm[i, m, 0:1]
+            near_ds = (weights * (dp_ref[i, m] - norm[i, m, 1:2])).astype(jnp.bfloat16)
+            low.append(jnp.concatenate([weights.astype(jnp.bfloat16), far_low[i, m]], axis=0))
+            ds.append(jnp.concatenate([near_ds, far_ds[i, m]], axis=0))
+        for i in slots:
+            grad_key = contract(ds[i][: 2 * span], queries[i], 1, 0) * scale
+            grad_value = contract(low[i][: 2 * span], grad_out[i], 1, 0)
+            prev_refs[i][m, 0] = grad_key[:span]
+            prev_refs[i][m, 1] = grad_value[:span]
+            own_refs[i][m, 0] = grad_key[span:]
+            own_refs[i][m, 1] = grad_value[span:]
+        for i in slots:
+            half = info_ref[i]
+            keys, values = (
+                jnp.concatenate([ref[i][m, which] for ref in (prev_kv, own_kv, far_kv)], axis=0)
+                for which in range(2)
+            )
+            out = contract(values, low[i], 0, 0)
+            grad_query = contract(keys, ds[i], 0, 0) * scale
             for g in range(group):
                 columns = slice(g * span, (g + 1) * span)
                 o_ref[half, m * group + g] = out[:, columns].T.astype(jnp.bfloat16)
                 dq_ref[half, m * group + g] = grad_query[:, columns].T.astype(jnp.bfloat16)
-        for copy in copies(m):
-            copy.start()
         return carry
 
-    for c in range(heads // chunk):
-        lax.fori_loop(0, chunk, functools.partial(one_head, far_kv[2 * c : 2 * c + 2], c * chunk), 0)
-
-    def finish(m, carry):
-        for copy in copies(m):
-            copy.wait()
-        return carry
-
-    lax.fori_loop(0, heads, finish, 0)
-
-
-def rest_call(scale, macs, info, q_t, do_t, low, ds, own, prev, far):
-    kv_heads = own[0].shape[0]
-    whole = pl.BlockSpec(memory_space=pltpu.VMEM)
-    outside = pl.BlockSpec(memory_space=pltpu.HBM)
-    shape = jax.ShapeDtypeStruct
-    terms = [shape(own[0].shape, jnp.float32)] * 4
-    outs = [shape(q_t.shape, jnp.bfloat16)] * 2
-    return pl.pallas_call(
-        functools.partial(rest_kernel, scale),
-        in_specs=[pl.BlockSpec(memory_space=pltpu.SMEM)] + [whole] * 12,
-        out_specs=[whole] * 2 + [outside] * 4,
-        out_shape=terms + outs,
-        scratch_shapes=[pltpu.VMEM(x.shape, x.dtype) for x in terms[2:] + outs]
-        + [pltpu.SemaphoreType.DMA((kv_heads, 4))],
-        compiler_params=pltpu.CompilerParams(vmem_limit_bytes=16 * 1024 * 1024),
-        cost_estimate=pl.CostEstimate(
-            flops=8 * macs, bytes_accessed=8 * 1024 * 1024, transcendentals=0
-        ),
-        name="rest",
-    )(info, q_t, do_t, low, ds, *own, *prev, *far)
+    lax.fori_loop(0, heads, one_head, 0)
 
 
 def unpack_kernel(info_ref, own_a, own_b, last_a, last_b, grad_keys_ref, grad_values_ref):
@@ -340,36 +325,44 @@
             ref[half, 0] = jnp.swapaxes(total, 0, 1).astype(jnp.bfloat16)
 
 
+def by_half(info, final_a, final_b):
+    even = info[:1].reshape((1,) * (final_a.ndim + 1)) == 1
+    halves = jnp.where(even, jnp.stack([final_b, final_a]), jnp.stack([final_a, final_b]))
+    halves = jnp.transpose(halves, (2, 0, 3, 1, 4))[:, :, None]
+    return halves[0], halves[1]
+
+
 def two_span_window(info, q_t, do_t, starts, own_a, own_b, pairs_a, pairs_b, scale):
     kv_heads, _, span, dim = own_a.shape
     heads = q_t.shape[1]
     rows = heads // kv_heads * span
     block = 2 * kv_heads * rows * span * dim
-    chunk = kv_heads // 2
     shape = jax.ShapeDtypeStruct
-    lows = [shape((2, kv_heads, 2, span, rows), jnp.bfloat16)] * 2
+    near = [shape((2, kv_heads, 2 * span, rows), jnp.float32)] * 2
+    near.append(shape((2, kv_heads, 8, rows), jnp.float32))
     deeps = [shape(own_a.shape, jnp.bfloat16)] * 2
+    lows = [shape((2, kv_heads, span, rows), jnp.bfloat16)] * 2
+    norm = shape((2, kv_heads, 8, rows), jnp.float32)
+    terms = [shape(own_a.shape, jnp.float32)] * 4
+    outs = [shape(q_t.shape, jnp.bfloat16)] * 2
 
     b1 = lax.ppermute(own_a, "seq", pairs_b)
     a1 = lax.ppermute(own_b, "seq", pairs_a)
-    far = []
-    for c in range(2):
-        heads_of = slice(c * chunk, (c + 1) * chunk)
-        far_b = lax.ppermute(a1[heads_of], "seq", pairs_b)
-        far_a = lax.ppermute(b1[heads_of], "seq", pairs_a)
-        far.append((far_a, far_b))
-    held = ()
-    for c in range(2):
-        args = (info, starts, q_t, do_t, own_a, own_b, a1, b1, *far[c])
-        held = vmem_call(
-            functools.partial(softmax_kernel, scale, c * chunk), deeps + lows, 4 * block, "softmax",
-            *args, *held, aliases={len(args) + i: i for i in range(len(held))},
-        )
-    deep_a, deep_b, low, ds = held
+    b2 = lax.ppermute(a1, "seq", pairs_b)
+    a2 = lax.ppermute(b1, "seq", pairs_a)
+    e, dp, stats = vmem_call(
+        functools.partial(near_kernel, scale), near, 4 * block, "near",
+        info, starts, q_t, do_t, own_a, own_b, a1, b1,
+    )
+    deep_a, deep_b, *far_parts = vmem_call(
+        functools.partial(far_kernel, scale), deeps + lows + [norm], 2 * block, "far",
+        info, starts, q_t, do_t, a2, b2, stats,
+    )
     from_a = lax.ppermute(deep_a, "seq", pairs_a)
     from_b = lax.ppermute(deep_b, "seq", pairs_b)
-    prev_a, prev_b, own_term_a, own_term_b, out, dq = rest_call(
-        scale, 10 * block, info, q_t, do_t, low, ds, (own_a, own_b), (a1, b1), (*far[0], *far[1])
+    prev_a, prev_b, own_term_a, own_term_b, out, dq = vmem_call(
+        functools.partial(rest_kernel, scale), terms + outs, 10 * block, "rest",
+        info, q_t, do_t, e, dp, *far_parts, own_a, own_b, a1, b1, a2, b2,
     )
     from_a, from_b = lax.optimization_barrier((from_a, from_b))
     next_a = (prev_a + from_b.astype(jnp.float32)).astype(jnp.bfloat16)
@@ -406,10 +399,7 @@
             now_b = (rest_b[t] + from_a.astype(jnp.float32)).astype(jnp.bfloat16)
         parts.append((out, dq, now_a, now_b))
     out, dq, final_a, final_b = (jnp.concatenate(arrays, axis=1) for arrays in zip(*parts))
-    final_a, final_b = jnp.swapaxes(final_a, 0, 1), jnp.swapaxes(final_b, 0, 1)
-    halves = jnp.where(info[0] == 1, jnp.stack([final_b, final_a]), jnp.stack([final_a, final_b]))
-    halves = jnp.transpose(halves, (2, 0, 3, 1, 4))[:, :, None]
-    return out, dq, halves[0], halves[1]
+    return out, dq, *by_half(info, jnp.swapaxes(final_a, 0, 1), jnp.swapaxes(final_b, 0, 1))
 
 
 def body(query, keys, values, grad_out, doc_starts):

time: 44.5 us -> 42.7 us (0.960)
  the two profiles are of different devices: /device:TPU:8 before, /device:TPU:12 now
where the time goes in v5:
time: 42.7 us; the launch traced here: 42.4 us
  starting transfers between devices  15.1 us (35%)
  Pallas kernels  12.2 us (29%)
  local copies, waits for them, and re-layouts  6.74 us (16%)
  waiting for transfers between devices  6.24 us (15%)
  other arithmetic  1.29 us (3%)
  between operations  0.83 us (2%)
    pallas_call x4, Pallas kernels, vmem_call(): pl.pallas_call(kernel, in_specs=[pl.BlockSpec(memory_space=pltpu.SMEM)] +...  12.2 us
    ppermute x1, starting transfers between devices, two_span_window(): b1 = lax.ppermute(own_a, 'seq', pairs_b)  4.61 us
    unnamed x2, local copies, waits for them, and re-layouts  3.3 us
    ppermute x1, starting transfers between devices, two_span_window(): b2 = lax.ppermute(a1, 'seq', pairs_b)  3.21 us
    ppermute x1, starting transfers between devices, two_span_window(): last_b = lax.ppermute(next_b, 'seq', pairs_b)  3.16 us
    ppermute x1, starting transfers between devices, two_span_window(): from_b = lax.ppermute(deep_b, 'seq', pairs_b)  3.15 us
    ppermute x1, waiting for transfers between devices, two_span_window(): b2 = lax.ppermute(a1, 'seq', pairs_b)  2.47 us
    transpose x1, local copies, waits for them, and re-layouts, body(): do_t = jnp.transpose(grad_out[:, 0], (0, 2, 1, 3))  2.08 us
  transfers between devices with their start and end apart: 8, of which 4 were waited for; matrix products, arithmetic and copies ran while one was open for 16% of the time, Pallas kernels for 18%

profile of v5, /device:TPU:12, one launch (start us, length us, event | category | flops | bytes accessed | tf_op | source)
XLA Modules:
  0.0 42.4 jit_solution(12760209242110166934)
XLA Ops:
  0.7 1.3 %constant_dynamic-slice_fusion = (bf16[1,1,128,4,128]{4,3,2,1,0:T(4,128)(2,1)S(1)}, bf16[1,1,128,4,128]{4,3,2,1,0:T(4,128)(2,1)S(1)}, bf16[1,1,128,4,128]{4,3,2,...) fusion(bf16[2,1,128,4,128]{4,3,2,1,0:T(4,128)(2,1)} %param.7, s32[]{:T(128)S(6)} %select_n.27, s32[]{:T(128)S(6)} %select_n.26, ...), kind=kLoop, calls=%fused_computation.12 | loop fusion | bytes 1048584 | tf_op jit(solution)/shard_map/jit(dynamic_index_in_dim)/dynamic_slice | solution.py:420
  2.0 0.5 %collective-permute-start = (bf16[4,2,128,128]{3,2,1,0:T(8,128)(2,1)S(1)}, bf16[4,2,128,128]{3,2,1,0:T(8,128)(2,1)S(1)}, u32[]{:S(2)}, u32[]{:S(2)}) collective-permute-start(bf16[4,2,128,128]{3,2,1,0:T(8,128)(2,1)S(1)} %maximum_bitcast_fusion.1.own_b.refs_4_), channel_id=1, source_target_pairs={{0,8},{8,0},{16,24},{24,16},{1,9},{9,1},{17,25},{25,17},{2,10},{10... | collective-permute-start | bytes 786440 | tf_op jit(solution)/shard_map/ppermute | solution.py:350
  2.6 4.6 %collective-permute-start.1 = (bf16[4,2,128,128]{3,2,1,0:T(8,128)(2,1)S(1)}, bf16[4,2,128,128]{3,2,1,0:T(8,128)(2,1)S(1)}, u32[]{:S(2)}, u32[]{:S(2)}) collective-permute-start(bf16[4,2,128,128]{3,2,1,0:T(8,128)(2,1)S(1)} %maximum_bitcast_fusion.own_a.refs_3_), channel_id=1, source_target_pairs={{8,16},{16,8},{24,24},{9,17},{17,9},{25,25},{10,18},{18,10},{26,26... | collective-permute-start | bytes 786440 | tf_op jit(solution)/shard_map/ppermute | solution.py:349
  7.3 0.1 add_multiply_fusion
  7.3 0.1 iota_add_fusion
  7.4 0.9 %select_reduce_fusion = s32[2,128]{1,0:T(2,128)S(1)} fusion(s32[2,128]{1,0:T(2,128)S(1)} %iota_add_fusion, s32[512]{0:T(512)} %param.9), kind=kLoop, calls=%fused_computation.4 | loop fusion | flops 392960 | bytes 4096 | tf_op jit(solution)/shard_map/reduce_max | solution.py:429
  8.3 2.1 %copy_bitcast_fusion = (bf16[2,16,128,128]{3,2,1,0:T(8,128)(2,1)S(1)}, bf16[2,16,128,128]{3,2,1,0:T(8,128)(2,1)S(1)}) fusion(bf16[2,1,128,16,128]{4,3,2,1,0:T(8,128)(2,1)} %param.8, bf16[2,1,128,16,128]{4,3,2,1,0:T(8,128)(2,1)} %param.5), kind=kLoop, calls=%fused_computation | loop fusion | bytes 4194304 | tf_op jit(solution)/shard_map/transpose | solution.py:425
  10.4 3.2 %collective-permute-start.3 = (bf16[4,2,128,128]{3,2,1,0:T(8,128)(2,1)S(1)}, bf16[4,2,128,128]{3,2,1,0:T(8,128)(2,1)S(1)}, u32[]{:S(2)}, u32[]{:S(2)}) collective-permute-start(bf16[4,2,128,128]{3,2,1,0:T(8,128)(2,1)S(1)} %collective-permute-done.prev_a.refs_5_), channel_id=1, source_target_pairs={{8,16},{16,8},{24,24},{9,17},{17,9},{25,25},{10,18},{18,10},{26,26... | collective-permute-start | bytes 786440 | tf_op jit(solution)/shard_map/ppermute | solution.py:351
  13.6 0.1 collective-permute-start.2
  13.7 0.1 pad_add_fusion.info_ref
  13.8 3.5 %near.1 = (f32[2,4,256,512]{3,2,1,0:T(8,128)S(1)}, f32[2,4,256,512]{3,2,1,0:T(8,128)S(1)}, f32[2,4,8,512]{3,2,1,0:T(8,128)S(1)}) custom-call(s32[4]{0:T(128)S(1)} %pad_add_fusion.info_ref, s32[2,1,128]{2,1,0:T(1,128)S(1)} %bitcast.39, bf16[2,16,128,128]{3,2,1,0:T(8,128)(2,1)S(1)} %get-tuple-element.55.q_ref, ...), custom_call_target="tpu_custom_call" | custom-call | flops 2147483648 | bytes 3146752 | tf_op jit(solution)/shard_map/near/pallas_call | solution.py:163
  17.3 2.5 %collective-permute-done.3.far_b.refs_8_ = bf16[4,2,128,128]{3,2,1,0:T(8,128)(2,1)S(1)} collective-permute-done((bf16[4,2,128,128]{3,2,1,0:T(8,128)(2,1)S(1)}, bf16[4,2,128,128]{3,2,1,0:T(8,128)(2,1)S(1)}, u32[]{:S(2)}, u32[]{:S(2)}) %collective-permute-start.3) | collective-permute-done | bytes 262176 | tf_op jit(solution)/shard_map/ppermute | solution.py:351
  19.8 0.8 %collective-permute-done.2.far_a.refs_7_ = bf16[4,2,128,128]{3,2,1,0:T(8,128)(2,1)S(1)} collective-permute-done((bf16[4,2,128,128]{3,2,1,0:T(8,128)(2,1)S(1)}, bf16[4,2,128,128]{3,2,1,0:T(8,128)(2,1)S(1)}, u32[]{:S(2)}, u32[]{:S(2)}) %collective-permute-start.2) | collective-permute-done | bytes 262176 | tf_op jit(solution)/shard_map/ppermute | solution.py:352
  20.6 3.2 %far.1 = (bf16[4,2,128,128]{3,2,1,0:T(8,128)(2,1)S(1)}, bf16[4,2,128,128]{3,2,1,0:T(8,128)(2,1)S(1)}, bf16[2,4,128,512]{3,2,1,0:T(8,128)(2,1)S(1)}, bf16[2,4,128...) custom-call(s32[4]{0:T(128)S(1)} %pad_add_fusion.info_ref, s32[2,1,128]{2,1,0:T(1,128)S(1)} %bitcast.40, ...), custom_call_target="tpu_custom_call" | custom-call | flops 1073741824 | bytes 2753536 | tf_op jit(solution)/shard_map/far/pallas_call | solution.py:163
  23.8 0.4 collective-permute-start.4
  24.1 3.1 %collective-permute-start.5 = (bf16[4,2,128,128]{3,2,1,0:T(8,128)(2,1)S(1)}, bf16[4,2,128,128]{3,2,1,0:T(8,128)(2,1)S(1)}, u32[]{:S(2)}, u32[]{:S(2)}) collective-permute-start(bf16[4,2,128,128]{3,2,1,0:T(8,128)(2,1)S(1)} %get-tuple-element.34), channel_id=1, source_target_pairs={{8,16},{16,8},{24,24},{9,17},{17,9},{25,25},{10,18},{18,10},{26,26... | collective-permute-start | bytes 786440 | tf_op jit(solution)/shard_map/ppermute | solution.py:362
  27.3 3.9 %rest.1 = (f32[4,2,128,128]{3,2,1,0:T(8,128)S(1)}, f32[4,2,128,128]{3,2,1,0:T(8,128)S(1)}, f32[4,2,128,128]{3,2,1,0:T(8,128)S(1)}, f32[4,2,128,128]{3,2,1,0:T(8,...) custom-call(s32[4]{0:T(128)S(1)} %pad_add_fusion.info_ref, ...), custom_call_target="tpu_custom_call" | custom-call | flops 5368709120 | bytes 14286848 | tf_op jit(solution)/shard_map/rest/pallas_call | solution.py:163
  31.2 1.1 %collective-permute-done.5 = bf16[4,2,128,128]{3,2,1,0:T(8,128)(2,1)S(1)} collective-permute-done((bf16[4,2,128,128]{3,2,1,0:T(8,128)(2,1)S(1)}, bf16[4,2,128,128]{3,2,1,0:T(8,128)(2,1)S(1)}, u32[]{:S(2)}, u32[]{:S(2)}) %collective-permute-start.5) | collective-permute-done | bytes 262176 | tf_op jit(solution)/shard_map/ppermute | solution.py:362
  32.4 0.1 collective-permute-start.6
  32.6 3.2 %collective-permute-start.7 = (bf16[4,2,128,128]{3,2,1,0:T(8,128)(2,1)S(1)}, bf16[4,2,128,128]{3,2,1,0:T(8,128)(2,1)S(1)}, u32[]{:S(2)}, u32[]{:S(2)}) collective-permute-start(bf16[4,2,128,128]{3,2,1,0:T(8,128)(2,1)S(1)} %add_convert_fusion), channel_id=1, source_target_pairs={{8,16},{16,8},{24,24},{9,17},{17,9},{25,25},{10,18},{18,10},{26,26... | collective-permute-start | bytes 786440 | tf_op jit(solution)/shard_map/ppermute | solution.py:371
  35.7 1.6 %copy.23 = bf16[2,1,128,16,128]{4,3,2,1,0:T(8,128)(2,1)} copy(bf16[2,1,128,16,128]{4,2,3,0,1:T(8,128)(2,1)S(1)} %bitcast.38) | data formatting | bytes 2097152
  37.4 1.6 %copy.24 = bf16[2,1,128,16,128]{4,3,2,1,0:T(8,128)(2,1)} copy(bf16[2,1,128,16,128]{4,2,3,0,1:T(8,128)(2,1)S(1)} %bitcast.37) | data formatting | bytes 2097152
  39.0 1.8 %collective-permute-done.7.last_b = bf16[4,2,128,128]{3,2,1,0:T(8,128)(2,1)S(1)} collective-permute-done((bf16[4,2,128,128]{3,2,1,0:T(8,128)(2,1)S(1)}, bf16[4,2,128,128]{3,2,1,0:T(8,128)(2,1)S(1)}, u32[]{:S(2)}, u32[]{:S(2)}) %collective-permute-start.7) | collective-permute-done | bytes 262176 | tf_op jit(solution)/shard_map/ppermute | solution.py:371
  40.8 1.6 %unpack.1 = (bf16[2,1,128,4,128]{4,3,2,1,0:T(4,128)(2,1)}, bf16[2,1,128,4,128]{4,3,2,1,0:T(4,128)(2,1)}) custom-call(s32[4]{0:T(128)S(1)} %pad_add_fusion.info_ref, f32[4,2,128,128]{3,2,1,0:T(8,128)S(1)} %get-tuple-element.30.own_a, f32[4,2,128,128]{3,2,1,0:T(8,128)S(1)} %get-tuple-element.31.own_b, ...), custom_call_target="tpu_custom_call" | custom-call | flops 8192 | bytes 1572864 | tf_op jit(solution)/shard_map/unpack/pallas_call | solution.py:163
  (12 shorter events, 0.3 us)
Async XLA Ops:
  2.0 8.4 %collective-permute-start = (bf16[4,2,128,128]{3,2,1,0:T(8,128)(2,1)S(1)}, bf16[4,2,128,128]{3,2,1,0:T(8,128)(2,1)S(1)}, u32[]{:S(2)}, u32[]{:S(2)}) collective-permute-start(bf16[4,2,128,128]{3,2,1,0:T(8,128)(2,1)S(1)} %maximum_bitcast_fusion.1.own_b.refs_4_), channel_id=1, source_target_pairs={{0,8},{8,0},{16,24},{24,16},{1,9},{9,1},{17,25},{25,17},{2,10},{10... | collective-permute-start | bytes 786440 | tf_op jit(solution)/shard_map/ppermute | solution.py:350
  2.6 11.0 %collective-permute-start.1 = (bf16[4,2,128,128]{3,2,1,0:T(8,128)(2,1)S(1)}, bf16[4,2,128,128]{3,2,1,0:T(8,128)(2,1)S(1)}, u32[]{:S(2)}, u32[]{:S(2)}) collective-permute-start(bf16[4,2,128,128]{3,2,1,0:T(8,128)(2,1)S(1)} %maximum_bitcast_fusion.own_a.refs_3_), channel_id=1, source_target_pairs={{8,16},{16,8},{24,24},{9,17},{17,9},{25,25},{10,18},{18,10},{26,26... | collective-permute-start | bytes 786440 | tf_op jit(solution)/shard_map/ppermute | solution.py:349
  10.4 9.4 %collective-permute-start.3 = (bf16[4,2,128,128]{3,2,1,0:T(8,128)(2,1)S(1)}, bf16[4,2,128,128]{3,2,1,0:T(8,128)(2,1)S(1)}, u32[]{:S(2)}, u32[]{:S(2)}) collective-permute-start(bf16[4,2,128,128]{3,2,1,0:T(8,128)(2,1)S(1)} %collective-permute-done.prev_a.refs_5_), channel_id=1, source_target_pairs={{8,16},{16,8},{24,24},{9,17},{17,9},{25,25},{10,18},{18,10},{26,26... | collective-permute-start | bytes 786440 | tf_op jit(solution)/shard_map/ppermute | solution.py:351
  13.6 7.0 %collective-permute-start.2 = (bf16[4,2,128,128]{3,2,1,0:T(8,128)(2,1)S(1)}, bf16[4,2,128,128]{3,2,1,0:T(8,128)(2,1)S(1)}, u32[]{:S(2)}, u32[]{:S(2)}) collective-permute-start(bf16[4,2,128,128]{3,2,1,0:T(8,128)(2,1)S(1)} %collective-permute-done.1.prev_b.refs_6_), channel_id=1, source_target_pairs={{0,8},{8,0},{16,24},{24,16},{1,9},{9,1},{17,25},{25,17},{2,10},{10... | collective-permute-start | bytes 786440 | tf_op jit(solution)/shard_map/ppermute | solution.py:352
  23.8 7.5 %collective-permute-start.4 = (bf16[4,2,128,128]{3,2,1,0:T(8,128)(2,1)S(1)}, bf16[4,2,128,128]{3,2,1,0:T(8,128)(2,1)S(1)}, u32[]{:S(2)}, u32[]{:S(2)}) collective-permute-start(bf16[4,2,128,128]{3,2,1,0:T(8,128)(2,1)S(1)} %get-tuple-element.33), channel_id=1, source_target_pairs={{0,8},{8,0},{16,24},{24,16},{1,9},{9,1},{17,25},{25,17},{2,10},{10... | collective-permute-start | bytes 786440 | tf_op jit(solution)/shard_map/ppermute | solution.py:361
  24.1 8.3 %collective-permute-start.5 = (bf16[4,2,128,128]{3,2,1,0:T(8,128)(2,1)S(1)}, bf16[4,2,128,128]{3,2,1,0:T(8,128)(2,1)S(1)}, u32[]{:S(2)}, u32[]{:S(2)}) collective-permute-start(bf16[4,2,128,128]{3,2,1,0:T(8,128)(2,1)S(1)} %get-tuple-element.34), channel_id=1, source_target_pairs={{8,16},{16,8},{24,24},{9,17},{17,9},{25,25},{10,18},{18,10},{26,26... | collective-permute-start | bytes 786440 | tf_op jit(solution)/shard_map/ppermute | solution.py:362
  32.4 6.6 %collective-permute-start.6 = (bf16[4,2,128,128]{3,2,1,0:T(8,128)(2,1)S(1)}, bf16[4,2,128,128]{3,2,1,0:T(8,128)(2,1)S(1)}, u32[]{:S(2)}, u32[]{:S(2)}) collective-permute-start(bf16[4,2,128,128]{3,2,1,0:T(8,128)(2,1)S(1)} %add_convert_fusion.1), channel_id=1, source_target_pairs={{0,8},{8,0},{16,24},{24,16},{1,9},{9,1},{17,25},{25,17},{2,10},{10... | collective-permute-start | bytes 786440 | tf_op jit(solution)/shard_map/ppermute | solution.py:370
  32.6 8.3 %collective-permute-start.7 = (bf16[4,2,128,128]{3,2,1,0:T(8,128)(2,1)S(1)}, bf16[4,2,128,128]{3,2,1,0:T(8,128)(2,1)S(1)}, u32[]{:S(2)}, u32[]{:S(2)}) collective-permute-start(bf16[4,2,128,128]{3,2,1,0:T(8,128)(2,1)S(1)} %add_convert_fusion), channel_id=1, source_target_pairs={{8,16},{16,8},{24,24},{9,17},{17,9},{25,25},{10,18},{18,10},{26,26... | collective-permute-start | bytes 786440 | tf_op jit(solution)/shard_map/ppermute | solution.py:371

commit v6 on v5

--- a/solution.py
+++ b/solution.py
@@ -272,7 +272,7 @@
             deep_refs[i][m, 1] = contract(low[i], grad_out[i], 1, 0).astype(jnp.bfloat16)
         return carry
 
-    lax.fori_loop(0, heads, one_head, 0)
+    lax.fori_loop(0, heads, one_head, 0, unroll=True)
 
 
 def rest_kernel(scale, info_ref, q_ref, do_ref, e_ref, dp_ref, *refs):

time: 42.7 us -> 42.2 us (0.988)
  the two profiles are of different devices: /device:TPU:12 before, /device:TPU:10 now
where the time goes in v6:
time: 42.2 us; the launch traced here: 41.9 us
  starting transfers between devices  15.1 us (36%)
  Pallas kernels  11.7 us (28%)
  local copies, waits for them, and re-layouts  6.74 us (16%)
  waiting for transfers between devices  6.24 us (15%)
  other arithmetic  1.29 us (3%)
  between operations  0.83 us (2%)
    pallas_call x4, Pallas kernels, vmem_call(): pl.pallas_call(kernel, in_specs=[pl.BlockSpec(memory_space=pltpu.SMEM)] +...  11.7 us
    ppermute x1, starting transfers between devices, two_span_window(): b1 = lax.ppermute(own_a, 'seq', pairs_b)  4.61 us
    unnamed x2, local copies, waits for them, and re-layouts  3.3 us
    ppermute x1, starting transfers between devices, two_span_window(): b2 = lax.ppermute(a1, 'seq', pairs_b)  3.21 us
    ppermute x1, starting transfers between devices, two_span_window(): last_b = lax.ppermute(next_b, 'seq', pairs_b)  3.16 us
    ppermute x1, starting transfers between devices, two_span_window(): from_b = lax.ppermute(deep_b, 'seq', pairs_b)  3.15 us
    ppermute x1, waiting for transfers between devices, two_span_window(): b2 = lax.ppermute(a1, 'seq', pairs_b)  2.47 us
    transpose x1, local copies, waits for them, and re-layouts, body(): do_t = jnp.transpose(grad_out[:, 0], (0, 2, 1, 3))  2.08 us
  transfers between devices with their start and end apart: 8, of which 4 were waited for; matrix products, arithmetic and copies ran while one was open for 16% of the time, Pallas kernels for 18%

profile of v6, /device:TPU:10, one launch (start us, length us, event | category | flops | bytes accessed | tf_op | source)
XLA Modules:
  0.0 41.9 jit_solution(10485418427452810424)
XLA Ops:
  0.7 1.3 %constant_dynamic-slice_fusion = (bf16[1,1,128,4,128]{4,3,2,1,0:T(4,128)(2,1)S(1)}, bf16[1,1,128,4,128]{4,3,2,1,0:T(4,128)(2,1)S(1)}, bf16[1,1,128,4,128]{4,3,2,...) fusion(bf16[2,1,128,4,128]{4,3,2,1,0:T(4,128)(2,1)} %param.7, s32[]{:T(128)S(6)} %select_n.27, s32[]{:T(128)S(6)} %select_n.26, ...), kind=kLoop, calls=%fused_computation.12 | loop fusion | bytes 1048584 | tf_op jit(solution)/shard_map/jit(dynamic_index_in_dim)/dynamic_slice | solution.py:420
  2.0 0.5 %collective-permute-start = (bf16[4,2,128,128]{3,2,1,0:T(8,128)(2,1)S(1)}, bf16[4,2,128,128]{3,2,1,0:T(8,128)(2,1)S(1)}, u32[]{:S(2)}, u32[]{:S(2)}) collective-permute-start(bf16[4,2,128,128]{3,2,1,0:T(8,128)(2,1)S(1)} %maximum_bitcast_fusion.1.own_b.refs_4_), channel_id=1, source_target_pairs={{0,8},{8,0},{16,24},{24,16},{1,9},{9,1},{17,25},{25,17},{2,10},{10... | collective-permute-start | bytes 786440 | tf_op jit(solution)/shard_map/ppermute | solution.py:350
  2.6 4.6 %collective-permute-start.1 = (bf16[4,2,128,128]{3,2,1,0:T(8,128)(2,1)S(1)}, bf16[4,2,128,128]{3,2,1,0:T(8,128)(2,1)S(1)}, u32[]{:S(2)}, u32[]{:S(2)}) collective-permute-start(bf16[4,2,128,128]{3,2,1,0:T(8,128)(2,1)S(1)} %maximum_bitcast_fusion.own_a.refs_3_), channel_id=1, source_target_pairs={{8,16},{16,8},{24,24},{9,17},{17,9},{25,25},{10,18},{18,10},{26,26... | collective-permute-start | bytes 786440 | tf_op jit(solution)/shard_map/ppermute | solution.py:349
  7.3 0.1 add_multiply_fusion
  7.3 0.1 iota_add_fusion
  7.4 0.9 %select_reduce_fusion = s32[2,128]{1,0:T(2,128)S(1)} fusion(s32[2,128]{1,0:T(2,128)S(1)} %iota_add_fusion, s32[512]{0:T(512)} %param.9), kind=kLoop, calls=%fused_computation.4 | loop fusion | flops 392960 | bytes 4096 | tf_op jit(solution)/shard_map/reduce_max | solution.py:429
  8.3 2.1 %copy_bitcast_fusion = (bf16[2,16,128,128]{3,2,1,0:T(8,128)(2,1)S(1)}, bf16[2,16,128,128]{3,2,1,0:T(8,128)(2,1)S(1)}) fusion(bf16[2,1,128,16,128]{4,3,2,1,0:T(8,128)(2,1)} %param.8, bf16[2,1,128,16,128]{4,3,2,1,0:T(8,128)(2,1)} %param.5), kind=kLoop, calls=%fused_computation | loop fusion | bytes 4194304 | tf_op jit(solution)/shard_map/transpose | solution.py:425
  10.4 3.2 %collective-permute-start.3 = (bf16[4,2,128,128]{3,2,1,0:T(8,128)(2,1)S(1)}, bf16[4,2,128,128]{3,2,1,0:T(8,128)(2,1)S(1)}, u32[]{:S(2)}, u32[]{:S(2)}) collective-permute-start(bf16[4,2,128,128]{3,2,1,0:T(8,128)(2,1)S(1)} %collective-permute-done.prev_a.refs_5_), channel_id=1, source_target_pairs={{8,16},{16,8},{24,24},{9,17},{17,9},{25,25},{10,18},{18,10},{26,26... | collective-permute-start | bytes 786440 | tf_op jit(solution)/shard_map/ppermute | solution.py:351
  13.6 0.1 collective-permute-start.2
  13.7 0.1 pad_add_fusion.info_ref
  13.8 3.5 %near.1 = (f32[2,4,256,512]{3,2,1,0:T(8,128)S(1)}, f32[2,4,256,512]{3,2,1,0:T(8,128)S(1)}, f32[2,4,8,512]{3,2,1,0:T(8,128)S(1)}) custom-call(s32[4]{0:T(128)S(1)} %pad_add_fusion.info_ref, s32[2,1,128]{2,1,0:T(1,128)S(1)} %bitcast.39, bf16[2,16,128,128]{3,2,1,0:T(8,128)(2,1)S(1)} %get-tuple-element.55.q_ref, ...), custom_call_target="tpu_custom_call" | custom-call | flops 2147483648 | bytes 3146752 | tf_op jit(solution)/shard_map/near/pallas_call | solution.py:163
  17.3 2.5 %collective-permute-done.3.far_b.refs_8_ = bf16[4,2,128,128]{3,2,1,0:T(8,128)(2,1)S(1)} collective-permute-done((bf16[4,2,128,128]{3,2,1,0:T(8,128)(2,1)S(1)}, bf16[4,2,128,128]{3,2,1,0:T(8,128)(2,1)S(1)}, u32[]{:S(2)}, u32[]{:S(2)}) %collective-permute-start.3) | collective-permute-done | bytes 262176 | tf_op jit(solution)/shard_map/ppermute | solution.py:351
  19.8 0.8 %collective-permute-done.2.far_a.refs_7_ = bf16[4,2,128,128]{3,2,1,0:T(8,128)(2,1)S(1)} collective-permute-done((bf16[4,2,128,128]{3,2,1,0:T(8,128)(2,1)S(1)}, bf16[4,2,128,128]{3,2,1,0:T(8,128)(2,1)S(1)}, u32[]{:S(2)}, u32[]{:S(2)}) %collective-permute-start.2) | collective-permute-done | bytes 262176 | tf_op jit(solution)/shard_map/ppermute | solution.py:352
  20.6 2.6 %far.1 = (bf16[4,2,128,128]{3,2,1,0:T(8,128)(2,1)S(1)}, bf16[4,2,128,128]{3,2,1,0:T(8,128)(2,1)S(1)}, bf16[2,4,128,512]{3,2,1,0:T(8,128)(2,1)S(1)}, bf16[2,4,128...) custom-call(s32[4]{0:T(128)S(1)} %pad_add_fusion.info_ref, s32[2,1,128]{2,1,0:T(1,128)S(1)} %bitcast.40, ...), custom_call_target="tpu_custom_call" | custom-call | flops 1073741824 | bytes 2753536 | tf_op jit(solution)/shard_map/far/pallas_call | solution.py:163
  23.2 0.4 collective-permute-start.4
  23.6 3.1 %collective-permute-start.5 = (bf16[4,2,128,128]{3,2,1,0:T(8,128)(2,1)S(1)}, bf16[4,2,128,128]{3,2,1,0:T(8,128)(2,1)S(1)}, u32[]{:S(2)}, u32[]{:S(2)}) collective-permute-start(bf16[4,2,128,128]{3,2,1,0:T(8,128)(2,1)S(1)} %get-tuple-element.34), channel_id=1, source_target_pairs={{8,16},{16,8},{24,24},{9,17},{17,9},{25,25},{10,18},{18,10},{26,26... | collective-permute-start | bytes 786440 | tf_op jit(solution)/shard_map/ppermute | solution.py:362
  26.7 3.9 %rest.1 = (f32[4,2,128,128]{3,2,1,0:T(8,128)S(1)}, f32[4,2,128,128]{3,2,1,0:T(8,128)S(1)}, f32[4,2,128,128]{3,2,1,0:T(8,128)S(1)}, f32[4,2,128,128]{3,2,1,0:T(8,...) custom-call(s32[4]{0:T(128)S(1)} %pad_add_fusion.info_ref, ...), custom_call_target="tpu_custom_call" | custom-call | flops 5368709120 | bytes 14286848 | tf_op jit(solution)/shard_map/rest/pallas_call | solution.py:163
  30.7 1.1 %collective-permute-done.5 = bf16[4,2,128,128]{3,2,1,0:T(8,128)(2,1)S(1)} collective-permute-done((bf16[4,2,128,128]{3,2,1,0:T(8,128)(2,1)S(1)}, bf16[4,2,128,128]{3,2,1,0:T(8,128)(2,1)S(1)}, u32[]{:S(2)}, u32[]{:S(2)}) %collective-permute-start.5) | collective-permute-done | bytes 262176 | tf_op jit(solution)/shard_map/ppermute | solution.py:362
  31.9 0.1 collective-permute-start.6
  32.1 3.2 %collective-permute-start.7 = (bf16[4,2,128,128]{3,2,1,0:T(8,128)(2,1)S(1)}, bf16[4,2,128,128]{3,2,1,0:T(8,128)(2,1)S(1)}, u32[]{:S(2)}, u32[]{:S(2)}) collective-permute-start(bf16[4,2,128,128]{3,2,1,0:T(8,128)(2,1)S(1)} %add_convert_fusion), channel_id=1, source_target_pairs={{8,16},{16,8},{24,24},{9,17},{17,9},{25,25},{10,18},{18,10},{26,26... | collective-permute-start | bytes 786440 | tf_op jit(solution)/shard_map/ppermute | solution.py:371
  35.2 1.6 %copy.23 = bf16[2,1,128,16,128]{4,3,2,1,0:T(8,128)(2,1)} copy(bf16[2,1,128,16,128]{4,2,3,0,1:T(8,128)(2,1)S(1)} %bitcast.38) | data formatting | bytes 2097152
  36.9 1.6 %copy.24 = bf16[2,1,128,16,128]{4,3,2,1,0:T(8,128)(2,1)} copy(bf16[2,1,128,16,128]{4,2,3,0,1:T(8,128)(2,1)S(1)} %bitcast.37) | data formatting | bytes 2097152
  38.5 1.8 %collective-permute-done.7.last_b = bf16[4,2,128,128]{3,2,1,0:T(8,128)(2,1)S(1)} collective-permute-done((bf16[4,2,128,128]{3,2,1,0:T(8,128)(2,1)S(1)}, bf16[4,2,128,128]{3,2,1,0:T(8,128)(2,1)S(1)}, u32[]{:S(2)}, u32[]{:S(2)}) %collective-permute-start.7) | collective-permute-done | bytes 262176 | tf_op jit(solution)/shard_map/ppermute | solution.py:371
  40.3 1.6 %unpack.1 = (bf16[2,1,128,4,128]{4,3,2,1,0:T(4,128)(2,1)}, bf16[2,1,128,4,128]{4,3,2,1,0:T(4,128)(2,1)}) custom-call(s32[4]{0:T(128)S(1)} %pad_add_fusion.info_ref, f32[4,2,128,128]{3,2,1,0:T(8,128)S(1)} %get-tuple-element.30.own_a, f32[4,2,128,128]{3,2,1,0:T(8,128)S(1)} %get-tuple-element.31.own_b, ...), custom_call_target="tpu_custom_call" | custom-call | flops 8192 | bytes 1572864 | tf_op jit(solution)/shard_map/unpack/pallas_call | solution.py:163
  (12 shorter events, 0.3 us)
Async XLA Ops:
  2.0 8.4 %collective-permute-start = (bf16[4,2,128,128]{3,2,1,0:T(8,128)(2,1)S(1)}, bf16[4,2,128,128]{3,2,1,0:T(8,128)(2,1)S(1)}, u32[]{:S(2)}, u32[]{:S(2)}) collective-permute-start(bf16[4,2,128,128]{3,2,1,0:T(8,128)(2,1)S(1)} %maximum_bitcast_fusion.1.own_b.refs_4_), channel_id=1, source_target_pairs={{0,8},{8,0},{16,24},{24,16},{1,9},{9,1},{17,25},{25,17},{2,10},{10... | collective-permute-start | bytes 786440 | tf_op jit(solution)/shard_map/ppermute | solution.py:350
  2.6 11.0 %collective-permute-start.1 = (bf16[4,2,128,128]{3,2,1,0:T(8,128)(2,1)S(1)}, bf16[4,2,128,128]{3,2,1,0:T(8,128)(2,1)S(1)}, u32[]{:S(2)}, u32[]{:S(2)}) collective-permute-start(bf16[4,2,128,128]{3,2,1,0:T(8,128)(2,1)S(1)} %maximum_bitcast_fusion.own_a.refs_3_), channel_id=1, source_target_pairs={{8,16},{16,8},{24,24},{9,17},{17,9},{25,25},{10,18},{18,10},{26,26... | collective-permute-start | bytes 786440 | tf_op jit(solution)/shard_map/ppermute | solution.py:349
  10.4 9.4 %collective-permute-start.3 = (bf16[4,2,128,128]{3,2,1,0:T(8,128)(2,1)S(1)}, bf16[4,2,128,128]{3,2,1,0:T(8,128)(2,1)S(1)}, u32[]{:S(2)}, u32[]{:S(2)}) collective-permute-start(bf16[4,2,128,128]{3,2,1,0:T(8,128)(2,1)S(1)} %collective-permute-done.prev_a.refs_5_), channel_id=1, source_target_pairs={{8,16},{16,8},{24,24},{9,17},{17,9},{25,25},{10,18},{18,10},{26,26... | collective-permute-start | bytes 786440 | tf_op jit(solution)/shard_map/ppermute | solution.py:351
  13.6 7.0 %collective-permute-start.2 = (bf16[4,2,128,128]{3,2,1,0:T(8,128)(2,1)S(1)}, bf16[4,2,128,128]{3,2,1,0:T(8,128)(2,1)S(1)}, u32[]{:S(2)}, u32[]{:S(2)}) collective-permute-start(bf16[4,2,128,128]{3,2,1,0:T(8,128)(2,1)S(1)} %collective-permute-done.1.prev_b.refs_6_), channel_id=1, source_target_pairs={{0,8},{8,0},{16,24},{24,16},{1,9},{9,1},{17,25},{25,17},{2,10},{10... | collective-permute-start | bytes 786440 | tf_op jit(solution)/shard_map/ppermute | solution.py:352
  23.2 7.5 %collective-permute-start.4 = (bf16[4,2,128,128]{3,2,1,0:T(8,128)(2,1)S(1)}, bf16[4,2,128,128]{3,2,1,0:T(8,128)(2,1)S(1)}, u32[]{:S(2)}, u32[]{:S(2)}) collective-permute-start(bf16[4,2,128,128]{3,2,1,0:T(8,128)(2,1)S(1)} %get-tuple-element.33), channel_id=1, source_target_pairs={{0,8},{8,0},{16,24},{24,16},{1,9},{9,1},{17,25},{25,17},{2,10},{10... | collective-permute-start | bytes 786440 | tf_op jit(solution)/shard_map/ppermute | solution.py:361
  23.6 8.3 %collective-permute-start.5 = (bf16[4,2,128,128]{3,2,1,0:T(8,128)(2,1)S(1)}, bf16[4,2,128,128]{3,2,1,0:T(8,128)(2,1)S(1)}, u32[]{:S(2)}, u32[]{:S(2)}) collective-permute-start(bf16[4,2,128,128]{3,2,1,0:T(8,128)(2,1)S(1)} %get-tuple-element.34), channel_id=1, source_target_pairs={{8,16},{16,8},{24,24},{9,17},{17,9},{25,25},{10,18},{18,10},{26,26... | collective-permute-start | bytes 786440 | tf_op jit(solution)/shard_map/ppermute | solution.py:362
  31.9 6.6 %collective-permute-start.6 = (bf16[4,2,128,128]{3,2,1,0:T(8,128)(2,1)S(1)}, bf16[4,2,128,128]{3,2,1,0:T(8,128)(2,1)S(1)}, u32[]{:S(2)}, u32[]{:S(2)}) collective-permute-start(bf16[4,2,128,128]{3,2,1,0:T(8,128)(2,1)S(1)} %add_convert_fusion.1), channel_id=1, source_target_pairs={{0,8},{8,0},{16,24},{24,16},{1,9},{9,1},{17,25},{25,17},{2,10},{10... | collective-permute-start | bytes 786440 | tf_op jit(solution)/shard_map/ppermute | solution.py:370
  32.1 8.3 %collective-permute-start.7 = (bf16[4,2,128,128]{3,2,1,0:T(8,128)(2,1)S(1)}, bf16[4,2,128,128]{3,2,1,0:T(8,128)(2,1)S(1)}, u32[]{:S(2)}, u32[]{:S(2)}) collective-permute-start(bf16[4,2,128,128]{3,2,1,0:T(8,128)(2,1)S(1)} %add_convert_fusion), channel_id=1, source_target_pairs={{8,16},{16,8},{24,24},{9,17},{17,9},{25,25},{10,18},{18,10},{26,26... | collective-permute-start | bytes 786440 | tf_op jit(solution)/shard_map/ppermute | solution.py:371

commit v7 on v6

--- a/solution.py
+++ b/solution.py
@@ -20,6 +20,15 @@
         pairs_b += [(i, i + 1), (i + 1, i)]
     pairs_b.append((count - 1, count - 1))
     return pairs_a, pairs_b
+
+
+def everyone_swaps(pairs, count, batch):
+    swaps = []
+    for b in range(batch):
+        lone = set(range(count)) - {source for source, target in pairs if source != target}
+        swaps += [(i * batch + b, j * batch + b) for i, j in pairs if i != j]
+        swaps += [(i * batch + b, i * batch + (b ^ 1)) for i in sorted(lone)]
+    return swaps
 
 
 def contract(lhs, rhs, lhs_dim, rhs_dim):
@@ -159,10 +168,10 @@
 
 def vmem_call(kernel, out_shape, macs, name, *args, aliases=None):
     whole = pl.BlockSpec(memory_space=pltpu.VMEM)
-    moved = sum(a.size * a.dtype.itemsize for a in args[1:])
+    moved = sum(a.size * a.dtype.itemsize for a in args)
     return pl.pallas_call(
         kernel,
-        in_specs=[pl.BlockSpec(memory_space=pltpu.SMEM)] + [whole] * (len(args) - 1),
+        in_specs=[whole] * len(args),
         out_specs=[whole] * len(out_shape),
         out_shape=out_shape,
         input_output_aliases=aliases or {},
@@ -172,25 +181,31 @@
     )(*args)
 
 
+def place(count):
+    device = lax.axis_index("seq")
+    half_a = 1 - device % 2
+    span_a = jnp.where(half_a == 0, device, 2 * count - 1 - device)
+    return (half_a, 1 - half_a), (span_a, 2 * count - 1 - span_a), device == count - 1
+
+
 def group_of(ref, half, m, group):
     return ref[half, pl.ds(m * group, group)].reshape(group * ref.shape[2], ref.shape[3])
 
 
-def near_kernel(scale, info_ref, starts_ref, q_ref, do_ref, own_a, own_b, prev_a, prev_b, e_ref, dp_ref, stats_ref):
+def near_kernel(scale, count, starts_ref, q_ref, do_ref, own_a, own_b, prev_a, prev_b, e_ref, dp_ref, stats_ref):
     heads, span, rows = e_ref.shape[1], e_ref.shape[2] // 2, e_ref.shape[3]
     group = rows // span
     row = lax.broadcasted_iota(jnp.int32, (span, span), 0)
     column = lax.broadcasted_iota(jnp.int32, (span, span), 1)
     slots = range(2)
     kv_refs = ((prev_a, own_a), (prev_b, own_b))
-    halves, biases = [], []
+    halves, spans, _ = place(count)
+    biases = []
     for slot in slots:
-        half = info_ref[slot]
-        first = info_ref[2 + slot] * span
-        start = starts_ref[half]
+        first = spans[slot] * span
+        start = starts_ref[spans[slot]]
         prev_bias = jnp.where(first - span + row >= start, 0.0, NEG)
         own_bias = jnp.where((first + row >= start) & (row <= column), 0.0, NEG)
-        halves.append(half)
         biases.append(jnp.concatenate([prev_bias, own_bias], axis=0))
 
     def one_head(m, carry):
@@ -215,32 +230,33 @@
     lax.fori_loop(0, heads, one_head, 0)
 
 
-def far_kernel(scale, info_ref, starts_ref, q_ref, do_ref, far_a, far_b, stats_ref, deep_a, deep_b, low_ref, ds_ref, norm_ref):
+def far_kernel(scale, count, starts_ref, q_ref, do_ref, prev_a, far_a, far_b, stats_ref, deep_a, deep_b,
+               low_ref, ds_ref, norm_ref):
     heads, span, rows = low_ref.shape[1:]
     group = rows // span
     row = lax.broadcasted_iota(jnp.int32, (span, span), 0)
     column = lax.broadcasted_iota(jnp.int32, (span, span), 1)
     factor = scale * LOG2E
     slots = range(2)
-    halves, biases = [], []
+    halves, spans, is_last = place(count)
+    biases = []
     for slot in slots:
-        half = info_ref[slot]
-        first = info_ref[2 + slot] * span
-        allowed = (first - 2 * span + row >= starts_ref[half]) & (row > column)
-        halves.append(half)
+        first = spans[slot] * span
+        allowed = (first - 2 * span + row >= starts_ref[spans[slot]]) & (row > column)
         biases.append(jnp.where(allowed, 0.0, NEG))
-    far_refs = (far_a, far_b)
     deep_refs = (deep_a, deep_b)
 
+
     def one_head(m, carry):
+        far_kv = [far_a[m], jnp.where(is_last, prev_a[m], far_b[m])]
         queries = [group_of(q_ref, halves[i], m, group) for i in slots]
         grad_out = [group_of(do_ref, halves[i], m, group) for i in slots]
         scores = [
-            contract(far_refs[i][m, 0], queries[i], 1, 1)
+            contract(far_kv[i][0], queries[i], 1, 1)
             + jnp.concatenate([biases[i]] * group, axis=1)
             for i in slots
         ]
-        grads = [contract(far_refs[i][m, 1], grad_out[i], 1, 1) for i in slots]
+        grads = [contract(far_kv[i][1], grad_out[i], 1, 1) for i in slots]
         near_top = [stats_ref[i, m, 0:1] for i in slots]
         top = [
             jnp.maximum(near_top[i], jnp.max(scores[i], axis=0, keepdims=True)) for i in slots
@@ -275,18 +291,19 @@
     lax.fori_loop(0, heads, one_head, 0, unroll=True)
 
 
-def rest_kernel(scale, info_ref, q_ref, do_ref, e_ref, dp_ref, *refs):
+def rest_kernel(scale, count, q_ref, do_ref, e_ref, dp_ref, *refs):
     far_low, far_ds, norm = refs[:3]
     own_kv, prev_kv, far_kv = refs[3:5], refs[5:7], refs[7:9]
     prev_refs, own_refs = refs[9:11], refs[11:13]
     o_ref, dq_ref = refs[13:]
+    halves, _, is_last = place(count)
     heads, span, rows = e_ref.shape[1], e_ref.shape[2] // 2, e_ref.shape[3]
     group = rows // span
     slots = range(2)
 
     def one_head(m, carry):
-        queries = [group_of(q_ref, info_ref[i], m, group) for i in slots]
-        grad_out = [group_of(do_ref, info_ref[i], m, group) for i in slots]
+        queries = [group_of(q_ref, halves[i], m, group) for i in slots]
+        grad_out = [group_of(do_ref, halves[i], m, group) for i in slots]
         low, ds = [], []
         for i in slots:
             weights = e_ref[i, m] * norm[i, m, 0:1]
@@ -301,9 +318,10 @@
             own_refs[i][m, 0] = grad_key[span:]
             own_refs[i][m, 1] = grad_value[span:]
         for i in slots:
-            half = info_ref[i]
+            half = halves[i]
+            far = far_kv[0][m] if i == 0 else jnp.where(is_last, prev_kv[0][m], far_kv[1][m])
             keys, values = (
-                jnp.concatenate([ref[i][m, which] for ref in (prev_kv, own_kv, far_kv)], axis=0)
+                jnp.concatenate([prev_kv[i][m, which], own_kv[i][m, which], far[which]], axis=0)
                 for which in range(2)
             )
             out = contract(values, low[i], 0, 0)
@@ -317,12 +335,16 @@
     lax.fori_loop(0, heads, one_head, 0)
 
 
-def unpack_kernel(info_ref, own_a, own_b, last_a, last_b, grad_keys_ref, grad_values_ref):
-    for slot, (own, last) in enumerate(((own_a, last_b), (own_b, last_a))):
-        half = info_ref[slot]
-        for which, ref in enumerate((grad_keys_ref, grad_values_ref)):
-            total = own[:, which] + last[:, which].astype(jnp.float32)
-            ref[half, 0] = jnp.swapaxes(total, 0, 1).astype(jnp.bfloat16)
+def unpack_kernel(count, own_a, own_b, last_a, last_b, next_b, grad_keys_ref, grad_values_ref):
+    halves, _, is_last = place(count)
+    for which, ref in enumerate((grad_keys_ref, grad_values_ref)):
+        sums = (
+            own_a[:, which]
+            + jnp.where(is_last, next_b[:, which], last_b[:, which]).astype(jnp.float32),
+            own_b[:, which] + last_a[:, which].astype(jnp.float32),
+        )
+        for slot, total in enumerate(sums):
+            ref[halves[slot], 0] = jnp.swapaxes(total, 0, 1).astype(jnp.bfloat16)
 
 
 def by_half(info, final_a, final_b):
@@ -332,7 +354,7 @@
     return halves[0], halves[1]
 
 
-def two_span_window(info, q_t, do_t, starts, own_a, own_b, pairs_a, pairs_b, scale):
+def two_span_window(count, q_t, do_t, starts, own_a, own_b, pairs_a, pairs_b, scale):
     kv_heads, _, span, dim = own_a.shape
     heads = q_t.shape[1]
     rows = heads // kv_heads * span
@@ -346,32 +368,40 @@
     terms = [shape(own_a.shape, jnp.float32)] * 4
     outs = [shape(q_t.shape, jnp.bfloat16)] * 2
 
-    b1 = lax.ppermute(own_a, "seq", pairs_b)
+    both_axes = ("seq", "batch")
+    swaps_b = everyone_swaps(pairs_b, count, lax.axis_size("batch"))
+    last = jnp.full((dim,), lax.axis_index("seq") == count - 1).astype(jnp.int32)
+    own_a, own_b, last = lax.optimization_barrier((own_a, own_b, last))
+    is_last = last == 1
+    b1 = lax.ppermute(own_a, both_axes, swaps_b)
     a1 = lax.ppermute(own_b, "seq", pairs_a)
-    b2 = lax.ppermute(a1, "seq", pairs_b)
+    b1 = jnp.where(is_last, own_a, b1)
+    b2 = lax.ppermute(a1, both_axes, swaps_b)
     a2 = lax.ppermute(b1, "seq", pairs_a)
     e, dp, stats = vmem_call(
-        functools.partial(near_kernel, scale), near, 4 * block, "near",
-        info, starts, q_t, do_t, own_a, own_b, a1, b1,
+        functools.partial(near_kernel, scale, count), near, 4 * block, "near",
+        starts, q_t, do_t, own_a, own_b, a1, b1,
     )
     deep_a, deep_b, *far_parts = vmem_call(
-        functools.partial(far_kernel, scale), deeps + lows + [norm], 2 * block, "far",
-        info, starts, q_t, do_t, a2, b2, stats,
+        functools.partial(far_kernel, scale, count), deeps + lows + [norm], 2 * block, "far",
+        starts, q_t, do_t, a1, a2, b2, stats,
     )
     from_a = lax.ppermute(deep_a, "seq", pairs_a)
-    from_b = lax.ppermute(deep_b, "seq", pairs_b)
+    from_b = lax.ppermute(deep_b, both_axes, swaps_b)
     prev_a, prev_b, own_term_a, own_term_b, out, dq = vmem_call(
-        functools.partial(rest_kernel, scale), terms + outs, 10 * block, "rest",
-        info, q_t, do_t, e, dp, *far_parts, own_a, own_b, a1, b1, a2, b2,
+        functools.partial(rest_kernel, scale, count), terms + outs, 10 * block, "rest",
+        q_t, do_t, e, dp, *far_parts, own_a, own_b, a1, b1, a2, b2,
     )
     from_a, from_b = lax.optimization_barrier((from_a, from_b))
+    from_b = jnp.where(is_last, deep_b, from_b)
     next_a = (prev_a + from_b.astype(jnp.float32)).astype(jnp.bfloat16)
     next_b = (prev_b + from_a.astype(jnp.float32)).astype(jnp.bfloat16)
     last_a = lax.ppermute(next_a, "seq", pairs_a)
-    last_b = lax.ppermute(next_b, "seq", pairs_b)
+    last_b = lax.ppermute(next_b, both_axes, swaps_b)
     grads = [shape((2, 1, span, kv_heads, dim), jnp.bfloat16)] * 2
     grad_keys, grad_values = vmem_call(
-        unpack_kernel, grads, 1024, "unpack", info, own_term_a, own_term_b, last_a, last_b
+        functools.partial(unpack_kernel, count), grads, 1024, "unpack",
+        own_term_a, own_term_b, last_a, last_b, next_b,
     )
     return out, dq, grad_keys, grad_values
 
@@ -402,6 +432,12 @@
     return out, dq, *by_half(info, jnp.swapaxes(final_a, 0, 1), jnp.swapaxes(final_b, 0, 1))
 
 
+def first_of_document(doc_starts, spans, span):
+    token = spans[:, None] * span + jnp.arange(span, dtype=jnp.int32)[None, :]
+    below = doc_starts[None, None, :] <= token[:, :, None]
+    return jnp.max(jnp.where(below, doc_starts[None, None, :], 0), axis=2)[:, None, :]
+
+
 def body(query, keys, values, grad_out, doc_starts):
     count = lax.axis_size("seq")
     device = lax.axis_index("seq")
@@ -410,29 +446,25 @@
     dim = query.shape[4]
     scale = dim ** (-0.5)
     pairs_a, pairs_b = swap_pairs(count)
-    parity = device % 2
-
-    half_a, half_b = 1 - parity, parity
-    span_a = jnp.where(half_a == 0, device, 2 * count - 1 - device)
-    info = jnp.stack([half_a, half_b, span_a, 2 * count - 1 - span_a]).astype(jnp.int32)
+    half_a = 1 - device % 2
 
     def payload(half):
         pair = [lax.dynamic_index_in_dim(x[:, 0], half, 0, keepdims=False) for x in (keys, values)]
         return jnp.transpose(jnp.stack(pair), (2, 0, 1, 3))
 
-    own_a, own_b = payload(half_a), payload(half_b)
+    own_a, own_b = payload(half_a), payload(1 - half_a)
     q_t = jnp.transpose(query[:, 0], (0, 2, 1, 3))
     do_t = jnp.transpose(grad_out[:, 0], (0, 2, 1, 3))
-    spans = jnp.stack([device, 2 * count - 1 - device])
-    token = spans[:, None] * span + jnp.arange(span, dtype=jnp.int32)[None, :]
-    below = doc_starts[None, None, :] <= token[:, :, None]
-    starts = jnp.max(jnp.where(below, doc_starts[None, None, :], 0), axis=2)[:, None, :]
-
     if window == 2:
+        starts = first_of_document(doc_starts, jnp.arange(2 * count, dtype=jnp.int32), span)
         out, dq, grad_keys, grad_values = two_span_window(
-            info, q_t, do_t, starts, own_a, own_b, pairs_a, pairs_b, scale
+            count, q_t, do_t, starts, own_a, own_b, pairs_a, pairs_b, scale
         )
     else:
+        spans = jnp.stack([device, 2 * count - 1 - device])
+        starts = first_of_document(doc_starts, spans, span)
+        span_a = jnp.where(half_a == 0, device, 2 * count - 1 - device)
+        info = jnp.stack([half_a, 1 - half_a, span_a, 2 * count - 1 - span_a]).astype(jnp.int32)
         out, dq, grad_keys, grad_values = any_window(
             info, q_t, do_t, starts, own_a, own_b, pairs_a, pairs_b, window, scale
         )

time: 42.2 us -> 37.5 us (0.89)
  the two profiles are of different devices: /device:TPU:10 before, /device:TPU:0 now
where the time goes in v7:
time: 37.5 us; the launch traced here: 37.4 us
  starting transfers between devices  14.6 us (39%)
  Pallas kernels  9.46 us (25%)
  waiting for transfers between devices  6.42 us (17%)
  local copies, waits for them, and re-layouts  5.36 us (14%)
  between operations  0.82 us (2%)
  other arithmetic  0.76 us (2%)
    pallas_call x4, Pallas kernels, vmem_call(): pl.pallas_call(kernel, in_specs=[whole] * len(args), out_specs=[whole] *...  9.46 us
    ppermute x1, starting transfers between devices, two_span_window(): a2 = lax.ppermute(b1, 'seq', pairs_a)  7.7 us
    unnamed x8, local copies, waits for them, and re-layouts  3.31 us
    ppermute x1, starting transfers between devices, two_span_window(): a1 = lax.ppermute(own_b, 'seq', pairs_a)  3.09 us
    ppermute x1, waiting for transfers between devices, two_span_window(): last_a = lax.ppermute(next_a, 'seq', pairs_a)  2 us
    ppermute x1, waiting for transfers between devices, two_span_window(): a2 = lax.ppermute(b1, 'seq', pairs_a)  1.99 us
    ppermute x1, starting transfers between devices, two_span_window(): from_a = lax.ppermute(deep_a, 'seq', pairs_a)  1.89 us
    ppermute x1, starting transfers between devices, two_span_window(): last_a = lax.ppermute(next_a, 'seq', pairs_a)  1.81 us
  transfers between devices with their start and end apart: 8, of which 4 were waited for; matrix products, arithmetic and copies ran while one was open for 12% of the time, Pallas kernels for 17%

profile of v7, /device:TPU:0, one launch (start us, length us, event | category | flops | bytes accessed | tf_op | source)
XLA Modules:
  0.0 37.4 jit_solution(10632741606562481109)
XLA Ops:
  0.7 1.4 %constant_dynamic-slice_fusion = (bf16[1,1,128,4,128]{4,3,2,1,0:T(4,128)(2,1)S(1)}, bf16[1,1,128,4,128]{4,3,2,1,0:T(4,128)(2,1)S(1)}, bf16[1,1,128,4,128]{4,3,2,...) fusion(bf16[2,1,128,4,128]{4,3,2,1,0:T(4,128)(2,1)} %param.7, s32[]{:T(128)S(6)} %select_n.30, s32[]{:T(128)S(6)} %select_n.29, ...), kind=kLoop, calls=%fused_computation.13 | loop fusion | bytes 1048584 | tf_op jit(solution)/shard_map/jit(dynamic_index_in_dim)/dynamic_slice | solution.py:452
  2.3 3.1 %collective-permute-start = (bf16[4,2,128,128]{3,2,1,0:T(8,128)(2,1)S(1)}, bf16[4,2,128,128]{3,2,1,0:T(8,128)(2,1)S(1)}, u32[]{:S(2)}, u32[]{:S(2)}) collective-permute-start(bf16[4,2,128,128]{3,2,1,0:T(8,128)(2,1)S(1)} %maximum_bitcast_fusion.1.own_b.refs_4_), channel_id=1, source_target_pairs={{0,8},{8,0},{16,24},{24,16},{1,9},{9,1},{17,25},{25,17},{2,10},{10... | collective-permute-start | bytes 786440 | tf_op jit(solution)/shard_map/ppermute | solution.py:377
  5.4 0.0 copy-start.2
  5.4 0.5 %copy_bitcast_fusion = (bf16[2,16,128,128]{3,2,1,0:T(8,128)(2,1)S(1)}, bf16[2,16,128,128]{3,2,1,0:T(8,128)(2,1)S(1)}) fusion(bf16[2,1,128,16,128]{4,3,2,1,0:T(8,128)(2,1)S(1)} %copy-done, bf16[2,1,128,16,128]{4,3,2,1,0:T(8,128)(2,1)S(1)} %copy-done.1), kind=kLoop, calls=%fused_computation.1 | loop fusion | bytes 4194304 | tf_op jit(solution)/shard_map/transpose | solution.py:457
  6.0 0.1 iota_add_fusion
  6.0 0.9 %collective-permute-done.1 = bf16[4,2,128,128]{3,2,1,0:T(8,128)(2,1)S(1)} collective-permute-done((bf16[4,2,128,128]{3,2,1,0:T(8,128)(2,1)S(1)}, bf16[4,2,128,128]{3,2,1,0:T(8,128)(2,1)S(1)}, u32[]{:S(2)}, u32[]{:S(2)}) %collective-permute-start.1) | collective-permute-done | bytes 262176 | tf_op jit(solution)/shard_map/ppermute | solution.py:376
  7.0 7.7 %collective-permute-start.2 = (bf16[4,2,128,128]{3,2,1,0:T(8,128)(2,1)S(1)}, bf16[4,2,128,128]{3,2,1,0:T(8,128)(2,1)S(1)}, u32[]{:S(2)}, u32[]{:S(2)}) collective-permute-start(bf16[4,2,128,128]{3,2,1,0:T(8,128)(2,1)S(1)} %broadcast_select_fusion.prev_b.refs_6_), channel_id=1, source_target_pairs={{0,8},{8,0},{16,24},{24,16},{1,9},{9,1},{17,25},{25,17},{2,10},{10... | collective-permute-start | bytes 786440 | tf_op jit(solution)/shard_map/ppermute | solution.py:380
  14.7 0.4 %select_reduce_fusion = s32[8,128]{1,0:T(8,128)S(1)} fusion(s32[8,128]{1,0:T(8,128)S(1)} %iota_add_fusion, s32[512]{0:T(512)S(1)} %copy-done.2), kind=kLoop, calls=%fused_computation | loop fusion | flops 1571840 | bytes 10240 | tf_op jit(solution)/shard_map/reduce_max | solution.py:438
  15.1 3.0 %near.1 = (f32[2,4,256,512]{3,2,1,0:T(8,128)S(1)}, f32[2,4,256,512]{3,2,1,0:T(8,128)S(1)}, f32[2,4,8,512]{3,2,1,0:T(8,128)S(1)}) custom-call(s32[8,1,128]{2,1,0:T(1,128)S(1)} %bitcast.33, bf16[2,16,128,128]{3,2,1,0:T(8,128)(2,1)S(1)} %get-tuple-element.61.q_ref, bf16[2,16,128,128]{3,2,1,0:T(8,128)(2,1)S(1)} %get-tuple-element.60.do_ref, ...), custom_call_target="tpu_custom_call" | custom-call | flops 2147483648 | bytes 3149824 | tf_op jit(solution)/shard_map/near/pallas_call | solution.py:172
  18.1 2.0 %collective-permute-done.2.far_a.refs_7_ = bf16[4,2,128,128]{3,2,1,0:T(8,128)(2,1)S(1)} collective-permute-done((bf16[4,2,128,128]{3,2,1,0:T(8,128)(2,1)S(1)}, bf16[4,2,128,128]{3,2,1,0:T(8,128)(2,1)S(1)}, u32[]{:S(2)}, u32[]{:S(2)}) %collective-permute-start.2) | collective-permute-done | bytes 262176 | tf_op jit(solution)/shard_map/ppermute | solution.py:380
  20.1 2.0 %far.1 = (bf16[4,2,128,128]{3,2,1,0:T(8,128)(2,1)S(1)}, bf16[4,2,128,128]{3,2,1,0:T(8,128)(2,1)S(1)}, bf16[2,4,128,512]{3,2,1,0:T(8,128)(2,1)S(1)}, bf16[2,4,128...) custom-call(s32[8,1,128]{2,1,0:T(1,128)S(1)} %bitcast.34, bf16[2,16,128,128]{3,2,1,0:T(8,128)(2,1)S(1)} %get-tuple-element.61.q_ref, ...), custom_call_target="tpu_custom_call" | custom-call | flops 1073741824 | bytes 3018752 | tf_op jit(solution)/shard_map/far/pallas_call | solution.py:172
  22.1 1.9 %collective-permute-start.4 = (bf16[4,2,128,128]{3,2,1,0:T(8,128)(2,1)S(1)}, bf16[4,2,128,128]{3,2,1,0:T(8,128)(2,1)S(1)}, u32[]{:S(2)}, u32[]{:S(2)}) collective-permute-start(bf16[4,2,128,128]{3,2,1,0:T(8,128)(2,1)S(1)} %get-tuple-element.40), channel_id=1, source_target_pairs={{0,8},{8,0},{16,24},{24,16},{1,9},{9,1},{17,25},{25,17},{2,10},{10... | collective-permute-start | bytes 786440 | tf_op jit(solution)/shard_map/ppermute | solution.py:389
  24.0 0.0 collective-permute-start.5
  24.0 3.4 %rest.1 = (f32[4,2,128,128]{3,2,1,0:T(8,128)S(1)}, f32[4,2,128,128]{3,2,1,0:T(8,128)S(1)}, f32[4,2,128,128]{3,2,1,0:T(8,128)S(1)}, f32[4,2,128,128]{3,2,1,0:T(8,...) custom-call(bf16[2,16,128,128]{3,2,1,0:T(8,128)(2,1)S(1)} %get-tuple-element.61.q_ref, ...), custom_call_target="tpu_custom_call" | custom-call | flops 5368709120 | bytes 14286848 | tf_op jit(solution)/shard_map/rest/pallas_call | solution.py:172
  27.4 1.5 %collective-permute-done.4 = bf16[4,2,128,128]{3,2,1,0:T(8,128)(2,1)S(1)} collective-permute-done((bf16[4,2,128,128]{3,2,1,0:T(8,128)(2,1)S(1)}, bf16[4,2,128,128]{3,2,1,0:T(8,128)(2,1)S(1)}, u32[]{:S(2)}, u32[]{:S(2)}) %collective-permute-start.4) | collective-permute-done | bytes 262176 | tf_op jit(solution)/shard_map/ppermute | solution.py:389
  29.0 0.1 add_convert_fusion.1
  29.1 1.8 %collective-permute-start.6 = (bf16[4,2,128,128]{3,2,1,0:T(8,128)(2,1)S(1)}, bf16[4,2,128,128]{3,2,1,0:T(8,128)(2,1)S(1)}, u32[]{:S(2)}, u32[]{:S(2)}) collective-permute-start(bf16[4,2,128,128]{3,2,1,0:T(8,128)(2,1)S(1)} %add_convert_fusion.1), channel_id=1, source_target_pairs={{0,8},{8,0},{16,24},{24,16},{1,9},{9,1},{17,25},{25,17},{2,10},{10... | collective-permute-start | bytes 786440 | tf_op jit(solution)/shard_map/ppermute | solution.py:399
  30.9 0.1 add_convert_fusion.next_b
  30.9 0.1 collective-permute-start.7
  31.0 1.6 %copy.23 = bf16[2,1,128,16,128]{4,3,2,1,0:T(8,128)(2,1)} copy(bf16[2,1,128,16,128]{4,2,3,0,1:T(8,128)(2,1)S(1)} %bitcast.32) | data formatting | bytes 2097152
  32.7 1.6 %copy.24 = bf16[2,1,128,16,128]{4,3,2,1,0:T(8,128)(2,1)} copy(bf16[2,1,128,16,128]{4,2,3,0,1:T(8,128)(2,1)S(1)} %bitcast.31) | data formatting | bytes 2097152
  34.3 2.0 %collective-permute-done.6.last_a = bf16[4,2,128,128]{3,2,1,0:T(8,128)(2,1)S(1)} collective-permute-done((bf16[4,2,128,128]{3,2,1,0:T(8,128)(2,1)S(1)}, bf16[4,2,128,128]{3,2,1,0:T(8,128)(2,1)S(1)}, u32[]{:S(2)}, u32[]{:S(2)}) %collective-permute-start.6) | collective-permute-done | bytes 262176 | tf_op jit(solution)/shard_map/ppermute | solution.py:399
  36.3 0.0 collective-permute-done.7.last_b
  36.3 1.1 %unpack.1 = (bf16[2,1,128,4,128]{4,3,2,1,0:T(4,128)(2,1)}, bf16[2,1,128,4,128]{4,3,2,1,0:T(4,128)(2,1)}) custom-call(f32[4,2,128,128]{3,2,1,0:T(8,128)S(1)} %get-tuple-element.36.own_a, f32[4,2,128,128]{3,2,1,0:T(8,128)S(1)} %get-tuple-element.37.own_b, bf16[4,2,128,128]{3,2,1,0:T(8,128)(2,1)S(1)} %collective-permute-done.6.last_a, ...), custom_call_target="tpu_custom_call" | custom-call | flops 8192 | bytes 1835008 | tf_op jit(solution)/shard_map/unpack/pallas_call | solution.py:172
  (20 shorter events, 0.2 us)
Async XLA Ops:
  0.6 4.8 %copy-start = (bf16[2,1,128,16,128]{4,3,2,1,0:T(8,128)(2,1)S(1)}, bf16[2,1,128,16,128]{4,3,2,1,0:T(8,128)(2,1)}, u32[]{:S(2)}) copy-start(bf16[2,1,128,16,128]{4,3,2,1,0:T(8,128)(2,1)} %param.8) | copy-start | bytes 3145732
  0.6 4.8 %copy-start.1 = (bf16[2,1,128,16,128]{4,3,2,1,0:T(8,128)(2,1)S(1)}, bf16[2,1,128,16,128]{4,3,2,1,0:T(8,128)(2,1)}, u32[]{:S(2)}) copy-start(bf16[2,1,128,16,128]{4,3,2,1,0:T(8,128)(2,1)} %param.5) | copy-start | bytes 3145732
  2.3 12.4 %collective-permute-start = (bf16[4,2,128,128]{3,2,1,0:T(8,128)(2,1)S(1)}, bf16[4,2,128,128]{3,2,1,0:T(8,128)(2,1)S(1)}, u32[]{:S(2)}, u32[]{:S(2)}) collective-permute-start(bf16[4,2,128,128]{3,2,1,0:T(8,128)(2,1)S(1)} %maximum_bitcast_fusion.1.own_b.refs_4_), channel_id=1, source_target_pairs={{0,8},{8,0},{16,24},{24,16},{1,9},{9,1},{17,25},{25,17},{2,10},{10... | collective-permute-start | bytes 786440 | tf_op jit(solution)/shard_map/ppermute | solution.py:377
  5.4 1.5 %collective-permute-start.1 = (bf16[4,2,128,128]{3,2,1,0:T(8,128)(2,1)S(1)}, bf16[4,2,128,128]{3,2,1,0:T(8,128)(2,1)S(1)}, u32[]{:S(2)}, u32[]{:S(2)}) collective-permute-start(bf16[4,2,128,128]{3,2,1,0:T(8,128)(2,1)S(1)} %maximum_bitcast_fusion.own_a.refs_3_), channel_id=1, source_target_pairs={{8,16},{16,8},{0,1},{24,25},{9,17},{17,9},{1,0},{25,24},{10,18},{1... | collective-permute-start | bytes 786440 | tf_op jit(solution)/shard_map/ppermute | solution.py:376
  5.4 9.3 %copy-start.2 = (s32[512]{0:T(512)S(1)}, s32[512]{0:T(512)}, u32[]{:S(2)}) copy-start(s32[512]{0:T(512)} %param.9) | copy-start | bytes 6148
  7.0 13.1 %collective-permute-start.2 = (bf16[4,2,128,128]{3,2,1,0:T(8,128)(2,1)S(1)}, bf16[4,2,128,128]{3,2,1,0:T(8,128)(2,1)S(1)}, u32[]{:S(2)}, u32[]{:S(2)}) collective-permute-start(bf16[4,2,128,128]{3,2,1,0:T(8,128)(2,1)S(1)} %broadcast_select_fusion.prev_b.refs_6_), channel_id=1, source_target_pairs={{0,8},{8,0},{16,24},{24,16},{1,9},{9,1},{17,25},{25,17},{2,10},{10... | collective-permute-start | bytes 786440 | tf_op jit(solution)/shard_map/ppermute | solution.py:380
  14.7 3.4 %collective-permute-start.3 = (bf16[4,2,128,128]{3,2,1,0:T(8,128)(2,1)S(1)}, bf16[4,2,128,128]{3,2,1,0:T(8,128)(2,1)S(1)}, u32[]{:S(2)}, u32[]{:S(2)}) collective-permute-start(bf16[4,2,128,128]{3,2,1,0:T(8,128)(2,1)S(1)} %collective-permute-done.prev_a.refs_5_), channel_id=1, source_target_pairs={{8,16},{16,8},{0,1},{24,25},{9,17},{17,9},{1,0},{25,24},{10,18},{1... | collective-permute-start | bytes 786440 | tf_op jit(solution)/shard_map/ppermute | solution.py:379
  22.1 6.8 %collective-permute-start.4 = (bf16[4,2,128,128]{3,2,1,0:T(8,128)(2,1)S(1)}, bf16[4,2,128,128]{3,2,1,0:T(8,128)(2,1)S(1)}, u32[]{:S(2)}, u32[]{:S(2)}) collective-permute-start(bf16[4,2,128,128]{3,2,1,0:T(8,128)(2,1)S(1)} %get-tuple-element.40), channel_id=1, source_target_pairs={{0,8},{8,0},{16,24},{24,16},{1,9},{9,1},{17,25},{25,17},{2,10},{10... | collective-permute-start | bytes 786440 | tf_op jit(solution)/shard_map/ppermute | solution.py:389
  24.0 4.9 %collective-permute-start.5 = (bf16[4,2,128,128]{3,2,1,0:T(8,128)(2,1)S(1)}, bf16[4,2,128,128]{3,2,1,0:T(8,128)(2,1)S(1)}, u32[]{:S(2)}, u32[]{:S(2)}) collective-permute-start(bf16[4,2,128,128]{3,2,1,0:T(8,128)(2,1)S(1)} %get-tuple-element.39), channel_id=1, source_target_pairs={{8,16},{16,8},{0,1},{24,25},{9,17},{17,9},{1,0},{25,24},{10,18},{1... | collective-permute-start | bytes 786440 | tf_op jit(solution)/shard_map/ppermute | solution.py:390
  29.1 7.3 %collective-permute-start.6 = (bf16[4,2,128,128]{3,2,1,0:T(8,128)(2,1)S(1)}, bf16[4,2,128,128]{3,2,1,0:T(8,128)(2,1)S(1)}, u32[]{:S(2)}, u32[]{:S(2)}) collective-permute-start(bf16[4,2,128,128]{3,2,1,0:T(8,128)(2,1)S(1)} %add_convert_fusion.1), channel_id=1, source_target_pairs={{0,8},{8,0},{16,24},{24,16},{1,9},{9,1},{17,25},{25,17},{2,10},{10... | collective-permute-start | bytes 786440 | tf_op jit(solution)/shard_map/ppermute | solution.py:399
  30.9 5.4 %collective-permute-start.7 = (bf16[4,2,128,128]{3,2,1,0:T(8,128)(2,1)S(1)}, bf16[4,2,128,128]{3,2,1,0:T(8,128)(2,1)S(1)}, u32[]{:S(2)}, u32[]{:S(2)}) collective-permute-start(bf16[4,2,128,128]{3,2,1,0:T(8,128)(2,1)S(1)} %add_convert_fusion.next_b), channel_id=1, source_target_pairs={{8,16},{16,8},{0,1},{24,25},{9,17},{17,9},{1,0},{25,24},{10,18},{1... | collective-permute-start | bytes 786440 | tf_op jit(solution)/shard_map/ppermute | solution.py:400

commit v8 on v7

--- a/solution.py
+++ b/solution.py
@@ -335,6 +335,13 @@
     lax.fori_loop(0, heads, one_head, 0)
 
 
+def merge_kernel(count, prev_a, prev_b, from_a, from_b, deep_b, next_a_ref, next_b_ref):
+    _, _, is_last = place(count)
+    from_far = jnp.where(is_last, deep_b[...], from_b[...])
+    next_a_ref[...] = (prev_a[...] + from_far.astype(jnp.float32)).astype(jnp.bfloat16)
+    next_b_ref[...] = (prev_b[...] + from_a[...].astype(jnp.float32)).astype(jnp.bfloat16)
+
+
 def unpack_kernel(count, own_a, own_b, last_a, last_b, next_b, grad_keys_ref, grad_values_ref):
     halves, _, is_last = place(count)
     for which, ref in enumerate((grad_keys_ref, grad_values_ref)):
@@ -392,10 +399,10 @@
         functools.partial(rest_kernel, scale, count), terms + outs, 10 * block, "rest",
         q_t, do_t, e, dp, *far_parts, own_a, own_b, a1, b1, a2, b2,
     )
-    from_a, from_b = lax.optimization_barrier((from_a, from_b))
-    from_b = jnp.where(is_last, deep_b, from_b)
-    next_a = (prev_a + from_b.astype(jnp.float32)).astype(jnp.bfloat16)
-    next_b = (prev_b + from_a.astype(jnp.float32)).astype(jnp.bfloat16)
+    next_a, next_b = vmem_call(
+        functools.partial(merge_kernel, count), deeps, 1024, "merge",
+        prev_a, prev_b, from_a, from_b, deep_b,
+    )
     last_a = lax.ppermute(next_a, "seq", pairs_a)
     last_b = lax.ppermute(next_b, both_axes, swaps_b)
     grads = [shape((2, 1, span, kv_heads, dim), jnp.bfloat16)] * 2

time: 37.5 us -> 37.5 us (level)
    pallas_call x4 -> x5, Pallas kernels: 9.46 us -> 9.56 us  [vmem_call(): pl.pallas_call(kernel, in_specs=[whole] * len(args), out_specs=[whole] *...]
where the time goes in v8:
time: 37.5 us; the launch traced here: 37.4 us
  starting transfers between devices  14.5 us (39%)
  Pallas kernels  9.56 us (25%)
  waiting for transfers between devices  6.57 us (18%)
  local copies, waits for them, and re-layouts  5.36 us (14%)
  between operations  0.82 us (2%)
  other arithmetic  0.59 us (2%)
    pallas_call x5, Pallas kernels, vmem_call(): pl.pallas_call(kernel, in_specs=[whole] * len(args), out_specs=[whole] *...  9.56 us
    ppermute x1, starting transfers between devices, two_span_window(): a2 = lax.ppermute(b1, 'seq', pairs_a)  7.7 us
    unnamed x8, local copies, waits for them, and re-layouts  3.31 us
    ppermute x1, starting transfers between devices, two_span_window(): a1 = lax.ppermute(own_b, 'seq', pairs_a)  3.09 us
    ppermute x1, waiting for transfers between devices, two_span_window(): last_a = lax.ppermute(next_a, 'seq', pairs_a)  2.13 us
    ppermute x1, waiting for transfers between devices, two_span_window(): a2 = lax.ppermute(b1, 'seq', pairs_a)  1.99 us
    ppermute x1, starting transfers between devices, two_span_window(): from_a = lax.ppermute(deep_a, 'seq', pairs_a)  1.89 us
    ppermute x1, starting transfers between devices, two_span_window(): last_a = lax.ppermute(next_a, 'seq', pairs_a)  1.81 us
  transfers between devices with their start and end apart: 8, of which 4 were waited for; matrix products, arithmetic and copies ran while one was open for 12% of the time, Pallas kernels for 17%

profile of v8, /device:TPU:0, one launch (start us, length us, event | category | flops | bytes accessed | tf_op | source)
XLA Modules:
  0.0 37.4 jit_solution(13743551158349604484)
XLA Ops:
  0.7 1.4 %constant_dynamic-slice_fusion = (bf16[1,1,128,4,128]{4,3,2,1,0:T(4,128)(2,1)S(1)}, bf16[1,1,128,4,128]{4,3,2,1,0:T(4,128)(2,1)S(1)}, bf16[1,1,128,4,128]{4,3,2,...) fusion(bf16[2,1,128,4,128]{4,3,2,1,0:T(4,128)(2,1)} %param.7, s32[]{:T(128)S(6)} %select_n.27, s32[]{:T(128)S(6)} %select_n.26, ...), kind=kLoop, calls=%fused_computation.11 | loop fusion | bytes 1048584 | tf_op jit(solution)/shard_map/jit(dynamic_index_in_dim)/dynamic_slice | solution.py:459
  2.3 3.1 %collective-permute-start = (bf16[4,2,128,128]{3,2,1,0:T(8,128)(2,1)S(1)}, bf16[4,2,128,128]{3,2,1,0:T(8,128)(2,1)S(1)}, u32[]{:S(2)}, u32[]{:S(2)}) collective-permute-start(bf16[4,2,128,128]{3,2,1,0:T(8,128)(2,1)S(1)} %maximum_bitcast_fusion.1.own_b.refs_4_), channel_id=1, source_target_pairs={{0,8},{8,0},{16,24},{24,16},{1,9},{9,1},{17,25},{25,17},{2,10},{10... | collective-permute-start | bytes 786440 | tf_op jit(solution)/shard_map/ppermute | solution.py:384
  5.4 0.0 collective-permute-start.1
  5.4 0.0 copy-start.2
  5.4 0.5 %copy_bitcast_fusion = (bf16[2,16,128,128]{3,2,1,0:T(8,128)(2,1)S(1)}, bf16[2,16,128,128]{3,2,1,0:T(8,128)(2,1)S(1)}) fusion(bf16[2,1,128,16,128]{4,3,2,1,0:T(8,128)(2,1)S(1)} %copy-done, bf16[2,1,128,16,128]{4,3,2,1,0:T(8,128)(2,1)S(1)} %copy-done.1), kind=kLoop, calls=%fused_computation.1 | loop fusion | bytes 4194304 | tf_op jit(solution)/shard_map/transpose | solution.py:464
  6.0 0.1 iota_add_fusion
  6.0 0.9 %collective-permute-done.1 = bf16[4,2,128,128]{3,2,1,0:T(8,128)(2,1)S(1)} collective-permute-done((bf16[4,2,128,128]{3,2,1,0:T(8,128)(2,1)S(1)}, bf16[4,2,128,128]{3,2,1,0:T(8,128)(2,1)S(1)}, u32[]{:S(2)}, u32[]{:S(2)}) %collective-permute-start.1) | collective-permute-done | bytes 262176 | tf_op jit(solution)/shard_map/ppermute | solution.py:383
  7.0 7.7 %collective-permute-start.2 = (bf16[4,2,128,128]{3,2,1,0:T(8,128)(2,1)S(1)}, bf16[4,2,128,128]{3,2,1,0:T(8,128)(2,1)S(1)}, u32[]{:S(2)}, u32[]{:S(2)}) collective-permute-start(bf16[4,2,128,128]{3,2,1,0:T(8,128)(2,1)S(1)} %broadcast_select_fusion.prev_b.refs_6_), channel_id=1, source_target_pairs={{0,8},{8,0},{16,24},{24,16},{1,9},{9,1},{17,25},{25,17},{2,10},{10... | collective-permute-start | bytes 786440 | tf_op jit(solution)/shard_map/ppermute | solution.py:387
  14.7 0.0 collective-permute-done.prev_a.refs_5_
  14.7 0.0 collective-permute-start.3
  14.7 0.4 %select_reduce_fusion = s32[8,128]{1,0:T(8,128)S(1)} fusion(s32[8,128]{1,0:T(8,128)S(1)} %iota_add_fusion, s32[512]{0:T(512)S(1)} %copy-done.2), kind=kLoop, calls=%fused_computation | loop fusion | flops 1571840 | bytes 10240 | tf_op jit(solution)/shard_map/reduce_max | solution.py:445
  15.1 3.0 %near.1 = (f32[2,4,256,512]{3,2,1,0:T(8,128)S(1)}, f32[2,4,256,512]{3,2,1,0:T(8,128)S(1)}, f32[2,4,8,512]{3,2,1,0:T(8,128)S(1)}) custom-call(s32[8,1,128]{2,1,0:T(1,128)S(1)} %bitcast.33, bf16[2,16,128,128]{3,2,1,0:T(8,128)(2,1)S(1)} %get-tuple-element.61.q_ref, bf16[2,16,128,128]{3,2,1,0:T(8,128)(2,1)S(1)} %get-tuple-element.60.do_ref, ...), custom_call_target="tpu_custom_call" | custom-call | flops 2147483648 | bytes 3149824 | tf_op jit(solution)/shard_map/near/pallas_call | solution.py:172
  18.1 0.0 collective-permute-done.3.far_b.refs_8_
  18.1 2.0 %collective-permute-done.2.far_a.refs_7_ = bf16[4,2,128,128]{3,2,1,0:T(8,128)(2,1)S(1)} collective-permute-done((bf16[4,2,128,128]{3,2,1,0:T(8,128)(2,1)S(1)}, bf16[4,2,128,128]{3,2,1,0:T(8,128)(2,1)S(1)}, u32[]{:S(2)}, u32[]{:S(2)}) %collective-permute-start.2) | collective-permute-done | bytes 262176 | tf_op jit(solution)/shard_map/ppermute | solution.py:387
  20.1 2.0 %far.1 = (bf16[4,2,128,128]{3,2,1,0:T(8,128)(2,1)S(1)}, bf16[4,2,128,128]{3,2,1,0:T(8,128)(2,1)S(1)}, bf16[2,4,128,512]{3,2,1,0:T(8,128)(2,1)S(1)}, bf16[2,4,128...) custom-call(s32[8,1,128]{2,1,0:T(1,128)S(1)} %bitcast.34, bf16[2,16,128,128]{3,2,1,0:T(8,128)(2,1)S(1)} %get-tuple-element.61.q_ref, ...), custom_call_target="tpu_custom_call" | custom-call | flops 1073741824 | bytes 3018752 | tf_op jit(solution)/shard_map/far/pallas_call | solution.py:172
  22.1 1.9 %collective-permute-start.4 = (bf16[4,2,128,128]{3,2,1,0:T(8,128)(2,1)S(1)}, bf16[4,2,128,128]{3,2,1,0:T(8,128)(2,1)S(1)}, u32[]{:S(2)}, u32[]{:S(2)}) collective-permute-start(bf16[4,2,128,128]{3,2,1,0:T(8,128)(2,1)S(1)} %get-tuple-element.40), channel_id=1, source_target_pairs={{0,8},{8,0},{16,24},{24,16},{1,9},{9,1},{17,25},{25,17},{2,10},{10... | collective-permute-start | bytes 786440 | tf_op jit(solution)/shard_map/ppermute | solution.py:396
  24.0 3.4 %rest.1 = (f32[4,2,128,128]{3,2,1,0:T(8,128)S(1)}, f32[4,2,128,128]{3,2,1,0:T(8,128)S(1)}, f32[4,2,128,128]{3,2,1,0:T(8,128)S(1)}, f32[4,2,128,128]{3,2,1,0:T(8,...) custom-call(bf16[2,16,128,128]{3,2,1,0:T(8,128)(2,1)S(1)} %get-tuple-element.61.q_ref, ...), custom_call_target="tpu_custom_call" | custom-call | flops 5368709120 | bytes 14286848 | tf_op jit(solution)/shard_map/rest/pallas_call | solution.py:172
  27.4 1.6 %collective-permute-done.4.from_a = bf16[4,2,128,128]{3,2,1,0:T(8,128)(2,1)S(1)} collective-permute-done((bf16[4,2,128,128]{3,2,1,0:T(8,128)(2,1)S(1)}, bf16[4,2,128,128]{3,2,1,0:T(8,128)(2,1)S(1)}, u32[]{:S(2)}, u32[]{:S(2)}) %collective-permute-start.4) | collective-permute-done | bytes 262176 | tf_op jit(solution)/shard_map/ppermute | solution.py:396
  29.0 0.1 merge.1
  29.1 1.8 %collective-permute-start.6 = (bf16[4,2,128,128]{3,2,1,0:T(8,128)(2,1)S(1)}, bf16[4,2,128,128]{3,2,1,0:T(8,128)(2,1)S(1)}, u32[]{:S(2)}, u32[]{:S(2)}) collective-permute-start(bf16[4,2,128,128]{3,2,1,0:T(8,128)(2,1)S(1)} %get-tuple-element.42), channel_id=1, source_target_pairs={{0,8},{8,0},{16,24},{24,16},{1,9},{9,1},{17,25},{25,17},{2,10},{10... | collective-permute-start | bytes 786440 | tf_op jit(solution)/shard_map/ppermute | solution.py:406
  30.9 1.6 %copy.23 = bf16[2,1,128,16,128]{4,3,2,1,0:T(8,128)(2,1)} copy(bf16[2,1,128,16,128]{4,2,3,0,1:T(8,128)(2,1)S(1)} %bitcast.32) | data formatting | bytes 2097152
  32.6 1.6 %copy.24 = bf16[2,1,128,16,128]{4,3,2,1,0:T(8,128)(2,1)} copy(bf16[2,1,128,16,128]{4,2,3,0,1:T(8,128)(2,1)S(1)} %bitcast.31) | data formatting | bytes 2097152
  34.2 2.1 %collective-permute-done.6.last_a = bf16[4,2,128,128]{3,2,1,0:T(8,128)(2,1)S(1)} collective-permute-done((bf16[4,2,128,128]{3,2,1,0:T(8,128)(2,1)S(1)}, bf16[4,2,128,128]{3,2,1,0:T(8,128)(2,1)S(1)}, u32[]{:S(2)}, u32[]{:S(2)}) %collective-permute-start.6) | collective-permute-done | bytes 262176 | tf_op jit(solution)/shard_map/ppermute | solution.py:406
  36.3 1.1 %unpack.1 = (bf16[2,1,128,4,128]{4,3,2,1,0:T(4,128)(2,1)}, bf16[2,1,128,4,128]{4,3,2,1,0:T(4,128)(2,1)}) custom-call(f32[4,2,128,128]{3,2,1,0:T(8,128)S(1)} %get-tuple-element.36.own_a, f32[4,2,128,128]{3,2,1,0:T(8,128)S(1)} %get-tuple-element.37.own_b, bf16[4,2,128,128]{3,2,1,0:T(8,128)(2,1)S(1)} %collective-permute-done.6.last_a, ...), custom_call_target="tpu_custom_call" | custom-call | flops 8192 | bytes 1835008 | tf_op jit(solution)/shard_map/unpack/pallas_call | solution.py:172
  (19 shorter events, 0.2 us)
Async XLA Ops:
  0.6 4.8 %copy-start = (bf16[2,1,128,16,128]{4,3,2,1,0:T(8,128)(2,1)S(1)}, bf16[2,1,128,16,128]{4,3,2,1,0:T(8,128)(2,1)}, u32[]{:S(2)}) copy-start(bf16[2,1,128,16,128]{4,3,2,1,0:T(8,128)(2,1)} %param.8) | copy-start | bytes 3145732
  0.6 4.8 %copy-start.1 = (bf16[2,1,128,16,128]{4,3,2,1,0:T(8,128)(2,1)S(1)}, bf16[2,1,128,16,128]{4,3,2,1,0:T(8,128)(2,1)}, u32[]{:S(2)}) copy-start(bf16[2,1,128,16,128]{4,3,2,1,0:T(8,128)(2,1)} %param.5) | copy-start | bytes 3145732
  2.3 12.4 %collective-permute-start = (bf16[4,2,128,128]{3,2,1,0:T(8,128)(2,1)S(1)}, bf16[4,2,128,128]{3,2,1,0:T(8,128)(2,1)S(1)}, u32[]{:S(2)}, u32[]{:S(2)}) collective-permute-start(bf16[4,2,128,128]{3,2,1,0:T(8,128)(2,1)S(1)} %maximum_bitcast_fusion.1.own_b.refs_4_), channel_id=1, source_target_pairs={{0,8},{8,0},{16,24},{24,16},{1,9},{9,1},{17,25},{25,17},{2,10},{10... | collective-permute-start | bytes 786440 | tf_op jit(solution)/shard_map/ppermute | solution.py:384
  5.4 1.5 %collective-permute-start.1 = (bf16[4,2,128,128]{3,2,1,0:T(8,128)(2,1)S(1)}, bf16[4,2,128,128]{3,2,1,0:T(8,128)(2,1)S(1)}, u32[]{:S(2)}, u32[]{:S(2)}) collective-permute-start(bf16[4,2,128,128]{3,2,1,0:T(8,128)(2,1)S(1)} %maximum_bitcast_fusion.own_a.refs_3_), channel_id=1, source_target_pairs={{8,16},{16,8},{0,1},{24,25},{9,17},{17,9},{1,0},{25,24},{10,18},{1... | collective-permute-start | bytes 786440 | tf_op jit(solution)/shard_map/ppermute | solution.py:383
  5.4 9.3 %copy-start.2 = (s32[512]{0:T(512)S(1)}, s32[512]{0:T(512)}, u32[]{:S(2)}) copy-start(s32[512]{0:T(512)} %param.9) | copy-start | bytes 6148
  7.0 13.1 %collective-permute-start.2 = (bf16[4,2,128,128]{3,2,1,0:T(8,128)(2,1)S(1)}, bf16[4,2,128,128]{3,2,1,0:T(8,128)(2,1)S(1)}, u32[]{:S(2)}, u32[]{:S(2)}) collective-permute-start(bf16[4,2,128,128]{3,2,1,0:T(8,128)(2,1)S(1)} %broadcast_select_fusion.prev_b.refs_6_), channel_id=1, source_target_pairs={{0,8},{8,0},{16,24},{24,16},{1,9},{9,1},{17,25},{25,17},{2,10},{10... | collective-permute-start | bytes 786440 | tf_op jit(solution)/shard_map/ppermute | solution.py:387
  14.7 3.4 %collective-permute-start.3 = (bf16[4,2,128,128]{3,2,1,0:T(8,128)(2,1)S(1)}, bf16[4,2,128,128]{3,2,1,0:T(8,128)(2,1)S(1)}, u32[]{:S(2)}, u32[]{:S(2)}) collective-permute-start(bf16[4,2,128,128]{3,2,1,0:T(8,128)(2,1)S(1)} %collective-permute-done.prev_a.refs_5_), channel_id=1, source_target_pairs={{8,16},{16,8},{0,1},{24,25},{9,17},{17,9},{1,0},{25,24},{10,18},{1... | collective-permute-start | bytes 786440 | tf_op jit(solution)/shard_map/ppermute | solution.py:386
  22.1 6.8 %collective-permute-start.4 = (bf16[4,2,128,128]{3,2,1,0:T(8,128)(2,1)S(1)}, bf16[4,2,128,128]{3,2,1,0:T(8,128)(2,1)S(1)}, u32[]{:S(2)}, u32[]{:S(2)}) collective-permute-start(bf16[4,2,128,128]{3,2,1,0:T(8,128)(2,1)S(1)} %get-tuple-element.40), channel_id=1, source_target_pairs={{0,8},{8,0},{16,24},{24,16},{1,9},{9,1},{17,25},{25,17},{2,10},{10... | collective-permute-start | bytes 786440 | tf_op jit(solution)/shard_map/ppermute | solution.py:396
  24.0 4.9 %collective-permute-start.5 = (bf16[4,2,128,128]{3,2,1,0:T(8,128)(2,1)S(1)}, bf16[4,2,128,128]{3,2,1,0:T(8,128)(2,1)S(1)}, u32[]{:S(2)}, u32[]{:S(2)}) collective-permute-start(bf16[4,2,128,128]{3,2,1,0:T(8,128)(2,1)S(1)} %get-tuple-element.41.deep_b), channel_id=1, source_target_pairs={{8,16},{16,8},{0,1},{24,25},{9,17},{17,9},{1,0},{25,24},{10,18},{1... | collective-permute-start | bytes 786440 | tf_op jit(solution)/shard_map/ppermute | solution.py:397
  29.1 7.2 %collective-permute-start.6 = (bf16[4,2,128,128]{3,2,1,0:T(8,128)(2,1)S(1)}, bf16[4,2,128,128]{3,2,1,0:T(8,128)(2,1)S(1)}, u32[]{:S(2)}, u32[]{:S(2)}) collective-permute-start(bf16[4,2,128,128]{3,2,1,0:T(8,128)(2,1)S(1)} %get-tuple-element.42), channel_id=1, source_target_pairs={{0,8},{8,0},{16,24},{24,16},{1,9},{9,1},{17,25},{25,17},{2,10},{10... | collective-permute-start | bytes 786440 | tf_op jit(solution)/shard_map/ppermute | solution.py:406
  30.9 5.4 %collective-permute-start.7 = (bf16[4,2,128,128]{3,2,1,0:T(8,128)(2,1)S(1)}, bf16[4,2,128,128]{3,2,1,0:T(8,128)(2,1)S(1)}, u32[]{:S(2)}, u32[]{:S(2)}) collective-permute-start(bf16[4,2,128,128]{3,2,1,0:T(8,128)(2,1)S(1)} %get-tuple-element.43.next_b), channel_id=1, source_target_pairs={{8,16},{16,8},{0,1},{24,25},{9,17},{17,9},{1,0},{25,24},{10,18},{1... | collective-permute-start | bytes 786440 | tf_op jit(solution)/shard_map/ppermute | solution.py:407

commit v9 on v7

--- a/solution.py
+++ b/solution.py
@@ -376,7 +376,7 @@
     b1 = lax.ppermute(own_a, both_axes, swaps_b)
     a1 = lax.ppermute(own_b, "seq", pairs_a)
     b1 = jnp.where(is_last, own_a, b1)
-    b2 = lax.ppermute(a1, both_axes, swaps_b)
+    b2 = lax.ppermute(lax.optimization_barrier((a1, own_b))[0], both_axes, swaps_b)
     a2 = lax.ppermute(b1, "seq", pairs_a)
     e, dp, stats = vmem_call(
         functools.partial(near_kernel, scale, count), near, 4 * block, "near",

time: 37.5 us -> 37.2 us (level)
  waiting for transfers between devices: 6.42 us -> 5.21 us
  starting transfers between devices: 14.6 us -> 15.5 us
    ppermute x1, starting transfers between devices: 7.7 us -> 5.89 us  [two_span_window(): a2 = lax.ppermute(b1, 'seq', pairs_a)]
    ppermute x1, starting transfers between devices: 3.09 us -> 4.15 us  [two_span_window(): a1 = lax.ppermute(own_b, 'seq', pairs_a)]
    ppermute x1, waiting for transfers between devices: 0.88 us -> 0.01 us  [two_span_window(): b1 = lax.ppermute(own_a, both_axes, swaps_b)]
    ppermute x1, starting transfers between devices: 1.89 us -> 2.68 us  [two_span_window(): from_a = lax.ppermute(deep_a, 'seq', pairs_a)]
    ppermute x1, waiting for transfers between devices: 1.55 us -> 0.98 us  [two_span_window(): from_a = lax.ppermute(deep_a, 'seq', pairs_a)]
    ppermute x1, starting transfers between devices: 0.01 us -> 0.52 us  [two_span_window(): b1 = lax.ppermute(own_a, both_axes, swaps_b)]
  transfers between devices with their start and end apart: 8 -> 8, of which waited for: 4 -> 3; matrix products, arithmetic and copies ran while one was open for 12% -> 12% of each run, Pallas kernels for 17% -> 17%
where the time goes in v9:
time: 37.2 us; the launch traced here: 37.1 us
  starting transfers between devices  15.5 us (42%)
  Pallas kernels  9.46 us (25%)
  local copies, waits for them, and re-layouts  5.36 us (14%)
  waiting for transfers between devices  5.21 us (14%)
  between operations  0.8 us (2%)
  other arithmetic  0.76 us (2%)
    pallas_call x4, Pallas kernels, vmem_call(): pl.pallas_call(kernel, in_specs=[whole] * len(args), out_specs=[whole] *...  9.46 us
    ppermute x1, starting transfers between devices, two_span_window(): a2 = lax.ppermute(b1, 'seq', pairs_a)  5.89 us
    ppermute x1, starting transfers between devices, two_span_window(): a1 = lax.ppermute(own_b, 'seq', pairs_a)  4.15 us
    unnamed x8, local copies, waits for them, and re-layouts  3.31 us
    ppermute x1, starting transfers between devices, two_span_window(): from_a = lax.ppermute(deep_a, 'seq', pairs_a)  2.68 us
    ppermute x1, waiting for transfers between devices, two_span_window(): last_a = lax.ppermute(next_a, 'seq', pairs_a)  2.22 us
    ppermute x1, starting transfers between devices, two_span_window(): last_a = lax.ppermute(next_a, 'seq', pairs_a)  2.16 us
    ppermute x1, waiting for transfers between devices, two_span_window(): a2 = lax.ppermute(b1, 'seq', pairs_a)  2 us
  transfers between devices with their start and end apart: 8, of which 3 were waited for; matrix products, arithmetic and copies ran while one was open for 12% of the time, Pallas kernels for 17%

profile of v9, /device:TPU:0, one launch (start us, length us, event | category | flops | bytes accessed | tf_op | source)
XLA Modules:
  0.0 37.1 jit_solution(5657961119326960112)
XLA Ops:
  0.7 1.4 %constant_dynamic-slice_fusion = (bf16[1,1,128,4,128]{4,3,2,1,0:T(4,128)(2,1)S(1)}, bf16[1,1,128,4,128]{4,3,2,1,0:T(4,128)(2,1)S(1)}, bf16[1,1,128,4,128]{4,3,2,...) fusion(bf16[2,1,128,4,128]{4,3,2,1,0:T(4,128)(2,1)} %param.7, s32[]{:T(128)S(6)} %select_n.30, s32[]{:T(128)S(6)} %select_n.29, ...), kind=kLoop, calls=%fused_computation.13 | loop fusion | bytes 1048584 | tf_op jit(solution)/shard_map/jit(dynamic_index_in_dim)/dynamic_slice | solution.py:452
  2.3 0.5 %collective-permute-start.1 = (bf16[4,2,128,128]{3,2,1,0:T(8,128)(2,1)S(1)}, bf16[4,2,128,128]{3,2,1,0:T(8,128)(2,1)S(1)}, u32[]{:S(2)}, u32[]{:S(2)}) collective-permute-start(bf16[4,2,128,128]{3,2,1,0:T(8,128)(2,1)S(1)} %maximum_bitcast_fusion.own_a.refs_3_), channel_id=1, source_target_pairs={{8,16},{16,8},{0,1},{24,25},{9,17},{17,9},{1,0},{25,24},{10,18},{1... | collective-permute-start | bytes 786440 | tf_op jit(solution)/shard_map/ppermute | solution.py:376
  2.8 4.1 %collective-permute-start = (bf16[4,2,128,128]{3,2,1,0:T(8,128)(2,1)S(1)}, bf16[4,2,128,128]{3,2,1,0:T(8,128)(2,1)S(1)}, u32[]{:S(2)}, u32[]{:S(2)}) collective-permute-start(bf16[4,2,128,128]{3,2,1,0:T(8,128)(2,1)S(1)} %maximum_bitcast_fusion.1.own_b.refs_4_), channel_id=1, source_target_pairs={{0,8},{8,0},{16,24},{24,16},{1,9},{9,1},{17,25},{25,17},{2,10},{10... | collective-permute-start | bytes 786440 | tf_op jit(solution)/shard_map/ppermute | solution.py:377
  7.0 0.5 %copy_bitcast_fusion = (bf16[2,16,128,128]{3,2,1,0:T(8,128)(2,1)S(1)}, bf16[2,16,128,128]{3,2,1,0:T(8,128)(2,1)S(1)}) fusion(bf16[2,1,128,16,128]{4,3,2,1,0:T(8,128)(2,1)S(1)} %copy-done, bf16[2,1,128,16,128]{4,3,2,1,0:T(8,128)(2,1)S(1)} %copy-done.1), kind=kLoop, calls=%fused_computation.1 | loop fusion | bytes 4194304 | tf_op jit(solution)/shard_map/transpose | solution.py:457
  7.5 0.1 iota_add_fusion
  7.6 0.0 collective-permute-done.1
  7.6 5.9 %collective-permute-start.2 = (bf16[4,2,128,128]{3,2,1,0:T(8,128)(2,1)S(1)}, bf16[4,2,128,128]{3,2,1,0:T(8,128)(2,1)S(1)}, u32[]{:S(2)}, u32[]{:S(2)}) collective-permute-start(bf16[4,2,128,128]{3,2,1,0:T(8,128)(2,1)S(1)} %broadcast_select_fusion.prev_b.refs_6_), channel_id=1, source_target_pairs={{0,8},{8,0},{16,24},{24,16},{1,9},{9,1},{17,25},{25,17},{2,10},{10... | collective-permute-start | bytes 786440 | tf_op jit(solution)/shard_map/ppermute | solution.py:380
  13.5 0.0 collective-permute-done.prev_a.refs_5_
  13.5 0.0 collective-permute-start.3
  13.5 0.4 %select_reduce_fusion = s32[8,128]{1,0:T(8,128)S(1)} fusion(s32[8,128]{1,0:T(8,128)S(1)} %iota_add_fusion, s32[512]{0:T(512)S(1)} %copy-done.2), kind=kLoop, calls=%fused_computation | loop fusion | flops 1571840 | bytes 10240 | tf_op jit(solution)/shard_map/reduce_max | solution.py:438
  14.0 3.0 %near.1 = (f32[2,4,256,512]{3,2,1,0:T(8,128)S(1)}, f32[2,4,256,512]{3,2,1,0:T(8,128)S(1)}, f32[2,4,8,512]{3,2,1,0:T(8,128)S(1)}) custom-call(s32[8,1,128]{2,1,0:T(1,128)S(1)} %bitcast.33, bf16[2,16,128,128]{3,2,1,0:T(8,128)(2,1)S(1)} %get-tuple-element.63.q_ref, bf16[2,16,128,128]{3,2,1,0:T(8,128)(2,1)S(1)} %get-tuple-element.62.do_ref, ...), custom_call_target="tpu_custom_call" | custom-call | flops 2147483648 | bytes 3149824 | tf_op jit(solution)/shard_map/near/pallas_call | solution.py:172
  17.0 2.0 %collective-permute-done.2.far_a.refs_7_ = bf16[4,2,128,128]{3,2,1,0:T(8,128)(2,1)S(1)} collective-permute-done((bf16[4,2,128,128]{3,2,1,0:T(8,128)(2,1)S(1)}, bf16[4,2,128,128]{3,2,1,0:T(8,128)(2,1)S(1)}, u32[]{:S(2)}, u32[]{:S(2)}) %collective-permute-start.2) | collective-permute-done | bytes 262176 | tf_op jit(solution)/shard_map/ppermute | solution.py:380
  19.0 2.0 %far.1 = (bf16[4,2,128,128]{3,2,1,0:T(8,128)(2,1)S(1)}, bf16[4,2,128,128]{3,2,1,0:T(8,128)(2,1)S(1)}, bf16[2,4,128,512]{3,2,1,0:T(8,128)(2,1)S(1)}, bf16[2,4,128...) custom-call(s32[8,1,128]{2,1,0:T(1,128)S(1)} %bitcast.34, bf16[2,16,128,128]{3,2,1,0:T(8,128)(2,1)S(1)} %get-tuple-element.63.q_ref, ...), custom_call_target="tpu_custom_call" | custom-call | flops 1073741824 | bytes 3018752 | tf_op jit(solution)/shard_map/far/pallas_call | solution.py:172
  21.0 2.7 %collective-permute-start.4 = (bf16[4,2,128,128]{3,2,1,0:T(8,128)(2,1)S(1)}, bf16[4,2,128,128]{3,2,1,0:T(8,128)(2,1)S(1)}, u32[]{:S(2)}, u32[]{:S(2)}) collective-permute-start(bf16[4,2,128,128]{3,2,1,0:T(8,128)(2,1)S(1)} %get-tuple-element.42), channel_id=1, source_target_pairs={{0,8},{8,0},{16,24},{24,16},{1,9},{9,1},{17,25},{25,17},{2,10},{10... | collective-permute-start | bytes 786440 | tf_op jit(solution)/shard_map/ppermute | solution.py:389
  23.7 3.4 %rest.1 = (f32[4,2,128,128]{3,2,1,0:T(8,128)S(1)}, f32[4,2,128,128]{3,2,1,0:T(8,128)S(1)}, f32[4,2,128,128]{3,2,1,0:T(8,128)S(1)}, f32[4,2,128,128]{3,2,1,0:T(8,...) custom-call(bf16[2,16,128,128]{3,2,1,0:T(8,128)(2,1)S(1)} %get-tuple-element.63.q_ref, ...), custom_call_target="tpu_custom_call" | custom-call | flops 5368709120 | bytes 14286848 | tf_op jit(solution)/shard_map/rest/pallas_call | solution.py:172
  27.1 1.0 %collective-permute-done.4 = bf16[4,2,128,128]{3,2,1,0:T(8,128)(2,1)S(1)} collective-permute-done((bf16[4,2,128,128]{3,2,1,0:T(8,128)(2,1)S(1)}, bf16[4,2,128,128]{3,2,1,0:T(8,128)(2,1)S(1)}, u32[]{:S(2)}, u32[]{:S(2)}) %collective-permute-start.4) | collective-permute-done | bytes 262176 | tf_op jit(solution)/shard_map/ppermute | solution.py:389
  28.1 0.1 add_convert_fusion.1
  28.2 2.2 %collective-permute-start.6 = (bf16[4,2,128,128]{3,2,1,0:T(8,128)(2,1)S(1)}, bf16[4,2,128,128]{3,2,1,0:T(8,128)(2,1)S(1)}, u32[]{:S(2)}, u32[]{:S(2)}) collective-permute-start(bf16[4,2,128,128]{3,2,1,0:T(8,128)(2,1)S(1)} %add_convert_fusion.1), channel_id=1, source_target_pairs={{0,8},{8,0},{16,24},{24,16},{1,9},{9,1},{17,25},{25,17},{2,10},{10... | collective-permute-start | bytes 786440 | tf_op jit(solution)/shard_map/ppermute | solution.py:399
  30.3 0.1 add_convert_fusion.next_b
  30.4 0.1 collective-permute-start.7
  30.5 1.6 %copy.23 = bf16[2,1,128,16,128]{4,3,2,1,0:T(8,128)(2,1)} copy(bf16[2,1,128,16,128]{4,2,3,0,1:T(8,128)(2,1)S(1)} %bitcast.32) | data formatting | bytes 2097152
  32.1 1.6 %copy.24 = bf16[2,1,128,16,128]{4,3,2,1,0:T(8,128)(2,1)} copy(bf16[2,1,128,16,128]{4,2,3,0,1:T(8,128)(2,1)S(1)} %bitcast.31) | data formatting | bytes 2097152
  33.8 2.2 %collective-permute-done.6.last_a = bf16[4,2,128,128]{3,2,1,0:T(8,128)(2,1)S(1)} collective-permute-done((bf16[4,2,128,128]{3,2,1,0:T(8,128)(2,1)S(1)}, bf16[4,2,128,128]{3,2,1,0:T(8,128)(2,1)S(1)}, u32[]{:S(2)}, u32[]{:S(2)}) %collective-permute-start.6) | collective-permute-done | bytes 262176 | tf_op jit(solution)/shard_map/ppermute | solution.py:399
  36.0 1.1 %unpack.1 = (bf16[2,1,128,4,128]{4,3,2,1,0:T(4,128)(2,1)}, bf16[2,1,128,4,128]{4,3,2,1,0:T(4,128)(2,1)}) custom-call(f32[4,2,128,128]{3,2,1,0:T(8,128)S(1)} %get-tuple-element.38.own_a, f32[4,2,128,128]{3,2,1,0:T(8,128)S(1)} %get-tuple-element.39.own_b, bf16[4,2,128,128]{3,2,1,0:T(8,128)(2,1)S(1)} %collective-permute-done.6.last_a, ...), custom_call_target="tpu_custom_call" | custom-call | flops 8192 | bytes 1835008 | tf_op jit(solution)/shard_map/unpack/pallas_call | solution.py:172
  (20 shorter events, 0.2 us)
Async XLA Ops:
  0.6 6.3 %copy-start = (bf16[2,1,128,16,128]{4,3,2,1,0:T(8,128)(2,1)S(1)}, bf16[2,1,128,16,128]{4,3,2,1,0:T(8,128)(2,1)}, u32[]{:S(2)}) copy-start(bf16[2,1,128,16,128]{4,3,2,1,0:T(8,128)(2,1)} %param.8) | copy-start | bytes 3145732
  0.6 6.3 %copy-start.1 = (bf16[2,1,128,16,128]{4,3,2,1,0:T(8,128)(2,1)S(1)}, bf16[2,1,128,16,128]{4,3,2,1,0:T(8,128)(2,1)}, u32[]{:S(2)}) copy-start(bf16[2,1,128,16,128]{4,3,2,1,0:T(8,128)(2,1)} %param.5) | copy-start | bytes 3145732
  2.3 5.3 %collective-permute-start.1 = (bf16[4,2,128,128]{3,2,1,0:T(8,128)(2,1)S(1)}, bf16[4,2,128,128]{3,2,1,0:T(8,128)(2,1)S(1)}, u32[]{:S(2)}, u32[]{:S(2)}) collective-permute-start(bf16[4,2,128,128]{3,2,1,0:T(8,128)(2,1)S(1)} %maximum_bitcast_fusion.own_a.refs_3_), channel_id=1, source_target_pairs={{8,16},{16,8},{0,1},{24,25},{9,17},{17,9},{1,0},{25,24},{10,18},{1... | collective-permute-start | bytes 786440 | tf_op jit(solution)/shard_map/ppermute | solution.py:376
  2.8 10.7 %collective-permute-start = (bf16[4,2,128,128]{3,2,1,0:T(8,128)(2,1)S(1)}, bf16[4,2,128,128]{3,2,1,0:T(8,128)(2,1)S(1)}, u32[]{:S(2)}, u32[]{:S(2)}) collective-permute-start(bf16[4,2,128,128]{3,2,1,0:T(8,128)(2,1)S(1)} %maximum_bitcast_fusion.1.own_b.refs_4_), channel_id=1, source_target_pairs={{0,8},{8,0},{16,24},{24,16},{1,9},{9,1},{17,25},{25,17},{2,10},{10... | collective-permute-start | bytes 786440 | tf_op jit(solution)/shard_map/ppermute | solution.py:377
  7.0 6.6 %copy-start.2 = (s32[512]{0:T(512)S(1)}, s32[512]{0:T(512)}, u32[]{:S(2)}) copy-start(s32[512]{0:T(512)} %param.9) | copy-start | bytes 6148
  7.6 11.3 %collective-permute-start.2 = (bf16[4,2,128,128]{3,2,1,0:T(8,128)(2,1)S(1)}, bf16[4,2,128,128]{3,2,1,0:T(8,128)(2,1)S(1)}, u32[]{:S(2)}, u32[]{:S(2)}) collective-permute-start(bf16[4,2,128,128]{3,2,1,0:T(8,128)(2,1)S(1)} %broadcast_select_fusion.prev_b.refs_6_), channel_id=1, source_target_pairs={{0,8},{8,0},{16,24},{24,16},{1,9},{9,1},{17,25},{25,17},{2,10},{10... | collective-permute-start | bytes 786440 | tf_op jit(solution)/shard_map/ppermute | solution.py:380
  13.5 5.4 %collective-permute-start.3 = (bf16[4,2,128,128]{3,2,1,0:T(8,128)(2,1)S(1)}, bf16[4,2,128,128]{3,2,1,0:T(8,128)(2,1)S(1)}, u32[]{:S(2)}, u32[]{:S(2)}) collective-permute-start(bf16[4,2,128,128]{3,2,1,0:T(8,128)(2,1)S(1)} %collective-permute-done.prev_a.refs_5_), channel_id=1, source_target_pairs={{8,16},{16,8},{0,1},{24,25},{9,17},{17,9},{1,0},{25,24},{10,18},{1... | collective-permute-start | bytes 786440 | tf_op jit(solution)/shard_map/ppermute | solution.py:379
  21.0 7.0 %collective-permute-start.4 = (bf16[4,2,128,128]{3,2,1,0:T(8,128)(2,1)S(1)}, bf16[4,2,128,128]{3,2,1,0:T(8,128)(2,1)S(1)}, u32[]{:S(2)}, u32[]{:S(2)}) collective-permute-start(bf16[4,2,128,128]{3,2,1,0:T(8,128)(2,1)S(1)} %get-tuple-element.42), channel_id=1, source_target_pairs={{0,8},{8,0},{16,24},{24,16},{1,9},{9,1},{17,25},{25,17},{2,10},{10... | collective-permute-start | bytes 786440 | tf_op jit(solution)/shard_map/ppermute | solution.py:389
  23.7 4.4 %collective-permute-start.5 = (bf16[4,2,128,128]{3,2,1,0:T(8,128)(2,1)S(1)}, bf16[4,2,128,128]{3,2,1,0:T(8,128)(2,1)S(1)}, u32[]{:S(2)}, u32[]{:S(2)}) collective-permute-start(bf16[4,2,128,128]{3,2,1,0:T(8,128)(2,1)S(1)} %get-tuple-element.41), channel_id=1, source_target_pairs={{8,16},{16,8},{0,1},{24,25},{9,17},{17,9},{1,0},{25,24},{10,18},{1... | collective-permute-start | bytes 786440 | tf_op jit(solution)/shard_map/ppermute | solution.py:390
  28.2 7.8 %collective-permute-start.6 = (bf16[4,2,128,128]{3,2,1,0:T(8,128)(2,1)S(1)}, bf16[4,2,128,128]{3,2,1,0:T(8,128)(2,1)S(1)}, u32[]{:S(2)}, u32[]{:S(2)}) collective-permute-start(bf16[4,2,128,128]{3,2,1,0:T(8,128)(2,1)S(1)} %add_convert_fusion.1), channel_id=1, source_target_pairs={{0,8},{8,0},{16,24},{24,16},{1,9},{9,1},{17,25},{25,17},{2,10},{10... | collective-permute-start | bytes 786440 | tf_op jit(solution)/shard_map/ppermute | solution.py:399
  30.4 5.6 %collective-permute-start.7 = (bf16[4,2,128,128]{3,2,1,0:T(8,128)(2,1)S(1)}, bf16[4,2,128,128]{3,2,1,0:T(8,128)(2,1)S(1)}, u32[]{:S(2)}, u32[]{:S(2)}) collective-permute-start(bf16[4,2,128,128]{3,2,1,0:T(8,128)(2,1)S(1)} %add_convert_fusion.next_b), channel_id=1, source_target_pairs={{8,16},{16,8},{0,1},{24,25},{9,17},{17,9},{1,0},{25,24},{10,18},{1... | collective-permute-start | bytes 786440 | tf_op jit(solution)/shard_map/ppermute | solution.py:400

commit v10 on v8

--- a/solution.py
+++ b/solution.py
@@ -383,7 +383,7 @@
     b1 = lax.ppermute(own_a, both_axes, swaps_b)
     a1 = lax.ppermute(own_b, "seq", pairs_a)
     b1 = jnp.where(is_last, own_a, b1)
-    b2 = lax.ppermute(a1, both_axes, swaps_b)
+    b2 = lax.ppermute(lax.optimization_barrier((a1, own_b))[0], both_axes, swaps_b)
     a2 = lax.ppermute(b1, "seq", pairs_a)
     e, dp, stats = vmem_call(
         functools.partial(near_kernel, scale, count), near, 4 * block, "near",

time: 37.5 us -> 37.2 us (level)
  waiting for transfers between devices: 6.57 us -> 5.36 us
  starting transfers between devices: 14.5 us -> 15.4 us
    ppermute x1, starting transfers between devices: 7.7 us -> 5.89 us  [two_span_window(): a2 = lax.ppermute(b1, 'seq', pairs_a)]
    ppermute x1, starting transfers between devices: 3.09 us -> 4.15 us  [two_span_window(): a1 = lax.ppermute(own_b, 'seq', pairs_a)]
    ppermute x1, waiting for transfers between devices: 0.88 us -> 0.01 us  [two_span_window(): b1 = lax.ppermute(own_a, both_axes, swaps_b)]
    ppermute x1, starting transfers between devices: 1.89 us -> 2.69 us  [two_span_window(): from_a = lax.ppermute(deep_a, 'seq', pairs_a)]
    ppermute x1, waiting for transfers between devices: 1.57 us -> 0.99 us  [two_span_window(): from_a = lax.ppermute(deep_a, 'seq', pairs_a)]
    ppermute x1, starting transfers between devices: 0.01 us -> 0.52 us  [two_span_window(): b1 = lax.ppermute(own_a, both_axes, swaps_b)]
  transfers between devices with their start and end apart: 8 -> 8, of which waited for: 4 -> 3; matrix products, arithmetic and copies ran while one was open for 12% -> 12% of each run, Pallas kernels for 17% -> 17%
where the time goes in v10:
time: 37.2 us; the launch traced here: 37.1 us
  starting transfers between devices  15.4 us (41%)
  Pallas kernels  9.56 us (26%)
  local copies, waits for them, and re-layouts  5.36 us (14%)
  waiting for transfers between devices  5.36 us (14%)
  between operations  0.8 us (2%)
  other arithmetic  0.59 us (2%)
    pallas_call x5, Pallas kernels, vmem_call(): pl.pallas_call(kernel, in_specs=[whole] * len(args), out_specs=[whole] *...  9.56 us
    ppermute x1, starting transfers between devices, two_span_window(): a2 = lax.ppermute(b1, 'seq', pairs_a)  5.89 us
    ppermute x1, starting transfers between devices, two_span_window(): a1 = lax.ppermute(own_b, 'seq', pairs_a)  4.15 us
    unnamed x8, local copies, waits for them, and re-layouts  3.31 us
    ppermute x1, starting transfers between devices, two_span_window(): from_a = lax.ppermute(deep_a, 'seq', pairs_a)  2.69 us
    ppermute x1, waiting for transfers between devices, two_span_window(): last_a = lax.ppermute(next_a, 'seq', pairs_a)  2.35 us
    ppermute x1, starting transfers between devices, two_span_window(): last_a = lax.ppermute(next_a, 'seq', pairs_a)  2.16 us
    ppermute x1, waiting for transfers between devices, two_span_window(): a2 = lax.ppermute(b1, 'seq', pairs_a)  2 us
  transfers between devices with their start and end apart: 8, of which 3 were waited for; matrix products, arithmetic and copies ran while one was open for 12% of the time, Pallas kernels for 17%

profile of v10, /device:TPU:0, one launch (start us, length us, event | category | flops | bytes accessed | tf_op | source)
XLA Modules:
  0.0 37.1 jit_solution(5545201850906174035)
XLA Ops:
  0.7 1.4 %constant_dynamic-slice_fusion = (bf16[1,1,128,4,128]{4,3,2,1,0:T(4,128)(2,1)S(1)}, bf16[1,1,128,4,128]{4,3,2,1,0:T(4,128)(2,1)S(1)}, bf16[1,1,128,4,128]{4,3,2,...) fusion(bf16[2,1,128,4,128]{4,3,2,1,0:T(4,128)(2,1)} %param.7, s32[]{:T(128)S(6)} %select_n.27, s32[]{:T(128)S(6)} %select_n.26, ...), kind=kLoop, calls=%fused_computation.11 | loop fusion | bytes 1048584 | tf_op jit(solution)/shard_map/jit(dynamic_index_in_dim)/dynamic_slice | solution.py:459
  2.3 0.5 %collective-permute-start.1 = (bf16[4,2,128,128]{3,2,1,0:T(8,128)(2,1)S(1)}, bf16[4,2,128,128]{3,2,1,0:T(8,128)(2,1)S(1)}, u32[]{:S(2)}, u32[]{:S(2)}) collective-permute-start(bf16[4,2,128,128]{3,2,1,0:T(8,128)(2,1)S(1)} %maximum_bitcast_fusion.own_a.refs_3_), channel_id=1, source_target_pairs={{8,16},{16,8},{0,1},{24,25},{9,17},{17,9},{1,0},{25,24},{10,18},{1... | collective-permute-start | bytes 786440 | tf_op jit(solution)/shard_map/ppermute | solution.py:383
  2.8 4.1 %collective-permute-start = (bf16[4,2,128,128]{3,2,1,0:T(8,128)(2,1)S(1)}, bf16[4,2,128,128]{3,2,1,0:T(8,128)(2,1)S(1)}, u32[]{:S(2)}, u32[]{:S(2)}) collective-permute-start(bf16[4,2,128,128]{3,2,1,0:T(8,128)(2,1)S(1)} %maximum_bitcast_fusion.1.own_b.refs_4_), channel_id=1, source_target_pairs={{0,8},{8,0},{16,24},{24,16},{1,9},{9,1},{17,25},{25,17},{2,10},{10... | collective-permute-start | bytes 786440 | tf_op jit(solution)/shard_map/ppermute | solution.py:384
  7.0 0.5 %copy_bitcast_fusion = (bf16[2,16,128,128]{3,2,1,0:T(8,128)(2,1)S(1)}, bf16[2,16,128,128]{3,2,1,0:T(8,128)(2,1)S(1)}) fusion(bf16[2,1,128,16,128]{4,3,2,1,0:T(8,128)(2,1)S(1)} %copy-done, bf16[2,1,128,16,128]{4,3,2,1,0:T(8,128)(2,1)S(1)} %copy-done.1), kind=kLoop, calls=%fused_computation.1 | loop fusion | bytes 4194304 | tf_op jit(solution)/shard_map/transpose | solution.py:464
  7.5 0.1 iota_add_fusion
  7.6 0.0 collective-permute-done.1
  7.6 5.9 %collective-permute-start.2 = (bf16[4,2,128,128]{3,2,1,0:T(8,128)(2,1)S(1)}, bf16[4,2,128,128]{3,2,1,0:T(8,128)(2,1)S(1)}, u32[]{:S(2)}, u32[]{:S(2)}) collective-permute-start(bf16[4,2,128,128]{3,2,1,0:T(8,128)(2,1)S(1)} %broadcast_select_fusion.prev_b.refs_6_), channel_id=1, source_target_pairs={{0,8},{8,0},{16,24},{24,16},{1,9},{9,1},{17,25},{25,17},{2,10},{10... | collective-permute-start | bytes 786440 | tf_op jit(solution)/shard_map/ppermute | solution.py:387
  13.5 0.0 collective-permute-done.prev_a.refs_5_
  13.5 0.0 collective-permute-start.3
  13.5 0.4 %select_reduce_fusion = s32[8,128]{1,0:T(8,128)S(1)} fusion(s32[8,128]{1,0:T(8,128)S(1)} %iota_add_fusion, s32[512]{0:T(512)S(1)} %copy-done.2), kind=kLoop, calls=%fused_computation | loop fusion | flops 1571840 | bytes 10240 | tf_op jit(solution)/shard_map/reduce_max | solution.py:445
  14.0 3.0 %near.1 = (f32[2,4,256,512]{3,2,1,0:T(8,128)S(1)}, f32[2,4,256,512]{3,2,1,0:T(8,128)S(1)}, f32[2,4,8,512]{3,2,1,0:T(8,128)S(1)}) custom-call(s32[8,1,128]{2,1,0:T(1,128)S(1)} %bitcast.33, bf16[2,16,128,128]{3,2,1,0:T(8,128)(2,1)S(1)} %get-tuple-element.63.q_ref, bf16[2,16,128,128]{3,2,1,0:T(8,128)(2,1)S(1)} %get-tuple-element.62.do_ref, ...), custom_call_target="tpu_custom_call" | custom-call | flops 2147483648 | bytes 3149824 | tf_op jit(solution)/shard_map/near/pallas_call | solution.py:172
  17.0 2.0 %collective-permute-done.2.far_a.refs_7_ = bf16[4,2,128,128]{3,2,1,0:T(8,128)(2,1)S(1)} collective-permute-done((bf16[4,2,128,128]{3,2,1,0:T(8,128)(2,1)S(1)}, bf16[4,2,128,128]{3,2,1,0:T(8,128)(2,1)S(1)}, u32[]{:S(2)}, u32[]{:S(2)}) %collective-permute-start.2) | collective-permute-done | bytes 262176 | tf_op jit(solution)/shard_map/ppermute | solution.py:387
  19.0 2.0 %far.1 = (bf16[4,2,128,128]{3,2,1,0:T(8,128)(2,1)S(1)}, bf16[4,2,128,128]{3,2,1,0:T(8,128)(2,1)S(1)}, bf16[2,4,128,512]{3,2,1,0:T(8,128)(2,1)S(1)}, bf16[2,4,128...) custom-call(s32[8,1,128]{2,1,0:T(1,128)S(1)} %bitcast.34, bf16[2,16,128,128]{3,2,1,0:T(8,128)(2,1)S(1)} %get-tuple-element.63.q_ref, ...), custom_call_target="tpu_custom_call" | custom-call | flops 1073741824 | bytes 3018752 | tf_op jit(solution)/shard_map/far/pallas_call | solution.py:172
  21.0 2.7 %collective-permute-start.4 = (bf16[4,2,128,128]{3,2,1,0:T(8,128)(2,1)S(1)}, bf16[4,2,128,128]{3,2,1,0:T(8,128)(2,1)S(1)}, u32[]{:S(2)}, u32[]{:S(2)}) collective-permute-start(bf16[4,2,128,128]{3,2,1,0:T(8,128)(2,1)S(1)} %get-tuple-element.42), channel_id=1, source_target_pairs={{0,8},{8,0},{16,24},{24,16},{1,9},{9,1},{17,25},{25,17},{2,10},{10... | collective-permute-start | bytes 786440 | tf_op jit(solution)/shard_map/ppermute | solution.py:396
  23.7 3.4 %rest.1 = (f32[4,2,128,128]{3,2,1,0:T(8,128)S(1)}, f32[4,2,128,128]{3,2,1,0:T(8,128)S(1)}, f32[4,2,128,128]{3,2,1,0:T(8,128)S(1)}, f32[4,2,128,128]{3,2,1,0:T(8,...) custom-call(bf16[2,16,128,128]{3,2,1,0:T(8,128)(2,1)S(1)} %get-tuple-element.63.q_ref, ...), custom_call_target="tpu_custom_call" | custom-call | flops 5368709120 | bytes 14286848 | tf_op jit(solution)/shard_map/rest/pallas_call | solution.py:172
  27.1 1.0 %collective-permute-done.4.from_a = bf16[4,2,128,128]{3,2,1,0:T(8,128)(2,1)S(1)} collective-permute-done((bf16[4,2,128,128]{3,2,1,0:T(8,128)(2,1)S(1)}, bf16[4,2,128,128]{3,2,1,0:T(8,128)(2,1)S(1)}, u32[]{:S(2)}, u32[]{:S(2)}) %collective-permute-start.4) | collective-permute-done | bytes 262176 | tf_op jit(solution)/shard_map/ppermute | solution.py:396
  28.1 0.0 collective-permute-done.5.from_b
  28.1 0.1 merge.1
  28.2 2.2 %collective-permute-start.6 = (bf16[4,2,128,128]{3,2,1,0:T(8,128)(2,1)S(1)}, bf16[4,2,128,128]{3,2,1,0:T(8,128)(2,1)S(1)}, u32[]{:S(2)}, u32[]{:S(2)}) collective-permute-start(bf16[4,2,128,128]{3,2,1,0:T(8,128)(2,1)S(1)} %get-tuple-element.44), channel_id=1, source_target_pairs={{0,8},{8,0},{16,24},{24,16},{1,9},{9,1},{17,25},{25,17},{2,10},{10... | collective-permute-start | bytes 786440 | tf_op jit(solution)/shard_map/ppermute | solution.py:406
  30.3 0.0 collective-permute-start.7
  30.3 1.6 %copy.23 = bf16[2,1,128,16,128]{4,3,2,1,0:T(8,128)(2,1)} copy(bf16[2,1,128,16,128]{4,2,3,0,1:T(8,128)(2,1)S(1)} %bitcast.32) | data formatting | bytes 2097152
  32.0 1.6 %copy.24 = bf16[2,1,128,16,128]{4,3,2,1,0:T(8,128)(2,1)} copy(bf16[2,1,128,16,128]{4,2,3,0,1:T(8,128)(2,1)S(1)} %bitcast.31) | data formatting | bytes 2097152
  33.6 2.4 %collective-permute-done.6.last_a = bf16[4,2,128,128]{3,2,1,0:T(8,128)(2,1)S(1)} collective-permute-done((bf16[4,2,128,128]{3,2,1,0:T(8,128)(2,1)S(1)}, bf16[4,2,128,128]{3,2,1,0:T(8,128)(2,1)S(1)}, u32[]{:S(2)}, u32[]{:S(2)}) %collective-permute-start.6) | collective-permute-done | bytes 262176 | tf_op jit(solution)/shard_map/ppermute | solution.py:406
  36.0 1.1 %unpack.1 = (bf16[2,1,128,4,128]{4,3,2,1,0:T(4,128)(2,1)}, bf16[2,1,128,4,128]{4,3,2,1,0:T(4,128)(2,1)}) custom-call(f32[4,2,128,128]{3,2,1,0:T(8,128)S(1)} %get-tuple-element.38.own_a, f32[4,2,128,128]{3,2,1,0:T(8,128)S(1)} %get-tuple-element.39.own_b, bf16[4,2,128,128]{3,2,1,0:T(8,128)(2,1)S(1)} %collective-permute-done.6.last_a, ...), custom_call_target="tpu_custom_call" | custom-call | flops 8192 | bytes 1835008 | tf_op jit(solution)/shard_map/unpack/pallas_call | solution.py:172
  (19 shorter events, 0.2 us)
Async XLA Ops:
  0.6 6.3 %copy-start = (bf16[2,1,128,16,128]{4,3,2,1,0:T(8,128)(2,1)S(1)}, bf16[2,1,128,16,128]{4,3,2,1,0:T(8,128)(2,1)}, u32[]{:S(2)}) copy-start(bf16[2,1,128,16,128]{4,3,2,1,0:T(8,128)(2,1)} %param.8) | copy-start | bytes 3145732
  0.6 6.3 %copy-start.1 = (bf16[2,1,128,16,128]{4,3,2,1,0:T(8,128)(2,1)S(1)}, bf16[2,1,128,16,128]{4,3,2,1,0:T(8,128)(2,1)}, u32[]{:S(2)}) copy-start(bf16[2,1,128,16,128]{4,3,2,1,0:T(8,128)(2,1)} %param.5) | copy-start | bytes 3145732
  2.3 5.3 %collective-permute-start.1 = (bf16[4,2,128,128]{3,2,1,0:T(8,128)(2,1)S(1)}, bf16[4,2,128,128]{3,2,1,0:T(8,128)(2,1)S(1)}, u32[]{:S(2)}, u32[]{:S(2)}) collective-permute-start(bf16[4,2,128,128]{3,2,1,0:T(8,128)(2,1)S(1)} %maximum_bitcast_fusion.own_a.refs_3_), channel_id=1, source_target_pairs={{8,16},{16,8},{0,1},{24,25},{9,17},{17,9},{1,0},{25,24},{10,18},{1... | collective-permute-start | bytes 786440 | tf_op jit(solution)/shard_map/ppermute | solution.py:383
  2.8 10.7 %collective-permute-start = (bf16[4,2,128,128]{3,2,1,0:T(8,128)(2,1)S(1)}, bf16[4,2,128,128]{3,2,1,0:T(8,128)(2,1)S(1)}, u32[]{:S(2)}, u32[]{:S(2)}) collective-permute-start(bf16[4,2,128,128]{3,2,1,0:T(8,128)(2,1)S(1)} %maximum_bitcast_fusion.1.own_b.refs_4_), channel_id=1, source_target_pairs={{0,8},{8,0},{16,24},{24,16},{1,9},{9,1},{17,25},{25,17},{2,10},{10... | collective-permute-start | bytes 786440 | tf_op jit(solution)/shard_map/ppermute | solution.py:384
  7.0 6.6 %copy-start.2 = (s32[512]{0:T(512)S(1)}, s32[512]{0:T(512)}, u32[]{:S(2)}) copy-start(s32[512]{0:T(512)} %param.9) | copy-start | bytes 6148
  7.6 11.3 %collective-permute-start.2 = (bf16[4,2,128,128]{3,2,1,0:T(8,128)(2,1)S(1)}, bf16[4,2,128,128]{3,2,1,0:T(8,128)(2,1)S(1)}, u32[]{:S(2)}, u32[]{:S(2)}) collective-permute-start(bf16[4,2,128,128]{3,2,1,0:T(8,128)(2,1)S(1)} %broadcast_select_fusion.prev_b.refs_6_), channel_id=1, source_target_pairs={{0,8},{8,0},{16,24},{24,16},{1,9},{9,1},{17,25},{25,17},{2,10},{10... | collective-permute-start | bytes 786440 | tf_op jit(solution)/shard_map/ppermute | solution.py:387
  13.5 5.4 %collective-permute-start.3 = (bf16[4,2,128,128]{3,2,1,0:T(8,128)(2,1)S(1)}, bf16[4,2,128,128]{3,2,1,0:T(8,128)(2,1)S(1)}, u32[]{:S(2)}, u32[]{:S(2)}) collective-permute-start(bf16[4,2,128,128]{3,2,1,0:T(8,128)(2,1)S(1)} %collective-permute-done.prev_a.refs_5_), channel_id=1, source_target_pairs={{8,16},{16,8},{0,1},{24,25},{9,17},{17,9},{1,0},{25,24},{10,18},{1... | collective-permute-start | bytes 786440 | tf_op jit(solution)/shard_map/ppermute | solution.py:386
  21.0 7.0 %collective-permute-start.4 = (bf16[4,2,128,128]{3,2,1,0:T(8,128)(2,1)S(1)}, bf16[4,2,128,128]{3,2,1,0:T(8,128)(2,1)S(1)}, u32[]{:S(2)}, u32[]{:S(2)}) collective-permute-start(bf16[4,2,128,128]{3,2,1,0:T(8,128)(2,1)S(1)} %get-tuple-element.42), channel_id=1, source_target_pairs={{0,8},{8,0},{16,24},{24,16},{1,9},{9,1},{17,25},{25,17},{2,10},{10... | collective-permute-start | bytes 786440 | tf_op jit(solution)/shard_map/ppermute | solution.py:396
  23.7 4.4 %collective-permute-start.5 = (bf16[4,2,128,128]{3,2,1,0:T(8,128)(2,1)S(1)}, bf16[4,2,128,128]{3,2,1,0:T(8,128)(2,1)S(1)}, u32[]{:S(2)}, u32[]{:S(2)}) collective-permute-start(bf16[4,2,128,128]{3,2,1,0:T(8,128)(2,1)S(1)} %get-tuple-element.43.deep_b), channel_id=1, source_target_pairs={{8,16},{16,8},{0,1},{24,25},{9,17},{17,9},{1,0},{25,24},{10,18},{1... | collective-permute-start | bytes 786440 | tf_op jit(solution)/shard_map/ppermute | solution.py:397
  28.2 7.8 %collective-permute-start.6 = (bf16[4,2,128,128]{3,2,1,0:T(8,128)(2,1)S(1)}, bf16[4,2,128,128]{3,2,1,0:T(8,128)(2,1)S(1)}, u32[]{:S(2)}, u32[]{:S(2)}) collective-permute-start(bf16[4,2,128,128]{3,2,1,0:T(8,128)(2,1)S(1)} %get-tuple-element.44), channel_id=1, source_target_pairs={{0,8},{8,0},{16,24},{24,16},{1,9},{9,1},{17,25},{25,17},{2,10},{10... | collective-permute-start | bytes 786440 | tf_op jit(solution)/shard_map/ppermute | solution.py:406
  30.3 5.7 %collective-permute-start.7 = (bf16[4,2,128,128]{3,2,1,0:T(8,128)(2,1)S(1)}, bf16[4,2,128,128]{3,2,1,0:T(8,128)(2,1)S(1)}, u32[]{:S(2)}, u32[]{:S(2)}) collective-permute-start(bf16[4,2,128,128]{3,2,1,0:T(8,128)(2,1)S(1)} %get-tuple-element.45.next_b), channel_id=1, source_target_pairs={{8,16},{16,8},{0,1},{24,25},{9,17},{17,9},{1,0},{25,24},{10,18},{1... | collective-permute-start | bytes 786440 | tf_op jit(solution)/shard_map/ppermute | solution.py:407

commit v11 on v10

--- a/solution.py
+++ b/solution.py
@@ -351,7 +351,7 @@
             own_b[:, which] + last_a[:, which].astype(jnp.float32),
         )
         for slot, total in enumerate(sums):
-            ref[halves[slot], 0] = jnp.swapaxes(total, 0, 1).astype(jnp.bfloat16)
+            ref[halves[slot], 0] = jnp.swapaxes(total.astype(jnp.bfloat16), 0, 1)
 
 
 def by_half(info, final_a, final_b):

time: 37.2 us -> 37.2 us (level)
  no operation moved by 1% of the time
where the time goes in v11:
time: 37.2 us; the launch traced here: 37 us
  starting transfers between devices  15.4 us (41%)
  Pallas kernels  9.53 us (26%)
  local copies, waits for them, and re-layouts  5.36 us (14%)
  waiting for transfers between devices  5.36 us (14%)
  between operations  0.8 us (2%)
  other arithmetic  0.59 us (2%)
    pallas_call x5, Pallas kernels, vmem_call(): pl.pallas_call(kernel, in_specs=[whole] * len(args), out_specs=[whole] *...  9.53 us
    ppermute x1, starting transfers between devices, two_span_window(): a2 = lax.ppermute(b1, 'seq', pairs_a)  5.89 us
    ppermute x1, starting transfers between devices, two_span_window(): a1 = lax.ppermute(own_b, 'seq', pairs_a)  4.15 us
    unnamed x8, local copies, waits for them, and re-layouts  3.31 us
    ppermute x1, starting transfers between devices, two_span_window(): from_a = lax.ppermute(deep_a, 'seq', pairs_a)  2.69 us
    ppermute x1, waiting for transfers between devices, two_span_window(): last_a = lax.ppermute(next_a, 'seq', pairs_a)  2.35 us
    ppermute x1, starting transfers between devices, two_span_window(): last_a = lax.ppermute(next_a, 'seq', pairs_a)  2.16 us
    ppermute x1, waiting for transfers between devices, two_span_window(): a2 = lax.ppermute(b1, 'seq', pairs_a)  2 us
  transfers between devices with their start and end apart: 8, of which 3 were waited for; matrix products, arithmetic and copies ran while one was open for 12% of the time, Pallas kernels for 17%

profile of v11, /device:TPU:0, one launch (start us, length us, event | category | flops | bytes accessed | tf_op | source)
XLA Modules:
  0.0 37.0 jit_solution(8474711822277786655)
XLA Ops:
  0.7 1.4 %constant_dynamic-slice_fusion = (bf16[1,1,128,4,128]{4,3,2,1,0:T(4,128)(2,1)S(1)}, bf16[1,1,128,4,128]{4,3,2,1,0:T(4,128)(2,1)S(1)}, bf16[1,1,128,4,128]{4,3,2,...) fusion(bf16[2,1,128,4,128]{4,3,2,1,0:T(4,128)(2,1)} %param.7, s32[]{:T(128)S(6)} %select_n.27, s32[]{:T(128)S(6)} %select_n.26, ...), kind=kLoop, calls=%fused_computation.11 | loop fusion | bytes 1048584 | tf_op jit(solution)/shard_map/jit(dynamic_index_in_dim)/dynamic_slice | solution.py:459
  2.3 0.5 %collective-permute-start.1 = (bf16[4,2,128,128]{3,2,1,0:T(8,128)(2,1)S(1)}, bf16[4,2,128,128]{3,2,1,0:T(8,128)(2,1)S(1)}, u32[]{:S(2)}, u32[]{:S(2)}) collective-permute-start(bf16[4,2,128,128]{3,2,1,0:T(8,128)(2,1)S(1)} %maximum_bitcast_fusion.own_a.refs_3_), channel_id=1, source_target_pairs={{8,16},{16,8},{0,1},{24,25},{9,17},{17,9},{1,0},{25,24},{10,18},{1... | collective-permute-start | bytes 786440 | tf_op jit(solution)/shard_map/ppermute | solution.py:383
  2.8 4.1 %collective-permute-start = (bf16[4,2,128,128]{3,2,1,0:T(8,128)(2,1)S(1)}, bf16[4,2,128,128]{3,2,1,0:T(8,128)(2,1)S(1)}, u32[]{:S(2)}, u32[]{:S(2)}) collective-permute-start(bf16[4,2,128,128]{3,2,1,0:T(8,128)(2,1)S(1)} %maximum_bitcast_fusion.1.own_b.refs_4_), channel_id=1, source_target_pairs={{0,8},{8,0},{16,24},{24,16},{1,9},{9,1},{17,25},{25,17},{2,10},{10... | collective-permute-start | bytes 786440 | tf_op jit(solution)/shard_map/ppermute | solution.py:384
  7.0 0.5 %copy_bitcast_fusion = (bf16[2,16,128,128]{3,2,1,0:T(8,128)(2,1)S(1)}, bf16[2,16,128,128]{3,2,1,0:T(8,128)(2,1)S(1)}) fusion(bf16[2,1,128,16,128]{4,3,2,1,0:T(8,128)(2,1)S(1)} %copy-done, bf16[2,1,128,16,128]{4,3,2,1,0:T(8,128)(2,1)S(1)} %copy-done.1), kind=kLoop, calls=%fused_computation.1 | loop fusion | bytes 4194304 | tf_op jit(solution)/shard_map/transpose | solution.py:464
  7.5 0.1 iota_add_fusion
  7.6 0.0 collective-permute-done.1
  7.6 5.9 %collective-permute-start.2 = (bf16[4,2,128,128]{3,2,1,0:T(8,128)(2,1)S(1)}, bf16[4,2,128,128]{3,2,1,0:T(8,128)(2,1)S(1)}, u32[]{:S(2)}, u32[]{:S(2)}) collective-permute-start(bf16[4,2,128,128]{3,2,1,0:T(8,128)(2,1)S(1)} %broadcast_select_fusion.prev_b.refs_6_), channel_id=1, source_target_pairs={{0,8},{8,0},{16,24},{24,16},{1,9},{9,1},{17,25},{25,17},{2,10},{10... | collective-permute-start | bytes 786440 | tf_op jit(solution)/shard_map/ppermute | solution.py:387
  13.5 0.0 collective-permute-done.prev_a.refs_5_
  13.5 0.0 collective-permute-start.3
  13.5 0.4 %select_reduce_fusion = s32[8,128]{1,0:T(8,128)S(1)} fusion(s32[8,128]{1,0:T(8,128)S(1)} %iota_add_fusion, s32[512]{0:T(512)S(1)} %copy-done.2), kind=kLoop, calls=%fused_computation | loop fusion | flops 1571840 | bytes 10240 | tf_op jit(solution)/shard_map/reduce_max | solution.py:445
  14.0 3.0 %near.1 = (f32[2,4,256,512]{3,2,1,0:T(8,128)S(1)}, f32[2,4,256,512]{3,2,1,0:T(8,128)S(1)}, f32[2,4,8,512]{3,2,1,0:T(8,128)S(1)}) custom-call(s32[8,1,128]{2,1,0:T(1,128)S(1)} %bitcast.33, bf16[2,16,128,128]{3,2,1,0:T(8,128)(2,1)S(1)} %get-tuple-element.63.q_ref, bf16[2,16,128,128]{3,2,1,0:T(8,128)(2,1)S(1)} %get-tuple-element.62.do_ref, ...), custom_call_target="tpu_custom_call" | custom-call | flops 2147483648 | bytes 3149824 | tf_op jit(solution)/shard_map/near/pallas_call | solution.py:172
  17.0 2.0 %collective-permute-done.2.far_a.refs_7_ = bf16[4,2,128,128]{3,2,1,0:T(8,128)(2,1)S(1)} collective-permute-done((bf16[4,2,128,128]{3,2,1,0:T(8,128)(2,1)S(1)}, bf16[4,2,128,128]{3,2,1,0:T(8,128)(2,1)S(1)}, u32[]{:S(2)}, u32[]{:S(2)}) %collective-permute-start.2) | collective-permute-done | bytes 262176 | tf_op jit(solution)/shard_map/ppermute | solution.py:387
  19.0 2.0 %far.1 = (bf16[4,2,128,128]{3,2,1,0:T(8,128)(2,1)S(1)}, bf16[4,2,128,128]{3,2,1,0:T(8,128)(2,1)S(1)}, bf16[2,4,128,512]{3,2,1,0:T(8,128)(2,1)S(1)}, bf16[2,4,128...) custom-call(s32[8,1,128]{2,1,0:T(1,128)S(1)} %bitcast.34, bf16[2,16,128,128]{3,2,1,0:T(8,128)(2,1)S(1)} %get-tuple-element.63.q_ref, ...), custom_call_target="tpu_custom_call" | custom-call | flops 1073741824 | bytes 3018752 | tf_op jit(solution)/shard_map/far/pallas_call | solution.py:172
  21.0 2.7 %collective-permute-start.4 = (bf16[4,2,128,128]{3,2,1,0:T(8,128)(2,1)S(1)}, bf16[4,2,128,128]{3,2,1,0:T(8,128)(2,1)S(1)}, u32[]{:S(2)}, u32[]{:S(2)}) collective-permute-start(bf16[4,2,128,128]{3,2,1,0:T(8,128)(2,1)S(1)} %get-tuple-element.42), channel_id=1, source_target_pairs={{0,8},{8,0},{16,24},{24,16},{1,9},{9,1},{17,25},{25,17},{2,10},{10... | collective-permute-start | bytes 786440 | tf_op jit(solution)/shard_map/ppermute | solution.py:396
  23.7 3.4 %rest.1 = (f32[4,2,128,128]{3,2,1,0:T(8,128)S(1)}, f32[4,2,128,128]{3,2,1,0:T(8,128)S(1)}, f32[4,2,128,128]{3,2,1,0:T(8,128)S(1)}, f32[4,2,128,128]{3,2,1,0:T(8,...) custom-call(bf16[2,16,128,128]{3,2,1,0:T(8,128)(2,1)S(1)} %get-tuple-element.63.q_ref, ...), custom_call_target="tpu_custom_call" | custom-call | flops 5368709120 | bytes 14286848 | tf_op jit(solution)/shard_map/rest/pallas_call | solution.py:172
  27.1 1.0 %collective-permute-done.4.from_a = bf16[4,2,128,128]{3,2,1,0:T(8,128)(2,1)S(1)} collective-permute-done((bf16[4,2,128,128]{3,2,1,0:T(8,128)(2,1)S(1)}, bf16[4,2,128,128]{3,2,1,0:T(8,128)(2,1)S(1)}, u32[]{:S(2)}, u32[]{:S(2)}) %collective-permute-start.4) | collective-permute-done | bytes 262176 | tf_op jit(solution)/shard_map/ppermute | solution.py:396
  28.1 0.0 collective-permute-done.5.from_b
  28.1 0.1 merge.1
  28.2 2.2 %collective-permute-start.6 = (bf16[4,2,128,128]{3,2,1,0:T(8,128)(2,1)S(1)}, bf16[4,2,128,128]{3,2,1,0:T(8,128)(2,1)S(1)}, u32[]{:S(2)}, u32[]{:S(2)}) collective-permute-start(bf16[4,2,128,128]{3,2,1,0:T(8,128)(2,1)S(1)} %get-tuple-element.44), channel_id=1, source_target_pairs={{0,8},{8,0},{16,24},{24,16},{1,9},{9,1},{17,25},{25,17},{2,10},{10... | collective-permute-start | bytes 786440 | tf_op jit(solution)/shard_map/ppermute | solution.py:406
  30.3 0.0 collective-permute-start.7
  30.3 1.6 %copy.23 = bf16[2,1,128,16,128]{4,3,2,1,0:T(8,128)(2,1)} copy(bf16[2,1,128,16,128]{4,2,3,0,1:T(8,128)(2,1)S(1)} %bitcast.32) | data formatting | bytes 2097152
  32.0 1.6 %copy.24 = bf16[2,1,128,16,128]{4,3,2,1,0:T(8,128)(2,1)} copy(bf16[2,1,128,16,128]{4,2,3,0,1:T(8,128)(2,1)S(1)} %bitcast.31) | data formatting | bytes 2097152
  33.6 2.4 %collective-permute-done.6.last_a = bf16[4,2,128,128]{3,2,1,0:T(8,128)(2,1)S(1)} collective-permute-done((bf16[4,2,128,128]{3,2,1,0:T(8,128)(2,1)S(1)}, bf16[4,2,128,128]{3,2,1,0:T(8,128)(2,1)S(1)}, u32[]{:S(2)}, u32[]{:S(2)}) %collective-permute-start.6) | collective-permute-done | bytes 262176 | tf_op jit(solution)/shard_map/ppermute | solution.py:406
  36.0 1.0 %unpack.1 = (bf16[2,1,128,4,128]{4,3,2,1,0:T(4,128)(2,1)}, bf16[2,1,128,4,128]{4,3,2,1,0:T(4,128)(2,1)}) custom-call(f32[4,2,128,128]{3,2,1,0:T(8,128)S(1)} %get-tuple-element.38.own_a, f32[4,2,128,128]{3,2,1,0:T(8,128)S(1)} %get-tuple-element.39.own_b, bf16[4,2,128,128]{3,2,1,0:T(8,128)(2,1)S(1)} %collective-permute-done.6.last_a, ...), custom_call_target="tpu_custom_call" | custom-call | flops 8192 | bytes 1835008 | tf_op jit(solution)/shard_map/unpack/pallas_call | solution.py:172
  (19 shorter events, 0.2 us)
Async XLA Ops:
  0.6 6.3 %copy-start = (bf16[2,1,128,16,128]{4,3,2,1,0:T(8,128)(2,1)S(1)}, bf16[2,1,128,16,128]{4,3,2,1,0:T(8,128)(2,1)}, u32[]{:S(2)}) copy-start(bf16[2,1,128,16,128]{4,3,2,1,0:T(8,128)(2,1)} %param.8) | copy-start | bytes 3145732
  0.6 6.3 %copy-start.1 = (bf16[2,1,128,16,128]{4,3,2,1,0:T(8,128)(2,1)S(1)}, bf16[2,1,128,16,128]{4,3,2,1,0:T(8,128)(2,1)}, u32[]{:S(2)}) copy-start(bf16[2,1,128,16,128]{4,3,2,1,0:T(8,128)(2,1)} %param.5) | copy-start | bytes 3145732
  2.3 5.3 %collective-permute-start.1 = (bf16[4,2,128,128]{3,2,1,0:T(8,128)(2,1)S(1)}, bf16[4,2,128,128]{3,2,1,0:T(8,128)(2,1)S(1)}, u32[]{:S(2)}, u32[]{:S(2)}) collective-permute-start(bf16[4,2,128,128]{3,2,1,0:T(8,128)(2,1)S(1)} %maximum_bitcast_fusion.own_a.refs_3_), channel_id=1, source_target_pairs={{8,16},{16,8},{0,1},{24,25},{9,17},{17,9},{1,0},{25,24},{10,18},{1... | collective-permute-start | bytes 786440 | tf_op jit(solution)/shard_map/ppermute | solution.py:383
  2.8 10.7 %collective-permute-start = (bf16[4,2,128,128]{3,2,1,0:T(8,128)(2,1)S(1)}, bf16[4,2,128,128]{3,2,1,0:T(8,128)(2,1)S(1)}, u32[]{:S(2)}, u32[]{:S(2)}) collective-permute-start(bf16[4,2,128,128]{3,2,1,0:T(8,128)(2,1)S(1)} %maximum_bitcast_fusion.1.own_b.refs_4_), channel_id=1, source_target_pairs={{0,8},{8,0},{16,24},{24,16},{1,9},{9,1},{17,25},{25,17},{2,10},{10... | collective-permute-start | bytes 786440 | tf_op jit(solution)/shard_map/ppermute | solution.py:384
  7.0 6.6 %copy-start.2 = (s32[512]{0:T(512)S(1)}, s32[512]{0:T(512)}, u32[]{:S(2)}) copy-start(s32[512]{0:T(512)} %param.9) | copy-start | bytes 6148
  7.6 11.3 %collective-permute-start.2 = (bf16[4,2,128,128]{3,2,1,0:T(8,128)(2,1)S(1)}, bf16[4,2,128,128]{3,2,1,0:T(8,128)(2,1)S(1)}, u32[]{:S(2)}, u32[]{:S(2)}) collective-permute-start(bf16[4,2,128,128]{3,2,1,0:T(8,128)(2,1)S(1)} %broadcast_select_fusion.prev_b.refs_6_), channel_id=1, source_target_pairs={{0,8},{8,0},{16,24},{24,16},{1,9},{9,1},{17,25},{25,17},{2,10},{10... | collective-permute-start | bytes 786440 | tf_op jit(solution)/shard_map/ppermute | solution.py:387
  13.5 5.4 %collective-permute-start.3 = (bf16[4,2,128,128]{3,2,1,0:T(8,128)(2,1)S(1)}, bf16[4,2,128,128]{3,2,1,0:T(8,128)(2,1)S(1)}, u32[]{:S(2)}, u32[]{:S(2)}) collective-permute-start(bf16[4,2,128,128]{3,2,1,0:T(8,128)(2,1)S(1)} %collective-permute-done.prev_a.refs_5_), channel_id=1, source_target_pairs={{8,16},{16,8},{0,1},{24,25},{9,17},{17,9},{1,0},{25,24},{10,18},{1... | collective-permute-start | bytes 786440 | tf_op jit(solution)/shard_map/ppermute | solution.py:386
  21.0 7.0 %collective-permute-start.4 = (bf16[4,2,128,128]{3,2,1,0:T(8,128)(2,1)S(1)}, bf16[4,2,128,128]{3,2,1,0:T(8,128)(2,1)S(1)}, u32[]{:S(2)}, u32[]{:S(2)}) collective-permute-start(bf16[4,2,128,128]{3,2,1,0:T(8,128)(2,1)S(1)} %get-tuple-element.42), channel_id=1, source_target_pairs={{0,8},{8,0},{16,24},{24,16},{1,9},{9,1},{17,25},{25,17},{2,10},{10... | collective-permute-start | bytes 786440 | tf_op jit(solution)/shard_map/ppermute | solution.py:396
  23.7 4.4 %collective-permute-start.5 = (bf16[4,2,128,128]{3,2,1,0:T(8,128)(2,1)S(1)}, bf16[4,2,128,128]{3,2,1,0:T(8,128)(2,1)S(1)}, u32[]{:S(2)}, u32[]{:S(2)}) collective-permute-start(bf16[4,2,128,128]{3,2,1,0:T(8,128)(2,1)S(1)} %get-tuple-element.43.deep_b), channel_id=1, source_target_pairs={{8,16},{16,8},{0,1},{24,25},{9,17},{17,9},{1,0},{25,24},{10,18},{1... | collective-permute-start | bytes 786440 | tf_op jit(solution)/shard_map/ppermute | solution.py:397
  28.2 7.8 %collective-permute-start.6 = (bf16[4,2,128,128]{3,2,1,0:T(8,128)(2,1)S(1)}, bf16[4,2,128,128]{3,2,1,0:T(8,128)(2,1)S(1)}, u32[]{:S(2)}, u32[]{:S(2)}) collective-permute-start(bf16[4,2,128,128]{3,2,1,0:T(8,128)(2,1)S(1)} %get-tuple-element.44), channel_id=1, source_target_pairs={{0,8},{8,0},{16,24},{24,16},{1,9},{9,1},{17,25},{25,17},{2,10},{10... | collective-permute-start | bytes 786440 | tf_op jit(solution)/shard_map/ppermute | solution.py:406
  30.3 5.7 %collective-permute-start.7 = (bf16[4,2,128,128]{3,2,1,0:T(8,128)(2,1)S(1)}, bf16[4,2,128,128]{3,2,1,0:T(8,128)(2,1)S(1)}, u32[]{:S(2)}, u32[]{:S(2)}) collective-permute-start(bf16[4,2,128,128]{3,2,1,0:T(8,128)(2,1)S(1)} %get-tuple-element.45.next_b), channel_id=1, source_target_pairs={{8,16},{16,8},{0,1},{24,25},{9,17},{17,9},{1,0},{25,24},{10,18},{1... | collective-permute-start | bytes 786440 | tf_op jit(solution)/shard_map/ppermute | solution.py:407
